TPU v7x, 256 devices: a whole 4x4x8 slice. The times are simulated.
256 devices in a mesh: blk: 8 (over y_lo, x), rows: 32 (over y_hi, z, core).
Axes of the slice: x: 4, y: 4 (y_hi: 2, y_lo: 2; y = y_hi * 2 + y_lo), z: 8, core: 2. Of those that a mesh axis runs over, the one named last changes fastest.
Arguments:
- embeddings: bfloat16 [524288, 768], P(('blk', 'rows')), may hold values from -6 to 6
- coverage: float32 [524288], P(('blk', 'rows')), may hold values from 0 to 4
- chosen_index: int32 [512], replicated, may hold values from 0 to 524287, as said below
- candidate_index: int32 [1024], P('blk'), may hold values from 0 to 524287, as said below
Outputs:
- new_coverage: float32 [524288], P(('blk', 'rows'))
- gains: float32 [1024], P(('blk', 'rows'))
Inputs may be any that keep to these rules, and one draw needn't show every extreme that they name: `chosen_index`: the entries are distinct; the rows r * 2048 to (r + 1) * 2048 - 1 hold at most 4 of them for every r, and exactly 4 for some r. `candidate_index`: entries b * 128 to (b + 1) * 128 - 1 lie in rows b * 65536 to (b + 1) * 65536 - 1.
All inputs are finite; a program needn't handle non-finite values.
Results may differ from a plain program's by a relative error of at most 0.00035.
Values may be sent and summed in bfloat16 or wider, within the bound.
No kernel may reach another device: no remote copies, remote signals or barrier semaphores. Data moves between devices by JAX's collectives and lax.ppermute only.
A program may use at most 64 MiB of HBM per device.

v0:
```python
import jax
import jax.numpy as jnp
from jax import lax
from jax.sharding import Mesh
from jax.sharding import PartitionSpec as P

BLK = ("blk_0", "blk_1")
BLK_ROWS = ("blk_0", "blk_1", "rows")


def in_order(pieces, dim):
    pieces = jnp.moveaxis(pieces, 0, dim)
    dims = pieces.shape
    return pieces.reshape(*dims[:dim], dims[dim] * dims[dim + 1], *dims[dim + 2 :])


def all_blocks(x, axes, sequence):
    pieces = x[None]
    for k in sequence:
        pieces = lax.all_gather(pieces, axes[k], axis=0, tiled=True)
    held = [lax.axis_size(axes[k]) for k in reversed(sequence)]
    pieces = pieces.reshape(*held, *x.shape)
    turned = sorted(range(len(sequence)), key=lambda place: sequence[len(sequence) - 1 - place])
    return pieces.transpose(*turned, *range(len(sequence), pieces.ndim)).reshape(-1, *x.shape)


def whole_of(x, axes, sequence, dim):
    return in_order(all_blocks(x, axes, sequence), dim)


def owned_rows(embeddings, indices, base_row):
    local_rows = embeddings.shape[0]
    offset = indices - base_row
    inside = (offset >= 0) & (offset < local_rows)
    safe = jnp.clip(offset, 0, local_rows - 1)
    picked = jnp.take(embeddings, safe, axis=0).astype(jnp.float32)
    return jnp.where(inside[:, None], picked, 0.0)


def local(embeddings, coverage, chosen_index, candidate_index):
    local_rows = embeddings.shape[0]
    width = embeddings.shape[1]
    scale = 1.0 / width**0.5
    device_pos = lax.axis_index(BLK) * lax.axis_size("rows") + lax.axis_index("rows")
    base_row = device_pos * local_rows
    chosen_f = lax.psum(owned_rows(embeddings, chosen_index, base_row), BLK_ROWS)
    chosen_rows = chosen_f.astype(jnp.bfloat16)
    sims = jnp.dot(embeddings, chosen_rows.T, preferred_element_type=jnp.float32) * scale
    best = jnp.max(sims, axis=1)
    new_coverage = jnp.maximum(coverage, best)
    every_index = whole_of(candidate_index, BLK, (0, 1), 0)
    every_f = lax.psum(owned_rows(embeddings, every_index, base_row), BLK_ROWS)
    every_rows = every_f.astype(jnp.bfloat16)
    cand_sims = jnp.dot(embeddings, every_rows.T, preferred_element_type=jnp.float32) * scale
    gain_part = jnp.sum(jnp.maximum(cand_sims - new_coverage[:, None], 0.0), axis=0)
    gains = lax.psum_scatter(gain_part, BLK_ROWS, scatter_dimension=0, tiled=True)
    return (new_coverage, gains)


def solution(mesh):
    torus = Mesh(mesh.devices.reshape(2, 4, mesh.shape["rows"]), ("blk_0", "blk_1", "rows"))
    return jax.shard_map(
        local,
        mesh=torus,
        in_specs=(P(BLK_ROWS, None), P(BLK_ROWS), P(), P(BLK)),
        out_specs=(P(BLK_ROWS), P(BLK_ROWS)),
        check_vma=False,
    )
```

profile of v0, /device:TPU:1, one launch (start us, length us, event | category | flops | bytes accessed | tf_op | source)
XLA Modules:
  0.0 248.3 jit_solution(17189368050249611175)
XLA Ops:
  0.6 0.0 copy-start
  0.7 0.8 compare_and_fusion.1
  1.5 1.0 copy-done
  2.5 0.0 copy-start.4
  2.5 2.7 %gather_fusion = bf16[512,768]{1,0:T(8,128)(2,1)} fusion(bf16[2048,768]{1,0:T(8,128)(2,1)S(1)} %copy-done, s32[1024]{0:T(1024)S(1)} %pad_clamp_fusion), kind=kCustom, calls=%fused_computation | custom fusion | bytes 1574912 | tf_op jit(solution)/shard_map/jit(_take)/gather | solution.py:36
  5.2 2.5 %convert_select_fusion.1 = f32[512,768]{1,0:T(8,128)} fusion(bf16[512,768]{1,0:T(8,128)(2,1)} %gather_fusion, pred[512]{0:T(512)(128)(4,1)S(1)} %get-tuple-element.4, pred[512]{0:T(512)(128)(4,1)S(1)} %get-tuple-element.6), kind=kLoop, calls=%fused_computation.6 | loop fusion | flops 1179648 | bytes 2360320 | tf_op jit(solution)/shard_map/jit(_where)/select_n | solution.py:37
  7.8 0.0 copy-done.4
  7.8 3.7 %all-gather.1 = s32[2,1,128]{2,1,0:T(1,128)S(1)} all-gather(s32[1,1,128]{2,1,0:T(1,128)S(1)} %bitcast.19), channel_id=2, replica_groups=mesh['blk_0'=2,'blk_1'=4,'rows'=32] {'blk_0'}, dimensions={0}, use_global_device_ids=true | all-gather | bytes 1536 | tf_op jit(solution)/shard_map/all_gather | solution.py:20
  11.5 7.9 %all-gather.2 = s32[4,2,128]{2,1,0:T(2,128)S(1)} all-gather(s32[1,2,128]{2,1,0:T(2,128)S(1)} %bitcast.18), channel_id=1, replica_groups=mesh['blk_0'=2,'blk_1'=4,'rows'=32] {'blk_1'}, dimensions={0}, use_global_device_ids=true | all-gather | bytes 5120 | tf_op jit(solution)/shard_map/all_gather | solution.py:20
  19.4 5.2 %gather_fusion.1 = bf16[1024,768]{1,0:T(8,128)(2,1)} fusion(bf16[2048,768]{1,0:T(8,128)(2,1)S(1)} %copy-done, s32[1024]{0:T(1024)S(1)} %broadcast_clamp_fusion), kind=kCustom, calls=%fused_computation.1 | custom fusion | bytes 3149824 | tf_op jit(solution)/shard_map/jit(_take)/gather | solution.py:36
  24.7 3.2 %convert_select_fusion = f32[1024,768]{1,0:T(8,128)} fusion(bf16[1024,768]{1,0:T(8,128)(2,1)} %gather_fusion.1, pred[1024]{0:T(1024)(128)(4,1)S(1)} %compare_and_fusion, pred[1024]{0:T(1024)(128)(4,1)S(1)} %bitcast.17), kind=kLoop, calls=%fused_computation.4 | loop fusion | flops 2359296 | bytes 4720640 | tf_op jit(solution)/shard_map/jit(_where)/select_n | solution.py:37
  27.9 138.1 %all-reduce.3 = (bf16[512,768]{1,0:T(8,128)(2,1)}, bf16[1024,768]{1,0:T(8,128)(2,1)}) all-reduce(f32[512,768]{1,0:T(8,128)} %convert_select_fusion.1, f32[1024,768]{1,0:T(8,128)} %convert_select_fusion), channel_id=1, replica_groups=mesh['blk_0'=2,'blk_1'=4,'rows'=32] {'blk_0','blk_1','rows'}, use_global_device_ids=true, to_apply=%region_0.1 | all-reduce | flops 1179648 | bytes 7077888 | tf_op jit(solution)/shard_map/psum | solution.py:46
  166.0 0.0 copy-start.1
  166.0 0.0 copy-start.3
  166.0 3.1 %multiply_reduce_fusion = f32[2048]{0:T(1024)S(1)} fusion(bf16[2048,768]{1,0:T(8,128)(2,1)S(1)} %copy-done, bf16[512,768]{1,0:T(8,128)(2,1)} %get-tuple-element.2), kind=kOutput, calls=%fused_computation.3 | convolution fusion | flops 1612707840 | bytes 3940352 | tf_op jit(solution)/shard_map/dot_general | solution.py:48
  169.1 0.0 copy-done.1
  169.1 0.0 copy-start.2
  169.2 0.0 copy-done.3
  169.2 3.9 %maximum_reduce_fusion = f32[1024]{0:T(1024)S(1)} fusion(bf16[2048,768]{1,0:T(8,128)(2,1)S(1)} %copy-done, f32[2048]{0:T(1024)S(1)} %max.18, bf16[1024,768]{1,0:T(8,128)(2,1)S(1)} %copy-done.3), kind=kOutput, calls=%fused_computation.2 | convolution fusion | flops 3229613056 | bytes 4730880 | tf_op jit(solution)/shard_map/dot_general | solution.py:54
  173.0 0.0 copy-done.2
  173.0 74.7 %all-reduce = f32[1024]{0:T(1024)S(1)} all-reduce(f32[1024]{0:T(1024)S(1)} %maximum_reduce_fusion), channel_id=3, replica_groups=mesh['blk_0'=2,'blk_1'=4,'rows'=32] {'blk_0','blk_1','rows'}, use_global_device_ids=true, to_apply=%region_4.5.clone | all-reduce | flops 1024 | bytes 8192
  247.8 0.6 dynamic-slice
  (9 shorter events, 0.1 us)
Async XLA Ops:
  0.6 1.9 copy-start
  2.5 5.3 %copy-start.4 = (s32[128]{0:T(128)S(1)}, s32[128]{0:T(128)}, u32[]{:S(2)}) copy-start(s32[128]{0:T(128)} %param.7) | copy-start | bytes 1540
  166.0 3.1 %copy-start.1 = (f32[2048]{0:T(1024)S(1)}, f32[2048]{0:T(1024)}, u32[]{:S(2)}) copy-start(f32[2048]{0:T(1024)} %param.5) | copy-start | bytes 24580
  166.0 3.1 %copy-start.3 = (bf16[1024,768]{1,0:T(8,128)(2,1)S(1)}, bf16[1024,768]{1,0:T(8,128)(2,1)}, u32[]{:S(2)}) copy-start(bf16[1024,768]{1,0:T(8,128)(2,1)} %get-tuple-element.3) | copy-start | bytes 4718596
  169.1 3.9 %copy-start.2 = (f32[2048]{0:T(1024)}, f32[2048]{0:T(1024)S(1)}, u32[]{:S(2)}) copy-start(f32[2048]{0:T(1024)S(1)} %max.18) | copy-start | bytes 24580
where the time goes:
time: 249 us; the launch traced here: 248 us
  blocking collectives  224 us (90%)
  local copies, waits for them, and re-layouts  9.6 us (4%)
  matrix products  6.95 us (3%)
  other arithmetic  6.67 us (3%)
    psum x1, blocking collectives, local(): lax.psum(owned_rows(embeddings, chosen_index, base_row), BLK_ROWS)  138 us
    unnamed x1, blocking collectives  74.7 us
    all_gather x2, blocking collectives, all_blocks(): pieces = lax.all_gather(pieces, axes[k], axis=0, tiled=True)  11.6 us
    gather x2, local copies, waits for them, and re-layouts, owned_rows(): picked = jnp.take(embeddings, safe, axis=0).astype(jnp.float32)  7.95 us
    select_n x2, other arithmetic, owned_rows(): return jnp.where(inside[:, None], picked, 0.0)  5.78 us

commit v1 on v0

v1 whole, which is shorter than its diff:
```python
import jax
import jax.numpy as jnp
from jax import lax
from jax.sharding import Mesh
from jax.sharding import PartitionSpec as P

AXES = ("ylo", "x", "yhi", "z", "core")
BLK = ("ylo", "x")
YHI_Z = ("yhi", "z")
YX = ("ylo", "x", "yhi")
MOST = 4
SWAP = [(0, 1), (1, 0)]


def local(embeddings, coverage, chosen_index, candidate_index):
    rows, width = embeddings.shape
    scale = 1.0 / width**0.5
    core = lax.axis_index("core")
    yhi = lax.axis_index("yhi")
    base = lax.axis_index(AXES) * rows

    off = chosen_index - base
    inside = (off >= 0) & (off < rows)
    rank = jnp.sum(inside[None, :] & (off[None, :] < off[:, None]), axis=1)
    slot = inside[None, :] & (rank[None, :] == jnp.arange(MOST)[:, None])
    spots = jnp.max(jnp.where(slot, off[None, :], -1), axis=1)
    targets = jnp.concatenate([candidate_index - base, spots, jnp.full((MOST,), -1, jnp.int32)])
    pick = (targets[:, None] == jnp.arange(rows)[None, :]).astype(jnp.bfloat16)
    picked = jnp.dot(pick, embeddings, preferred_element_type=jnp.float32).astype(jnp.bfloat16)

    cands = picked[:128].reshape(2, 2, 32, width)
    chosen = picked[128 : 128 + MOST]
    mine = lax.dynamic_index_in_dim(cands, core, 1, keepdims=False)
    theirs = lax.dynamic_index_in_dim(cands, 1 - core, 1, keepdims=False)
    half = mine + lax.ppermute(theirs, "core", SWAP)

    send = jnp.concatenate(
        [
            jnp.broadcast_to(half[:, None], (2, 8, 32, width)),
            jnp.broadcast_to(chosen, (2, 8, MOST, width)),
        ],
        axis=2,
    ).reshape(16, 32 + MOST, width)
    got = lax.all_to_all(send, YHI_Z, 0, 0)
    quarter = jnp.sum(got[:, :32].astype(jnp.float32), axis=0).astype(jnp.bfloat16)
    near = lax.dynamic_slice_in_dim(got[:, 32:], yhi * 8, 8, 0).reshape(8 * MOST, width)

    block = jnp.concatenate([quarter, near], axis=0)
    all_xy = lax.all_to_all(jnp.broadcast_to(block, (16, 64, width)), YX, 0, 0)
    other = lax.ppermute(all_xy, "core", SWAP)
    first = jnp.where(core == 0, all_xy, other)
    second = jnp.where(core == 0, other, all_xy)
    both = jnp.stack([first, second], axis=1)

    all_chosen = both[:, :, 32:].reshape(1024, width)
    all_cands = both[:, :, :32].reshape(1024, width)
    sims = jnp.dot(embeddings, all_chosen.T, preferred_element_type=jnp.float32) * scale
    new_coverage = jnp.maximum(coverage, jnp.max(sims, axis=1))
    cand_sims = jnp.dot(embeddings, all_cands.T, preferred_element_type=jnp.float32) * scale
    part = jnp.sum(jnp.maximum(cand_sims - new_coverage[:, None], 0.0), axis=0)
    parts = lax.all_to_all(part.reshape(256, 4), AXES, 0, 0)
    gains = jnp.sum(parts, axis=0)
    return new_coverage, gains


def solution(mesh):
    torus = Mesh(mesh.devices.reshape(2, 4, 2, 8, 2), AXES)
    return jax.shard_map(
        local,
        mesh=torus,
        in_specs=(P(AXES, None), P(AXES), P(), P(BLK)),
        out_specs=(P(AXES), P(AXES)),
        check_vma=False,
    )
```

time: 249 us -> 113 us (0.45)
  blocking collectives: 224 us -> 45.4 us
  waiting for transfers between devices: 0 us -> 29.6 us
  starting transfers between devices: 0 us -> 16.4 us
  local copies, waits for them, and re-layouts: 9.6 us -> 3.35 us
    psum x1 -> x0, blocking collectives: 138 us -> none  [local(): lax.psum(owned_rows(embeddings, chosen_index, base_row), BLK_ROWS)]
    unnamed x1 -> x0, blocking collectives: 74.7 us -> none
    all_to_all x0 -> x2, blocking collectives: none -> 45.4 us  [the longest x1 23.9 us: local(): all_xy = lax.all_to_all(jnp.broadcast_to(block, (16, 64, width)), YX, 0, 0)]
    all_to_all x0 -> x1, waiting for transfers between devices: none -> 25.5 us  [local(): got = lax.all_to_all(send, YHI_Z, 0, 0)]
    all_gather x2 -> x0, blocking collectives: 11.6 us -> none  [all_blocks(): pieces = lax.all_gather(pieces, axes[k], axis=0, tiled=True)]
    all_to_all x0 -> x1, starting transfers between devices: none -> 9.23 us  [local(): got = lax.all_to_all(send, YHI_Z, 0, 0)]
    gather x2 -> x0, local copies, waits for them, and re-layouts: 7.95 us -> none  [owned_rows(): picked = jnp.take(embeddings, safe, axis=0).astype(jnp.float32)]
    ppermute x0 -> x2, starting transfers between devices: none -> 7.14 us  [the longest x1 3.9 us: local(): other = lax.ppermute(all_xy, 'core', SWAP)]
  transfers between devices with their start and end apart: 0 -> 3, of which waited for: 0 -> 3; matrix products, arithmetic and copies ran while one was open for 0% -> 1% of each run, Pallas kernels for 0% -> 0%
where the time goes in v1:
time: 113 us; the launch traced here: 112 us
  blocking collectives  45.4 us (40%)
  waiting for transfers between devices  29.6 us (26%)
  starting transfers between devices  16.4 us (15%)
  other arithmetic  8.44 us (7%)
  matrix products  8.23 us (7%)
  local copies, waits for them, and re-layouts  3.35 us (3%)
    all_to_all x1, waiting for transfers between devices, local(): got = lax.all_to_all(send, YHI_Z, 0, 0)  25.5 us
    all_to_all x1, blocking collectives, local(): all_xy = lax.all_to_all(jnp.broadcast_to(block, (16, 64, width)), YX, 0, 0)  23.9 us
    all_to_all x1, blocking collectives, local(): parts = lax.all_to_all(part.reshape(256, 4), AXES, 0, 0)  21.5 us
    all_to_all x1, starting transfers between devices, local(): got = lax.all_to_all(send, YHI_Z, 0, 0)  9.23 us
    ppermute x1, starting transfers between devices, local(): other = lax.ppermute(all_xy, 'core', SWAP)  3.9 us
    dot_general x1, matrix products, local(): jnp.dot(embeddings, all_cands.T, preferred_element_type=jnp.float32) * scale  3.87 us
    dot_general x1, matrix products, local(): jnp.dot(embeddings, all_chosen.T, preferred_element_type=jnp.float32)  3.7 us
    ppermute x1, waiting for transfers between devices, local(): other = lax.ppermute(all_xy, 'core', SWAP)  3.38 us
  transfers between devices with their start and end apart: 3, of which 3 were waited for; matrix products, arithmetic and copies ran while one was open for 1% of the time, Pallas kernels for 0%

profile of v1, /device:TPU:1, one launch (start us, length us, event | category | flops | bytes accessed | tf_op | source)
XLA Modules:
  0.0 112.2 jit_solution(14303009496489343337)
XLA Ops:
  0.7 0.8 broadcast_subtract_fusion.1
  1.5 0.8 compare_and_fusion
  2.3 0.3 convert_reduce_fusion
  2.8 0.7 convolution_convert_fusion
  3.5 0.6 dynamic-slice_bitcast_fusion
  4.1 3.2 %collective-permute-start = (bf16[2,32,768]{2,1,0:T(8,128)(2,1)}, bf16[2,32,768]{2,1,0:T(8,128)(2,1)}, u32[]{:S(2)}, u32[]{:S(2)}) collective-permute-start(bf16[2,32,768]{2,1,0:T(8,128)(2,1)} %dynamic-slice_bitcast_fusion), channel_id=1, source_target_pairs={{0,1},{1,0},{2,3},{3,2},{4,5},{5,4},{6,7},{7,6},{8,9},{9,8},{10,11... | collective-permute-start | bytes 294920 | tf_op jit(solution)/shard_map/ppermute | solution.py:35
  7.4 0.6 slice.25
  8.0 0.7 collective-permute-done
  8.6 0.9 bitcast_add_fusion
  9.6 0.7 broadcast_in_dim.21
  10.4 1.1 pad_maximum_fusion.1
  11.4 9.2 %all-to-all-start = ((bf16[16,36,768]{2,1,0:T(8,128)(2,1)}), bf16[16,36,768]{2,1,0:T(8,128)(2,1)}, u32[]{:S(2)}, u32[]{:S(2)}) async-start(bf16[16,36,768]{2,1,0:T(8,128)(2,1)} %bitcast.20), calls=%async_computation | async-start | bytes 1966080 | tf_op jit(solution)/shard_map/all_to_all | solution.py:44
  20.7 25.5 %all-to-all-done = bf16[16,36,768]{2,1,0:T(8,128)(2,1)} async-done(((bf16[16,36,768]{2,1,0:T(8,128)(2,1)}), bf16[16,36,768]{2,1,0:T(8,128)(2,1)}, u32[]{:S(2)}, u32[]{:S(2)}) %all-to-all-start) | async-done | bytes 884768 | tf_op jit(solution)/shard_map/all_to_all | solution.py:44
  46.2 1.0 slice.27
  47.2 1.3 %slice_reduce_fusion = bf16[32,768]{1,0:T(8,128)(2,1)S(1)} fusion(bf16[16,36,768]{2,1,0:T(8,128)(2,1)} %all-to-all-done), kind=kLoop, calls=%fused_computation.12 | loop fusion | flops 368640 | bytes 835584 | tf_op jit(solution)/shard_map/reduce_sum | solution.py:45
  48.7 23.9 %all_to_all.19 = bf16[16,64,768]{2,1,0:T(8,128)(2,1)} all-to-all(bf16[16,64,768]{2,1,0:T(8,128)(2,1)S(1)} %broadcast_in_dim.22), channel_id=1, replica_groups=mesh['ylo'=2,'x'=4,'yhi'=2,'z'=8,'core'=2] {'ylo','x','yhi'}, dimensions={0} | all-to-all | bytes 3145728 | tf_op jit(solution)/shard_map/all_to_all | solution.py:49
  72.5 3.9 %collective-permute-start.1 = (bf16[16,64,768]{2,1,0:T(8,128)(2,1)}, bf16[16,64,768]{2,1,0:T(8,128)(2,1)}, u32[]{:S(2)}, u32[]{:S(2)}) collective-permute-start(bf16[16,64,768]{2,1,0:T(8,128)(2,1)} %all_to_all.19), channel_id=1, source_target_pairs={{0,1},{1,0},{2,3},{3,2},{4,5},{5,4},{6,7},{7,6},{8,9},{9,8},{10,11... | collective-permute-start | bytes 4718600 | tf_op jit(solution)/shard_map/ppermute | solution.py:50
  76.4 3.4 %collective-permute-done.1 = bf16[16,64,768]{2,1,0:T(8,128)(2,1)} collective-permute-done((bf16[16,64,768]{2,1,0:T(8,128)(2,1)}, bf16[16,64,768]{2,1,0:T(8,128)(2,1)}, u32[]{:S(2)}, u32[]{:S(2)}) %collective-permute-start.1) | collective-permute-done | bytes 1572896 | tf_op jit(solution)/shard_map/ppermute | solution.py:50
  79.8 2.1 %select_bitcast_fusion = (bf16[16,1,64,768]{3,2,1,0:T(8,128)(2,1)S(1)}, bf16[16,1,64,768]{3,2,1,0:T(8,128)(2,1)S(1)}) fusion(bf16[16,64,768]{2,1,0:T(8,128)(2,1)} %collective-permute-done.1, bf16[16,64,768]{2,1,0:T(8,128)(2,1)} %all_to_all.19, pred[]{:T(512)S(6)} %eq.14), kind=kLoop, calls=%fused_computation.6 | loop fusion | flops 1572864 | bytes 6291457 | tf_op jit(solution)/shard_map/stack | solution.py:53
  81.9 0.2 pad_maximum_fusion
  82.1 3.7 %multiply_reduce_fusion = f32[2048]{0:T(1024)S(1)} fusion(bf16[1024,768]{1,0:T(8,128)(2,1)S(1)} %bitcast.22, bf16[2048,768]{1,0:T(8,128)(2,1)S(1)} %copy-done), kind=kOutput, calls=%fused_computation.1 | convolution fusion | flops 3225417728 | bytes 4726784 | tf_op jit(solution)/shard_map/dot_general | solution.py:57
  85.9 3.9 %maximum_reduce_fusion = f32[1024]{0:T(1024)S(1)} fusion(bf16[1024,768]{1,0:T(8,128)(2,1)S(1)} %bitcast.21, bf16[2048,768]{1,0:T(8,128)(2,1)S(1)} %copy-done, f32[2048]{0:T(1024)S(1)} %max.10), kind=kOutput, calls=%fused_computation | convolution fusion | flops 3229613056 | bytes 4730880 | tf_op jit(solution)/shard_map/dot_general | solution.py:59
  89.9 21.5 %all_to_all.20 = f32[256,1,4]{2,1,0:T(1,128)S(1)} all-to-all(f32[256,1,4]{2,1,0:T(1,128)S(1)} %bitcast.25), channel_id=1, replica_groups=mesh['ylo'=2,'x'=4,'yhi'=2,'z'=8,'core'=2] {'ylo','x','yhi','z','core'}, dimensions={0} | all-to-all | bytes 8192 | tf_op jit(solution)/shard_map/all_to_all | solution.py:61
  111.4 0.8 reduce_sum.42
  (17 shorter events, 0.7 us)
Async XLA Ops:
  0.6 2.2 %copy-start = (bf16[2048,768]{1,0:T(8,128)(2,1)S(1)}, bf16[2048,768]{1,0:T(8,128)(2,1)}, u32[]{:S(2)}) copy-start(bf16[2048,768]{1,0:T(8,128)(2,1)} %param.4) | copy-start | bytes 9437188
  4.1 4.5 %collective-permute-start = (bf16[2,32,768]{2,1,0:T(8,128)(2,1)}, bf16[2,32,768]{2,1,0:T(8,128)(2,1)}, u32[]{:S(2)}, u32[]{:S(2)}) collective-permute-start(bf16[2,32,768]{2,1,0:T(8,128)(2,1)} %dynamic-slice_bitcast_fusion), channel_id=1, source_target_pairs={{0,1},{1,0},{2,3},{3,2},{4,5},{5,4},{6,7},{7,6},{8,9},{9,8},{10,11... | collective-permute-start | bytes 294920 | tf_op jit(solution)/shard_map/ppermute | solution.py:35
  11.4 34.8 %all-to-all-start = ((bf16[16,36,768]{2,1,0:T(8,128)(2,1)}), bf16[16,36,768]{2,1,0:T(8,128)(2,1)}, u32[]{:S(2)}, u32[]{:S(2)}) async-start(bf16[16,36,768]{2,1,0:T(8,128)(2,1)} %bitcast.20), calls=%async_computation | async-start | bytes 1966080 | tf_op jit(solution)/shard_map/all_to_all | solution.py:44
  72.5 7.3 %collective-permute-start.1 = (bf16[16,64,768]{2,1,0:T(8,128)(2,1)}, bf16[16,64,768]{2,1,0:T(8,128)(2,1)}, u32[]{:S(2)}, u32[]{:S(2)}) collective-permute-start(bf16[16,64,768]{2,1,0:T(8,128)(2,1)} %all_to_all.19), channel_id=1, source_target_pairs={{0,1},{1,0},{2,3},{3,2},{4,5},{5,4},{6,7},{7,6},{8,9},{9,8},{10,11... | collective-permute-start | bytes 4718600 | tf_op jit(solution)/shard_map/ppermute | solution.py:50
  82.1 3.7 %copy-start.1 = (f32[2048]{0:T(1024)S(1)}, f32[2048]{0:T(1024)}, u32[]{:S(2)}) copy-start(f32[2048]{0:T(1024)} %param.5) | copy-start | bytes 24580
  85.8 3.9 %copy-start.2 = (f32[2048]{0:T(1024)}, f32[2048]{0:T(1024)S(1)}, u32[]{:S(2)}) copy-start(f32[2048]{0:T(1024)S(1)} %max.10) | copy-start | bytes 24580

commit v2 on v1

v2 whole, which is shorter than its diff:
```python
import jax
import jax.numpy as jnp
from jax import lax
from jax.sharding import Mesh
from jax.sharding import PartitionSpec as P

AXES = ("ylo", "x", "yhi", "z", "core")
SIZES = (2, 4, 2, 8, 2)
BLK = ("ylo", "x")
CHIPS = ("ylo", "x", "yhi", "z")
MOST = 4


def place(y, x, z, core):
    return (((y % 2) * 4 + x) * 2 + y // 2) * 16 + z * 2 + core


def pairs_of(move):
    return [
        (place(y, x, z, core), place(*move(y, x, z, core)))
        for y in range(4)
        for x in range(4)
        for z in range(8)
        for core in range(2)
    ]


def swap(value, y_mask, core_mask):
    return lax.ppermute(value, AXES, pairs_of(lambda y, x, z, c: (y ^ y_mask, x, z, c ^ core_mask)))


def turn(value, mask, first):
    return lax.ppermute(
        value,
        AXES,
        pairs_of(lambda y, x, z, c: (y, x ^ mask, z, c) if (c == 0) == first else (y ^ mask, x, z, c)),
    )


def flipped(flag, value, dim):
    return jnp.where(flag == 1, jnp.flip(value, dim), value)


def local(embeddings, coverage, chosen_index, candidate_index):
    rows, width = embeddings.shape
    scale = 1.0 / width**0.5
    core = lax.axis_index("core")
    yhi = lax.axis_index("yhi")
    ylo = lax.axis_index("ylo")
    x = lax.axis_index("x")
    base = lax.axis_index(AXES) * rows

    partner = swap(embeddings, 0, 1)

    off = chosen_index - base
    inside = (off >= 0) & (off < rows)
    rank = jnp.sum(inside[None, :] & (off[None, :] < off[:, None]), axis=1)
    slot = inside[None, :] & (rank[None, :] == jnp.arange(MOST)[:, None])
    spots = jnp.max(jnp.where(slot, off[None, :], -1), axis=1)
    wanted = (candidate_index - base).reshape(2, 8, 2, 4).transpose(0, 2, 1, 3)
    wanted = flipped(yhi, flipped(core, wanted, 1), 0).reshape(128)
    targets = jnp.concatenate([wanted, spots, jnp.full((MOST,), -1, jnp.int32)])
    pick = (targets[:, None] == jnp.arange(rows)[None, :]).astype(jnp.bfloat16)
    picked = jnp.dot(pick, embeddings, preferred_element_type=jnp.float32).astype(jnp.bfloat16)

    quarter = (
        picked[:32]
        + swap(picked[32:64], 0, 1)
        + swap(picked[64:96], 2, 0)
        + swap(picked[96:128], 2, 1)
    )
    send = jnp.concatenate([quarter, picked[128 : 128 + MOST]], axis=0)
    got = lax.all_to_all(jnp.broadcast_to(send, (8, 32 + MOST, width)), "z", 0, 0)
    quarter = jnp.sum(got[:, :32].astype(jnp.float32), axis=0).astype(jnp.bfloat16)
    near = got[:, 32:].reshape(8 * MOST, width)

    block = jnp.concatenate([quarter, near], axis=0)
    line = jnp.stack([block] + [turn(block, s, True) for s in (1, 2, 3)])
    plane = [line] + [turn(line, s, False) for s in (1, 2, 3)]
    cands = jnp.concatenate([p[:, :32] for p in plane]).reshape(512, width)
    chosen = jnp.concatenate([p[:, 32:] for p in plane]).reshape(512, width)

    def best(table):
        return jnp.max(jnp.dot(table, chosen.T, preferred_element_type=jnp.float32) * scale, axis=1)

    best_own = jnp.maximum(coverage, best(embeddings))
    best_partner = best(partner)
    swapped = swap(jnp.stack([best_own, best_partner]), 0, 1)
    new_coverage = jnp.maximum(best_own, swapped[1])
    cover_partner = jnp.maximum(best_partner, swapped[0])

    def gain(table, cover):
        sims = jnp.dot(table, cands.T, preferred_element_type=jnp.float32) * scale
        return jnp.sum(jnp.maximum(sims - cover[:, None], 0.0), axis=0)

    part = gain(embeddings, new_coverage) + gain(partner, cover_partner)
    part = part.reshape(4, 4, 32)
    part = jnp.where(core == 0, part, part.transpose(1, 0, 2)).reshape(2, 2, 2, 2, 32)
    part = flipped(ylo, flipped(yhi, part, 0), 1)
    part = flipped(x % 2, flipped(x // 2, part, 2), 3)
    part = part.transpose(1, 2, 3, 0, 4).reshape(128, 4)
    parts = lax.all_to_all(part, CHIPS, 0, 0)
    return new_coverage, jnp.sum(parts, axis=0)


def solution(mesh):
    torus = Mesh(mesh.devices.reshape(SIZES), AXES)
    return jax.shard_map(
        local,
        mesh=torus,
        in_specs=(P(AXES, None), P(AXES), P(), P(BLK)),
        out_specs=(P(AXES), P(AXES)),
        check_vma=False,
    )
```

time: 113 us -> 101 us (0.89)
  waiting for transfers between devices: 29.6 us -> 16 us
  matrix products: 8.23 us -> 15.1 us
  starting transfers between devices: 16.4 us -> 22.1 us
  blocking collectives: 45.4 us -> 40.1 us
  other arithmetic: 8.44 us -> 4.97 us
  local copies, waits for them, and re-layouts: 3.35 us -> 1.48 us
    all_to_all x1 -> x0, waiting for transfers between devices: 25.5 us -> none  [local(): got = lax.all_to_all(send, YHI_Z, 0, 0)]
    ppermute x2 -> x11, starting transfers between devices: 7.14 us -> 22.1 us  [the longest x5 14.2 us: swap(): lax.ppermute(value, AXES, pairs_of(lambda y, x, z, c: (y ^ y_mask, x, z,...]
    ppermute x2 -> x11, waiting for transfers between devices: 4.07 us -> 16 us  [the longest x6 12.2 us: turn(): lax.ppermute(value, AXES, pairs_of(lambda y, x, z, c: (y, x ^ mask, z, c)...]
    all_to_all x1 -> x0, starting transfers between devices: 9.23 us -> none  [local(): got = lax.all_to_all(send, YHI_Z, 0, 0)]
    all_to_all x2, blocking collectives: 45.4 us -> 40.1 us  [the longest x1 23.9 us: local(): lax.all_to_all(jnp.broadcast_to(send, (8, 32 + MOST, width)), 'z', 0, 0)]
    dot_general x2 -> x4, matrix products: 7.57 us -> 12.5 us  [the longest x2 6.96 us: gain(): sims = jnp.dot(table, cands.T, preferred_element_type=jnp.float32) * scale]
    another operation x2 -> x3, other arithmetic: 2.29 us -> 0.09 us  [the longest x2 0.07 us: local(): line = jnp.stack([block] + [turn(block, s, True) for s in (1, 2, 3)])]
    dot_general x1, matrix products: 0.66 us -> 2.55 us  [local(): jnp.dot(pick, embeddings, preferred_element_type=jnp.float32)]
  transfers between devices with their start and end apart: 3 -> 11, of which waited for: 3 -> 8; matrix products, arithmetic and copies ran while one was open for 1% -> 4% of each run, Pallas kernels for 0% -> 0%
where the time goes in v2:
time: 101 us
  blocking collectives  40.1 us (40%)
  starting transfers between devices  22.1 us (22%)
  waiting for transfers between devices  16 us (16%)
  matrix products  15.1 us (15%)
  other arithmetic  4.97 us (5%)
  local copies, waits for them, and re-layouts  1.48 us (1%)
    all_to_all x1, blocking collectives, local(): lax.all_to_all(jnp.broadcast_to(send, (8, 32 + MOST, width)), 'z', 0, 0)  23.9 us
    all_to_all x1, blocking collectives, local(): parts = lax.all_to_all(part, CHIPS, 0, 0)  16.1 us
    ppermute x5, starting transfers between devices, swap(): lax.ppermute(value, AXES, pairs_of(lambda y, x, z, c: (y ^ y_mask, x, z,...  14.2 us
    ppermute x6, waiting for transfers between devices, turn(): lax.ppermute(value, AXES, pairs_of(lambda y, x, z, c: (y, x ^ mask, z, c)...  12.2 us
    ppermute x6, starting transfers between devices, turn(): lax.ppermute(value, AXES, pairs_of(lambda y, x, z, c: (y, x ^ mask, z, c)...  7.89 us
    dot_general x2, matrix products, gain(): sims = jnp.dot(table, cands.T, preferred_element_type=jnp.float32) * scale  6.96 us
    dot_general x2, matrix products, best(): jnp.dot(table, chosen.T, preferred_element_type=jnp.float32) * scale  5.56 us
    ppermute x5, waiting for transfers between devices, swap(): lax.ppermute(value, AXES, pairs_of(lambda y, x, z, c: (y ^ y_mask, x, z,...  3.86 us
  transfers between devices with their start and end apart: 11, of which 8 were waited for; matrix products, arithmetic and copies ran while one was open for 4% of the time, Pallas kernels for 0%

profile of v2, /device:TPU:1, one launch (start us, length us, event | category | flops | bytes accessed | tf_op | source)
XLA Modules:
  0.0 100.6 jit_solution(16033907057233438868)
XLA Ops:
  3.0 2.5 %convolution_convert_fusion = bf16[136,768]{1,0:T(8,128)(2,1)S(1)} fusion(bf16[2048,768]{1,0:T(8,128)(2,1)} %param.4, s32[136]{0:T(256)S(1)} %pad_add_fusion), kind=kOutput, calls=%fused_computation.4 | convolution fusion | flops 428201984 | bytes 3355168 | tf_op jit(solution)/shard_map/dot_general | solution.py:64
  5.6 3.3 %collective-permute-start = (bf16[32,768]{1,0:T(8,128)(2,1)S(1)}, bf16[32,768]{1,0:T(8,128)(2,1)S(1)}, u32[]{:S(2)}, u32[]{:S(2)}) collective-permute-start(bf16[32,768]{1,0:T(8,128)(2,1)S(1)} %get-tuple-element.12), channel_id=1, source_target_pairs={{0,1},{1,0},{2,3},{3,2},{4,5},{5,4},{6,7},{7,6},{8,9},{9,8},{10,11... | collective-permute-start | bytes 147464 | tf_op jit(solution)/shard_map/ppermute | solution.py:29
  8.9 1.2 %collective-permute-start.1 = (bf16[32,768]{1,0:T(8,128)(2,1)S(1)}, bf16[32,768]{1,0:T(8,128)(2,1)S(1)}, u32[]{:S(2)}, u32[]{:S(2)}) collective-permute-start(bf16[32,768]{1,0:T(8,128)(2,1)S(1)} %get-tuple-element.14), channel_id=1, source_target_pairs={{0,16},{1,17},{2,18},{3,19},{4,20},{5,21},{6,22},{7,23},{8,24},{9,... | collective-permute-start | bytes 147464 | tf_op jit(solution)/shard_map/ppermute | solution.py:29
  10.1 2.0 %collective-permute-start.2 = (bf16[32,768]{1,0:T(8,128)(2,1)S(1)}, bf16[32,768]{1,0:T(8,128)(2,1)S(1)}, u32[]{:S(2)}, u32[]{:S(2)}) collective-permute-start(bf16[32,768]{1,0:T(8,128)(2,1)S(1)} %get-tuple-element.13), channel_id=1, source_target_pairs={{0,17},{1,16},{2,19},{3,18},{4,21},{5,20},{6,23},{7,22},{8,25},{9,... | collective-permute-start | bytes 147464 | tf_op jit(solution)/shard_map/ppermute | solution.py:29
  12.3 1.1 %collective-permute-done.1 = bf16[32,768]{1,0:T(8,128)(2,1)S(1)} collective-permute-done((bf16[32,768]{1,0:T(8,128)(2,1)S(1)}, bf16[32,768]{1,0:T(8,128)(2,1)S(1)}, u32[]{:S(2)}, u32[]{:S(2)}) %collective-permute-start.1) | collective-permute-done | bytes 49184 | tf_op jit(solution)/shard_map/ppermute | solution.py:29
  13.4 2.0 %collective-permute-done.2 = bf16[32,768]{1,0:T(8,128)(2,1)S(1)} collective-permute-done((bf16[32,768]{1,0:T(8,128)(2,1)S(1)}, bf16[32,768]{1,0:T(8,128)(2,1)S(1)}, u32[]{:S(2)}, u32[]{:S(2)}) %collective-permute-start.2) | collective-permute-done | bytes 49184 | tf_op jit(solution)/shard_map/ppermute | solution.py:29
  15.4 23.9 %all_to_all.14 = bf16[8,36,768]{2,1,0:T(8,128)(2,1)S(1)} all-to-all(bf16[8,36,768]{2,1,0:T(8,128)(2,1)S(1)} %broadcast_in_dim.16), channel_id=1, replica_groups=mesh['ylo'=2,'x'=4,'yhi'=2,'z'=8,'core'=2] {'z'}, dimensions={0} | all-to-all | bytes 884736 | tf_op jit(solution)/shard_map/all_to_all | solution.py:73
  40.2 1.1 %slice_reduce_fusion = bf16[32,768]{1,0:T(8,128)(2,1)S(1)} fusion(bf16[8,36,768]{2,1,0:T(8,128)(2,1)} %copy-done.1), kind=kLoop, calls=%fused_computation.10 | loop fusion | flops 172032 | bytes 442368 | tf_op jit(solution)/shard_map/reduce_sum | solution.py:74
  41.7 1.7 %collective-permute-start.4 = (bf16[64,768]{1,0:T(8,128)(2,1)S(1)}, bf16[64,768]{1,0:T(8,128)(2,1)S(1)}, u32[]{:S(2)}, u32[]{:S(2)}) collective-permute-start(bf16[64,768]{1,0:T(8,128)(2,1)S(1)} %get-tuple-element.16), channel_id=1, source_target_pairs={{0,64},{1,17},{2,66},{3,19},{4,68},{5,21},{6,70},{7,23},{8,72},{9,... | collective-permute-start | bytes 294920 | tf_op jit(solution)/shard_map/ppermute | solution.py:33
  43.4 1.8 %collective-permute-start.5 = (bf16[64,768]{1,0:T(8,128)(2,1)S(1)}, bf16[64,768]{1,0:T(8,128)(2,1)S(1)}, u32[]{:S(2)}, u32[]{:S(2)}) collective-permute-start(bf16[64,768]{1,0:T(8,128)(2,1)S(1)} %get-tuple-element.16), channel_id=1, source_target_pairs={{0,96},{1,145},{2,98},{3,147},{4,100},{5,149},{6,102},{7,151},{8,1... | collective-permute-start | bytes 294920 | tf_op jit(solution)/shard_map/ppermute | solution.py:33
  45.2 1.5 %collective-permute-done.4 = bf16[64,768]{1,0:T(8,128)(2,1)S(1)} collective-permute-done((bf16[64,768]{1,0:T(8,128)(2,1)S(1)}, bf16[64,768]{1,0:T(8,128)(2,1)S(1)}, u32[]{:S(2)}, u32[]{:S(2)}) %collective-permute-start.4) | collective-permute-done | bytes 98336 | tf_op jit(solution)/shard_map/ppermute | solution.py:33
  46.7 1.4 %collective-permute-done.5 = bf16[64,768]{1,0:T(8,128)(2,1)S(1)} collective-permute-done((bf16[64,768]{1,0:T(8,128)(2,1)S(1)}, bf16[64,768]{1,0:T(8,128)(2,1)S(1)}, u32[]{:S(2)}, u32[]{:S(2)}) %collective-permute-start.5) | collective-permute-done | bytes 98336 | tf_op jit(solution)/shard_map/ppermute | solution.py:33
  48.1 2.6 %collective-permute-start.8 = (bf16[4,64,768]{2,1,0:T(8,128)(2,1)S(1)}, bf16[4,64,768]{2,1,0:T(8,128)(2,1)S(1)}, u32[]{:S(2)}, u32[]{:S(2)}) collective-permute-start(bf16[4,64,768]{2,1,0:T(8,128)(2,1)S(1)} %pad_maximum_fusion.2), channel_id=1, source_target_pairs={{0,144},{1,97},{2,146},{3,99},{4,148},{5,101},{6,150},{7,103},{8,1... | collective-permute-start | bytes 1179656 | tf_op jit(solution)/shard_map/ppermute | solution.py:33
  50.7 1.4 %collective-permute-start.7 = (bf16[4,64,768]{2,1,0:T(8,128)(2,1)S(1)}, bf16[4,64,768]{2,1,0:T(8,128)(2,1)S(1)}, u32[]{:S(2)}, u32[]{:S(2)}) collective-permute-start(bf16[4,64,768]{2,1,0:T(8,128)(2,1)S(1)} %pad_maximum_fusion.2), channel_id=1, source_target_pairs={{0,16},{1,65},{2,18},{3,67},{4,20},{5,69},{6,22},{7,71},{8,24},{9,... | collective-permute-start | bytes 1179656 | tf_op jit(solution)/shard_map/ppermute | solution.py:33
  52.1 4.6 %collective-permute-done.8 = bf16[4,64,768]{2,1,0:T(8,128)(2,1)S(1)} collective-permute-done((bf16[4,64,768]{2,1,0:T(8,128)(2,1)S(1)}, bf16[4,64,768]{2,1,0:T(8,128)(2,1)S(1)}, u32[]{:S(2)}, u32[]{:S(2)}) %collective-permute-start.8) | collective-permute-done | bytes 393248 | tf_op jit(solution)/shard_map/ppermute | solution.py:33
  56.7 0.9 collective-permute-done.6
  57.6 3.8 %collective-permute-done.7 = bf16[4,64,768]{2,1,0:T(8,128)(2,1)S(1)} collective-permute-done((bf16[4,64,768]{2,1,0:T(8,128)(2,1)S(1)}, bf16[4,64,768]{2,1,0:T(8,128)(2,1)S(1)}, u32[]{:S(2)}, u32[]{:S(2)}) %collective-permute-start.7) | collective-permute-done | bytes 393248 | tf_op jit(solution)/shard_map/ppermute | solution.py:33
  61.5 1.1 %pad_maximum_fusion = (bf16[16,32,768]{2,1,0:T(8,128)(2,1)S(1)}, bf16[16,32,768]{2,1,0:T(8,128)(2,1)}) fusion(bf16[4,32,768]{2,1,0:T(8,128)(2,1)S(1)} %get-tuple-element.11, bf16[4,32,768]{2,1,0:T(8,128)(2,1)S(1)} %get-tuple-element.9, bf16[4,32,768]{2,1,0:T(8,128)(2,1)S(1)} %get-tuple-element.7, bf16[4,32,768]{2,1,0:T(8,128)(2,1)S(1)} %get-tuple-element.5, ...), kind=kLoop, calls=%fused_computation.7 | loop fusion | flops 2359296 | bytes 3145728 | tf_op jit(solution)/shard_map/concatenate | solution.py:81
  62.6 1.8 %multiply_reduce_fusion.1 = f32[2048]{0:T(1024)S(1)} fusion(bf16[512,768]{1,0:T(8,128)(2,1)S(1)} %bitcast.32, bf16[2048,768]{1,0:T(8,128)(2,1)S(1)} %copy-done), kind=kOutput, calls=%fused_computation.3 | convolution fusion | flops 1612707840 | bytes 3940352 | tf_op jit(solution)/shard_map/dot_general | solution.py:84
  64.4 3.7 %multiply_reduce_fusion = f32[2048]{0:T(1024)S(1)} fusion(bf16[512,768]{1,0:T(8,128)(2,1)S(1)} %bitcast.33, bf16[2048,768]{1,0:T(8,128)(2,1)} %collective-permute-done.9), kind=kOutput, calls=%fused_computation.2 | convolution fusion | flops 1612707840 | bytes 3940352 | tf_op jit(solution)/shard_map/dot_general | solution.py:84
  68.2 7.5 %collective-permute-start.10 = (f32[2,2048]{1,0:T(2,128)S(1)}, f32[2,2048]{1,0:T(2,128)S(1)}, u32[]{:S(2)}, u32[]{:S(2)}) collective-permute-start(f32[2,2048]{1,0:T(2,128)S(1)} %pad_maximum_fusion.5), channel_id=1, source_target_pairs={{0,1},{1,0},{2,3},{3,2},{4,5},{5,4},{6,7},{7,6},{8,9},{9,8},{10,11... | collective-permute-start | bytes 49160 | tf_op jit(solution)/shard_map/ppermute | solution.py:29
  76.6 3.1 %maximum_reduce_fusion.1 = f32[512]{0:T(512)S(1)} fusion(f32[2048]{0:T(1024)S(1)} %max.22, bf16[512,768]{1,0:T(8,128)(2,1)} %bitcast.30, bf16[2048,768]{1,0:T(8,128)(2,1)S(1)} %copy-done), kind=kOutput, calls=%fused_computation.1 | convolution fusion | flops 1614806528 | bytes 3942400 | tf_op jit(solution)/shard_map/dot_general | solution.py:93
  79.7 3.8 %maximum_reduce_fusion = f32[512]{0:T(512)S(1)} fusion(f32[2048]{0:T(1024)S(1)} %max.24, bf16[512,768]{1,0:T(8,128)(2,1)S(1)} %bitcast.31, bf16[2048,768]{1,0:T(8,128)(2,1)} %collective-permute-done.9), kind=kOutput, calls=%fused_computation | convolution fusion | flops 1614806528 | bytes 3942400 | tf_op jit(solution)/shard_map/dot_general | solution.py:93
  83.9 16.1 %all_to_all.15 = f32[128,1,4]{2,1,0:T(1,128)S(1)} all-to-all(f32[128,1,4]{2,1,0:T(1,128)S(1)} %bitcast.34), channel_id=1, replica_groups=mesh['ylo'=2,'x'=4,'yhi'=2,'z'=8,'core'=2] {'ylo','x','yhi','z'}, dimensions={0} | all-to-all | bytes 4096 | tf_op jit(solution)/shard_map/all_to_all | solution.py:102
  (58 shorter events, 5.8 us)
Async XLA Ops:
  0.6 11.5 %copy-start = (bf16[2048,768]{1,0:T(8,128)(2,1)S(1)}, bf16[2048,768]{1,0:T(8,128)(2,1)}, u32[]{:S(2)}) copy-start(bf16[2048,768]{1,0:T(8,128)(2,1)} %param.4) | copy-start | bytes 9437188
  5.6 6.7 %collective-permute-start = (bf16[32,768]{1,0:T(8,128)(2,1)S(1)}, bf16[32,768]{1,0:T(8,128)(2,1)S(1)}, u32[]{:S(2)}, u32[]{:S(2)}) collective-permute-start(bf16[32,768]{1,0:T(8,128)(2,1)S(1)} %get-tuple-element.12), channel_id=1, source_target_pairs={{0,1},{1,0},{2,3},{3,2},{4,5},{5,4},{6,7},{7,6},{8,9},{9,8},{10,11... | collective-permute-start | bytes 147464 | tf_op jit(solution)/shard_map/ppermute | solution.py:29
  8.9 4.5 %collective-permute-start.1 = (bf16[32,768]{1,0:T(8,128)(2,1)S(1)}, bf16[32,768]{1,0:T(8,128)(2,1)S(1)}, u32[]{:S(2)}, u32[]{:S(2)}) collective-permute-start(bf16[32,768]{1,0:T(8,128)(2,1)S(1)} %get-tuple-element.14), channel_id=1, source_target_pairs={{0,16},{1,17},{2,18},{3,19},{4,20},{5,21},{6,22},{7,23},{8,24},{9,... | collective-permute-start | bytes 147464 | tf_op jit(solution)/shard_map/ppermute | solution.py:29
  10.1 5.2 %collective-permute-start.2 = (bf16[32,768]{1,0:T(8,128)(2,1)S(1)}, bf16[32,768]{1,0:T(8,128)(2,1)S(1)}, u32[]{:S(2)}, u32[]{:S(2)}) collective-permute-start(bf16[32,768]{1,0:T(8,128)(2,1)S(1)} %get-tuple-element.13), channel_id=1, source_target_pairs={{0,17},{1,16},{2,19},{3,18},{4,21},{5,20},{6,23},{7,22},{8,25},{9,... | collective-permute-start | bytes 147464 | tf_op jit(solution)/shard_map/ppermute | solution.py:29
  12.1 52.3 %collective-permute-start.9 = (bf16[2048,768]{1,0:T(8,128)(2,1)S(1)}, bf16[2048,768]{1,0:T(8,128)(2,1)}, u32[]{:S(2)}, u32[]{:S(2)}) collective-permute-start(bf16[2048,768]{1,0:T(8,128)(2,1)S(1)} %copy-done), channel_id=1, source_target_pairs={{0,1},{1,0},{2,3},{3,2},{4,5},{5,4},{6,7},{7,6},{8,9},{9,8},{10,11... | collective-permute-start | bytes 9437192 | tf_op jit(solution)/shard_map/ppermute | solution.py:29
  39.3 0.8 copy-start.1
  41.2 3.9 %collective-permute-start.3 = (bf16[64,768]{1,0:T(8,128)(2,1)S(1)}, bf16[64,768]{1,0:T(8,128)(2,1)S(1)}, u32[]{:S(2)}, u32[]{:S(2)}) collective-permute-start(bf16[64,768]{1,0:T(8,128)(2,1)S(1)} %get-tuple-element.16), channel_id=1, source_target_pairs={{0,32},{1,129},{2,34},{3,131},{4,36},{5,133},{6,38},{7,135},{8,40}... | collective-permute-start | bytes 294920 | tf_op jit(solution)/shard_map/ppermute | solution.py:33
  41.7 5.0 %collective-permute-start.4 = (bf16[64,768]{1,0:T(8,128)(2,1)S(1)}, bf16[64,768]{1,0:T(8,128)(2,1)S(1)}, u32[]{:S(2)}, u32[]{:S(2)}) collective-permute-start(bf16[64,768]{1,0:T(8,128)(2,1)S(1)} %get-tuple-element.16), channel_id=1, source_target_pairs={{0,64},{1,17},{2,66},{3,19},{4,68},{5,21},{6,70},{7,23},{8,72},{9,... | collective-permute-start | bytes 294920 | tf_op jit(solution)/shard_map/ppermute | solution.py:33
  43.4 4.7 %collective-permute-start.5 = (bf16[64,768]{1,0:T(8,128)(2,1)S(1)}, bf16[64,768]{1,0:T(8,128)(2,1)S(1)}, u32[]{:S(2)}, u32[]{:S(2)}) collective-permute-start(bf16[64,768]{1,0:T(8,128)(2,1)S(1)} %get-tuple-element.16), channel_id=1, source_target_pairs={{0,96},{1,145},{2,98},{3,147},{4,100},{5,149},{6,102},{7,151},{8,1... | collective-permute-start | bytes 294920 | tf_op jit(solution)/shard_map/ppermute | solution.py:33
  48.1 8.6 %collective-permute-start.8 = (bf16[4,64,768]{2,1,0:T(8,128)(2,1)S(1)}, bf16[4,64,768]{2,1,0:T(8,128)(2,1)S(1)}, u32[]{:S(2)}, u32[]{:S(2)}) collective-permute-start(bf16[4,64,768]{2,1,0:T(8,128)(2,1)S(1)} %pad_maximum_fusion.2), channel_id=1, source_target_pairs={{0,144},{1,97},{2,146},{3,99},{4,148},{5,101},{6,150},{7,103},{8,1... | collective-permute-start | bytes 1179656 | tf_op jit(solution)/shard_map/ppermute | solution.py:33
  50.7 6.9 %collective-permute-start.6 = (bf16[4,64,768]{2,1,0:T(8,128)(2,1)S(1)}, bf16[4,64,768]{2,1,0:T(8,128)(2,1)S(1)}, u32[]{:S(2)}, u32[]{:S(2)}) collective-permute-start(bf16[4,64,768]{2,1,0:T(8,128)(2,1)S(1)} %pad_maximum_fusion.2), channel_id=1, source_target_pairs={{0,128},{1,33},{2,130},{3,35},{4,132},{5,37},{6,134},{7,39},{8,136... | collective-permute-start | bytes 1179656 | tf_op jit(solution)/shard_map/ppermute | solution.py:33
  50.7 10.8 %collective-permute-start.7 = (bf16[4,64,768]{2,1,0:T(8,128)(2,1)S(1)}, bf16[4,64,768]{2,1,0:T(8,128)(2,1)S(1)}, u32[]{:S(2)}, u32[]{:S(2)}) collective-permute-start(bf16[4,64,768]{2,1,0:T(8,128)(2,1)S(1)} %pad_maximum_fusion.2), channel_id=1, source_target_pairs={{0,16},{1,65},{2,18},{3,67},{4,20},{5,69},{6,22},{7,71},{8,24},{9,... | collective-permute-start | bytes 1179656 | tf_op jit(solution)/shard_map/ppermute | solution.py:33
  62.6 1.8 %copy-start.3 = (f32[2048]{0:T(1024)S(1)}, f32[2048]{0:T(1024)}, u32[]{:S(2)}) copy-start(f32[2048]{0:T(1024)} %param.5) | copy-start | bytes 24580
  68.2 8.3 %collective-permute-start.10 = (f32[2,2048]{1,0:T(2,128)S(1)}, f32[2,2048]{1,0:T(2,128)S(1)}, u32[]{:S(2)}, u32[]{:S(2)}) collective-permute-start(f32[2,2048]{1,0:T(2,128)S(1)} %pad_maximum_fusion.5), channel_id=1, source_target_pairs={{0,1},{1,0},{2,3},{3,2},{4,5},{5,4},{6,7},{7,6},{8,9},{9,8},{10,11... | collective-permute-start | bytes 49160 | tf_op jit(solution)/shard_map/ppermute | solution.py:29
  76.6 3.1 %copy-start.4 = (f32[2048]{0:T(1024)}, f32[2048]{0:T(1024)S(1)}, u32[]{:S(2)}) copy-start(f32[2048]{0:T(1024)S(1)} %max.22) | copy-start | bytes 24580
  76.6 3.1 %copy-start.2 = (bf16[16,32,768]{2,1,0:T(8,128)(2,1)S(1)}, bf16[16,32,768]{2,1,0:T(8,128)(2,1)}, u32[]{:S(2)}) copy-start(bf16[16,32,768]{2,1,0:T(8,128)(2,1)} %get-tuple-element.20) | copy-start | bytes 2359300

commit v3 on v2

v3 whole, which is shorter than its diff:
```python
import functools

import jax
import jax.numpy as jnp
from jax import lax
from jax.experimental import pallas as pl
from jax.experimental.pallas import tpu as pltpu
from jax.sharding import Mesh
from jax.sharding import PartitionSpec as P

AXES = ("ylo", "x", "yhi", "z", "core")
SIZES = (2, 4, 2, 8, 2)
BLK = ("ylo", "x")
CHIPS = ("ylo", "x", "yhi", "z")
MOST = 4
STEP = 512


def place(y, x, z, core):
    return (((y % 2) * 4 + x) * 2 + y // 2) * 16 + z * 2 + core


def pairs_of(move):
    return [
        (place(y, x, z, core), place(*move(y, x, z, core)))
        for y in range(4)
        for x in range(4)
        for z in range(8)
        for core in range(2)
    ]


def swap(value, y_mask, core_mask):
    return lax.ppermute(value, AXES, pairs_of(lambda y, x, z, c: (y ^ y_mask, x, z, c ^ core_mask)))


def turn(value, mask, first):
    return lax.ppermute(
        value,
        AXES,
        pairs_of(lambda y, x, z, c: (y, x ^ mask, z, c) if (c == 0) == first else (y ^ mask, x, z, c)),
    )


def turned_table(pieces, turned):
    for k, piece in enumerate(pieces):
        turned[:, k * 128 : k * 128 + 128] = piece[...].T


def tile_sims(table, turned, start):
    return jnp.dot(table[pl.ds(start, STEP), :], turned[...], preferred_element_type=jnp.float32)


def fetches(source, target, arrivals):
    step = target.shape[0] // arrivals.shape[0]
    parts = [pl.ds(k * step, step) for k in range(arrivals.shape[0])]
    return [
        pltpu.make_async_copy(source.at[at, :], target.at[at, :], arrivals.at[k])
        for k, at in enumerate(parts)
    ]


def best_kernel(own_ref, coverage_ref, c0, c1, c2, c3, partner_ref, best_ref, partner, turned, arrivals):
    rows, width = own_ref.shape
    scale = 1.0 / width**0.5
    copies = fetches(partner_ref, partner, arrivals)
    for copy in copies:
        copy.start()
    turned_table((c0, c1, c2, c3), turned)
    for t, table in enumerate((own_ref, partner)):
        for k, start in enumerate(range(0, rows, STEP)):
            if t == 1:
                copies[k].wait()
            sims = tile_sims(table, turned, start)
            top = functools.reduce(jnp.maximum, [sims[:, l : l + 128] for l in range(0, 512, 128)])
            for r in range(0, STEP, 128):
                here = pl.ds(start + r, 128)
                row = jnp.max(top[r : r + 128].T, axis=0, keepdims=True) * scale
                if t == 0:
                    row = jnp.maximum(row, coverage_ref[:, here])
                best_ref[t : t + 1, here] = row


def gain_kernel(own_ref, cover_ref, c0, c1, c2, c3, partner_ref, gain_ref, partner, turned, arrivals):
    rows, width = own_ref.shape
    scale = 1.0 / width**0.5
    copies = fetches(partner_ref, partner, arrivals)
    for copy in copies:
        copy.start()
    turned_table((c0, c1, c2, c3), turned)
    total = jnp.zeros((8, 512), jnp.float32)
    for t, table in enumerate((own_ref, partner)):
        for k, start in enumerate(range(0, rows, STEP)):
            if t == 1:
                copies[k].wait()
            sims = tile_sims(table, turned, start)
            for r in range(0, STEP, 128):
                line = cover_ref[t : t + 1, pl.ds(start + r, 128)] * width**0.5
                floor = jnp.broadcast_to(line, (128, 128)).T
                over = jnp.maximum(sims[r : r + 128] - jnp.concatenate([floor] * 4, axis=1), 0.0)
                total = total + jnp.sum(over.reshape(16, 8, 512), axis=0)
    sums = jnp.sum(total, axis=0, keepdims=True) * scale
    first = lax.axis_index("core") == 0
    x = lax.axis_index("x")
    yhi, ylo = lax.axis_index("yhi"), lax.axis_index("ylo")
    for late in range(4):
        for early in range(4):
            x_mask = jnp.where(first, early, late)
            y_mask = jnp.where(first, late, early)
            at = ((ylo ^ (y_mask & 1)) * 4 + (x ^ x_mask)) * 2 + (yhi ^ (y_mask >> 1))
            lane = late * 128 + early * 32
            gain_ref[pl.ds(at, 1), :] = sums[:, lane : lane + 32]


def on_chip(kernel, out, *operands):
    rows, width = operands[0].shape
    vmem = pl.BlockSpec(memory_space=pltpu.VMEM)
    return pl.pallas_call(
        kernel,
        out_shape=jax.ShapeDtypeStruct(out, jnp.float32),
        in_specs=[vmem] * (len(operands) - 1) + [pl.BlockSpec(memory_space=pl.ANY)],
        out_specs=vmem,
        scratch_shapes=[
            pltpu.VMEM((rows, width), jnp.bfloat16),
            pltpu.VMEM((width, 512), jnp.bfloat16),
            pltpu.SemaphoreType.DMA((rows // STEP,)),
        ],
        compiler_params=pltpu.CompilerParams(vmem_limit_bytes=24 << 20),
        cost_estimate=pl.CostEstimate(flops=4096 * 512 * 768 * 2, bytes_accessed=8 << 20, transcendentals=0),
    )(*operands)


def pick_kernel(chosen_ref, cand_ref, table_ref, q0, q1, q2, q3, chosen_rows_ref, table, arrivals):
    rows, width = table.shape
    copies = fetches(table_ref, table, arrivals)
    for copy in copies:
        copy.start()
    core, yhi = lax.axis_index("core"), lax.axis_index("yhi")
    base = lax.axis_index(AXES) * rows

    lane = lax.broadcasted_iota(jnp.int32, (8, 128), 1)
    quarter = lane >> 5
    source = ((yhi ^ (quarter >> 1)) << 6) | ((lane & 28) << 1) | ((core ^ (quarter & 1)) << 2) | (lane & 3)
    wanted = jnp.take_along_axis(jnp.broadcast_to(cand_ref[...], (8, 128)), source, axis=1) - base
    wanted = jnp.broadcast_to(wanted[:1], (128, 128)).T

    left = chosen_ref[...] - base
    left = jnp.where((left >= 0) & (left < rows), left, rows).astype(jnp.float32)
    row = lax.broadcasted_iota(jnp.int32, (8, 128), 0)
    spots = jnp.full((8, 128), -1, jnp.int32)
    for s in range(MOST):
        least = jnp.min(jnp.min(left, axis=0, keepdims=True), axis=1, keepdims=True)
        left = jnp.where(left == least, float(rows), left)
        spots = jnp.where(row == s, least.astype(jnp.int32), spots)

    targets = jnp.concatenate([wanted, spots], axis=0)
    total = jnp.zeros((136, width), jnp.float32)
    step = rows // len(copies)
    lanes = lax.broadcasted_iota(jnp.int32, (136, 128), 1)
    for k, copy in enumerate(copies):
        hits = [targets == lanes + (k * step + l) for l in range(0, step, 128)]
        pick = jnp.concatenate([jnp.where(h, 1.0, 0.0) for h in hits], axis=1).astype(jnp.bfloat16)
        copy.wait()
        total = total + jnp.dot(pick, table[pl.ds(k * step, step), :], preferred_element_type=jnp.float32)
    picked = total.astype(jnp.bfloat16)
    for k, out in enumerate((q0, q1, q2, q3)):
        out[...] = picked[k * 32 : k * 32 + 32]
    chosen_rows_ref[...] = total[128 : 128 + MOST].astype(jnp.bfloat16)


def own_picks(chosen_index, candidate_index, embeddings):
    rows, width = embeddings.shape
    vmem = pl.BlockSpec(memory_space=pltpu.VMEM)
    return pl.pallas_call(
        pick_kernel,
        out_shape=[jax.ShapeDtypeStruct((32, width), jnp.bfloat16)] * 4
        + [jax.ShapeDtypeStruct((MOST, width), jnp.bfloat16)],
        in_specs=[vmem, vmem, pl.BlockSpec(memory_space=pl.ANY)],
        out_specs=[vmem] * 5,
        scratch_shapes=[pltpu.VMEM((rows, width), jnp.bfloat16), pltpu.SemaphoreType.DMA((8,))],
        compiler_params=pltpu.CompilerParams(vmem_limit_bytes=60 << 20),
        cost_estimate=pl.CostEstimate(flops=136 * 2048 * 768 * 2, bytes_accessed=4 << 20, transcendentals=0),
    )(chosen_index.reshape(4, 128), candidate_index.reshape(1, 128), embeddings)


def local(embeddings, coverage, chosen_index, candidate_index):
    rows, width = embeddings.shape
    q0, q1, q2, q3, found = own_picks(chosen_index, candidate_index, embeddings)
    q1, q2, q3, later = lax.optimization_barrier((q1, q2, q3, embeddings))
    partner = swap(later, 0, 1)
    quarter = q0 + swap(q1, 0, 1) + swap(q2, 2, 0) + swap(q3, 2, 1)
    send = jnp.concatenate([quarter, found], axis=0)
    got = lax.all_to_all(jnp.broadcast_to(send, (8, 32 + MOST, width)), "z", 0, 0)
    quarter = jnp.sum(got[:, :32].astype(jnp.float32), axis=0).astype(jnp.bfloat16)
    near = got[:, 32:].reshape(8 * MOST, width)

    block = jnp.concatenate([quarter, near], axis=0)
    line = jnp.stack([block] + [turn(block, s, True) for s in (1, 2, 3)])
    cands, chosen = line[:, :32].reshape(128, width), line[:, 32:].reshape(128, width)
    chosen = [chosen] + [turn(chosen, s, False) for s in (1, 2, 3)]
    cands = [cands] + [turn(cands, s, False) for s in (1, 2, 3)]

    best = on_chip(best_kernel, (2, rows), embeddings, coverage.reshape(1, rows), *chosen, partner)
    cover = jnp.maximum(best, swap(best, 0, 1)[::-1])
    part = on_chip(gain_kernel, (16, 32), embeddings, cover, *cands, partner).reshape(128, 4)
    parts = lax.all_to_all(part, CHIPS, 0, 0)
    return cover[0], jnp.sum(parts, axis=0)


def solution(mesh):
    torus = Mesh(mesh.devices.reshape(SIZES), AXES)
    return jax.shard_map(
        local,
        mesh=torus,
        in_specs=(P(AXES, None), P(AXES), P(), P(BLK)),
        out_specs=(P(AXES), P(AXES)),
        check_vma=False,
    )
```

time: 101 us -> 96.5 us (0.955)
  blocking collectives: 40.1 us -> 23.8 us
  Pallas kernels: 0 us -> 15.2 us
  matrix products: 15.1 us -> 0 us
  starting transfers between devices: 22.1 us -> 28.9 us
  waiting for transfers between devices: 16 us -> 21.6 us
  other arithmetic: 4.97 us -> 3.32 us
  local copies, waits for them, and re-layouts: 1.48 us -> 2.59 us
    all_to_all x1 -> x0, blocking collectives: 16.1 us -> none  [local(): parts = lax.all_to_all(part, CHIPS, 0, 0)]
    pallas_call x0 -> x3, Pallas kernels: none -> 15.2 us  [the longest x2 11.1 us: on_chip(): pl.pallas_call(kernel, out_shape=jax.ShapeDtypeStruct(out, jnp.float32),...]
    dot_general x5 -> x0, matrix products: 15.1 us -> none  [the longest x2 6.96 us: gain(): sims = jnp.dot(table, cands.T, preferred_element_type=jnp.float32) * scale]
    all_to_all x0 -> x1, waiting for transfers between devices: none -> 9.97 us  [local(): parts = lax.all_to_all(part, CHIPS, 0, 0)]
    all_to_all x0 -> x1, starting transfers between devices: none -> 6.11 us  [local(): parts = lax.all_to_all(part, CHIPS, 0, 0)]
    ppermute x6 -> x9, waiting for transfers between devices: 12.2 us -> 7.11 us  [turn(): lax.ppermute(value, AXES, pairs_of(lambda y, x, z, c: (y, x ^ mask, z, c)...]
    ppermute x6 -> x9, starting transfers between devices: 7.89 us -> 10.9 us  [turn(): lax.ppermute(value, AXES, pairs_of(lambda y, x, z, c: (y, x ^ mask, z, c)...]
    ppermute x5, starting transfers between devices: 14.2 us -> 11.9 us  [swap(): lax.ppermute(value, AXES, pairs_of(lambda y, x, z, c: (y ^ y_mask, x, z,...]
  transfers between devices with their start and end apart: 11 -> 15, of which waited for: 8 -> 9; matrix products, arithmetic and copies ran while one was open for 4% -> 4% of each run, Pallas kernels for 0% -> 5%
where the time goes in v3:
time: 96.5 us; the launch traced here: 96.2 us
  starting transfers between devices  28.9 us (30%)
  blocking collectives  23.8 us (25%)
  waiting for transfers between devices  21.6 us (22%)
  Pallas kernels  15.2 us (16%)
  other arithmetic  3.32 us (3%)
  local copies, waits for them, and re-layouts  2.59 us (3%)
    all_to_all x1, blocking collectives, local(): lax.all_to_all(jnp.broadcast_to(send, (8, 32 + MOST, width)), 'z', 0, 0)  23.8 us
    ppermute x5, starting transfers between devices, swap(): lax.ppermute(value, AXES, pairs_of(lambda y, x, z, c: (y ^ y_mask, x, z,...  11.9 us
    pallas_call x2, Pallas kernels, on_chip(): pl.pallas_call(kernel, out_shape=jax.ShapeDtypeStruct(out, jnp.float32),...  11.1 us
    ppermute x9, starting transfers between devices, turn(): lax.ppermute(value, AXES, pairs_of(lambda y, x, z, c: (y, x ^ mask, z, c)...  10.9 us
    all_to_all x1, waiting for transfers between devices, local(): parts = lax.all_to_all(part, CHIPS, 0, 0)  9.97 us
    ppermute x9, waiting for transfers between devices, turn(): lax.ppermute(value, AXES, pairs_of(lambda y, x, z, c: (y, x ^ mask, z, c)...  7.11 us
    all_to_all x1, starting transfers between devices, local(): parts = lax.all_to_all(part, CHIPS, 0, 0)  6.11 us
    ppermute x5, waiting for transfers between devices, swap(): lax.ppermute(value, AXES, pairs_of(lambda y, x, z, c: (y ^ y_mask, x, z,...  4.52 us
  transfers between devices with their start and end apart: 15, of which 9 were waited for; matrix products, arithmetic and copies ran while one was open for 4% of the time, Pallas kernels for 5%

profile of v3, /device:TPU:1, one launch (start us, length us, event | category | flops | bytes accessed | tf_op | source)
XLA Modules:
  0.0 96.2 jit_solution(411818414685705617)
XLA Ops:
  0.7 4.0 %shard_map.59 = (bf16[32,768]{1,0:T(8,128)(2,1)}, bf16[32,768]{1,0:T(8,128)(2,1)}, bf16[32,768]{1,0:T(8,128)(2,1)}, bf16[32,768]{1,0:T(8,128)(2,1)}, bf16[4,768]{1,0:T(4,128)(2,1)}) custom-call(s32[4,128]{1,0:T(4,128)} %bitcast.25, s32[1,128]{1,0:T(1,128)} %bitcast.26, bf16[2048,768]{1,0:T(8,128)(2,1)} %own_ref.3), custom_call_target="tpu_custom_call" | custom-call | flops 427819008 | bytes 4194304 | tf_op jit(solution)/shard_map/pallas_call | solution.py:174
  4.7 3.3 %collective-permute-start.9 = (bf16[2048,768]{1,0:T(8,128)(2,1)S(1)}, bf16[2048,768]{1,0:T(8,128)(2,1)}, u32[]{:S(2)}, u32[]{:S(2)}) collective-permute-start(bf16[2048,768]{1,0:T(8,128)(2,1)S(1)} %copy-done), channel_id=1, source_target_pairs={{0,1},{1,0},{2,3},{3,2},{4,5},{5,4},{6,7},{7,6},{8,9},{9,8},{10,11... | collective-permute-start | bytes 9437192 | tf_op jit(solution)/shard_map/ppermute | solution.py:34
  8.1 1.2 %collective-permute-start.1 = (bf16[32,768]{1,0:T(8,128)(2,1)}, bf16[32,768]{1,0:T(8,128)(2,1)S(1)}, u32[]{:S(2)}, u32[]{:S(2)}) collective-permute-start(bf16[32,768]{1,0:T(8,128)(2,1)} %get-tuple-element.16), channel_id=1, source_target_pairs={{0,16},{1,17},{2,18},{3,19},{4,20},{5,21},{6,22},{7,23},{8,24},{9,... | collective-permute-start | bytes 147464 | tf_op jit(solution)/shard_map/ppermute | solution.py:34
  9.3 2.4 %collective-permute-start.2 = (bf16[32,768]{1,0:T(8,128)(2,1)}, bf16[32,768]{1,0:T(8,128)(2,1)S(1)}, u32[]{:S(2)}, u32[]{:S(2)}) collective-permute-start(bf16[32,768]{1,0:T(8,128)(2,1)} %get-tuple-element.17), channel_id=1, source_target_pairs={{0,17},{1,16},{2,19},{3,18},{4,21},{5,20},{6,23},{7,22},{8,25},{9,... | collective-permute-start | bytes 147464 | tf_op jit(solution)/shard_map/ppermute | solution.py:34
  11.7 1.8 %collective-permute-done = bf16[32,768]{1,0:T(8,128)(2,1)S(1)} collective-permute-done((bf16[32,768]{1,0:T(8,128)(2,1)}, bf16[32,768]{1,0:T(8,128)(2,1)S(1)}, u32[]{:S(2)}, u32[]{:S(2)}) %collective-permute-start) | collective-permute-done | bytes 49184 | tf_op jit(solution)/shard_map/ppermute | solution.py:34
  13.5 1.9 %collective-permute-done.2 = bf16[32,768]{1,0:T(8,128)(2,1)S(1)} collective-permute-done((bf16[32,768]{1,0:T(8,128)(2,1)}, bf16[32,768]{1,0:T(8,128)(2,1)S(1)}, u32[]{:S(2)}, u32[]{:S(2)}) %collective-permute-start.2) | collective-permute-done | bytes 49184 | tf_op jit(solution)/shard_map/ppermute | solution.py:34
  16.9 23.8 %all_to_all.14 = bf16[8,36,768]{2,1,0:T(8,128)(2,1)S(1)} all-to-all(bf16[8,36,768]{2,1,0:T(8,128)(2,1)S(1)} %broadcast_in_dim.3), channel_id=1, replica_groups=mesh['ylo'=2,'x'=4,'yhi'=2,'z'=8,'core'=2] {'z'}, dimensions={0} | all-to-all | bytes 884736 | tf_op jit(solution)/shard_map/all_to_all | solution.py:193
  41.6 1.1 %slice_reduce_fusion = bf16[32,768]{1,0:T(8,128)(2,1)S(1)} fusion(bf16[8,36,768]{2,1,0:T(8,128)(2,1)} %copy-done.2), kind=kLoop, calls=%fused_computation | loop fusion | flops 172032 | bytes 442368 | tf_op jit(solution)/shard_map/reduce_sum | solution.py:194
  43.2 1.6 %collective-permute-start.4 = (bf16[64,768]{1,0:T(8,128)(2,1)S(1)}, bf16[64,768]{1,0:T(8,128)(2,1)S(1)}, u32[]{:S(2)}, u32[]{:S(2)}) collective-permute-start(bf16[64,768]{1,0:T(8,128)(2,1)S(1)} %get-tuple-element.23), channel_id=1, source_target_pairs={{0,64},{1,17},{2,66},{3,19},{4,68},{5,21},{6,70},{7,23},{8,72},{9,... | collective-permute-start | bytes 294920 | tf_op jit(solution)/shard_map/ppermute | solution.py:38
  44.7 1.9 %collective-permute-start.5 = (bf16[64,768]{1,0:T(8,128)(2,1)S(1)}, bf16[64,768]{1,0:T(8,128)(2,1)S(1)}, u32[]{:S(2)}, u32[]{:S(2)}) collective-permute-start(bf16[64,768]{1,0:T(8,128)(2,1)S(1)} %get-tuple-element.23), channel_id=1, source_target_pairs={{0,96},{1,145},{2,98},{3,147},{4,100},{5,149},{6,102},{7,151},{8,1... | collective-permute-start | bytes 294920 | tf_op jit(solution)/shard_map/ppermute | solution.py:38
  46.6 1.5 %collective-permute-done.4 = bf16[64,768]{1,0:T(8,128)(2,1)S(1)} collective-permute-done((bf16[64,768]{1,0:T(8,128)(2,1)S(1)}, bf16[64,768]{1,0:T(8,128)(2,1)S(1)}, u32[]{:S(2)}, u32[]{:S(2)}) %collective-permute-start.4) | collective-permute-done | bytes 98336 | tf_op jit(solution)/shard_map/ppermute | solution.py:38
  48.1 1.3 %collective-permute-done.5 = bf16[64,768]{1,0:T(8,128)(2,1)S(1)} collective-permute-done((bf16[64,768]{1,0:T(8,128)(2,1)S(1)}, bf16[64,768]{1,0:T(8,128)(2,1)S(1)}, u32[]{:S(2)}, u32[]{:S(2)}) %collective-permute-start.5) | collective-permute-done | bytes 98336 | tf_op jit(solution)/shard_map/ppermute | solution.py:38
  49.5 1.3 %collective-permute-start.6 = (bf16[128,768]{1,0:T(8,128)(2,1)S(1)}, bf16[128,768]{1,0:T(8,128)(2,1)S(1)}, u32[]{:S(2)}, u32[]{:S(2)}) collective-permute-start(bf16[128,768]{1,0:T(8,128)(2,1)S(1)} %bitcast.16), channel_id=1, source_target_pairs={{0,128},{1,33},{2,130},{3,35},{4,132},{5,37},{6,134},{7,39},{8,136... | collective-permute-start | bytes 589832 | tf_op jit(solution)/shard_map/ppermute | solution.py:38
  50.8 2.5 %collective-permute-start.7 = (bf16[128,768]{1,0:T(8,128)(2,1)S(1)}, bf16[128,768]{1,0:T(8,128)(2,1)S(1)}, u32[]{:S(2)}, u32[]{:S(2)}) collective-permute-start(bf16[128,768]{1,0:T(8,128)(2,1)S(1)} %bitcast.17), channel_id=1, source_target_pairs={{0,16},{1,65},{2,18},{3,67},{4,20},{5,69},{6,22},{7,71},{8,24},{9,... | collective-permute-start | bytes 589832 | tf_op jit(solution)/shard_map/ppermute | solution.py:38
  53.4 0.9 collective-permute-done.6.c1
  54.3 2.8 %collective-permute-start.12 = (bf16[128,768]{1,0:T(8,128)(2,1)S(1)}, bf16[128,768]{1,0:T(8,128)(2,1)}, u32[]{:S(2)}, u32[]{:S(2)}) collective-permute-start(bf16[128,768]{1,0:T(8,128)(2,1)S(1)} %bitcast.13), channel_id=1, source_target_pairs={{0,16},{1,65},{2,18},{3,67},{4,20},{5,69},{6,22},{7,71},{8,24},{9,... | collective-permute-start | bytes 589832 | tf_op jit(solution)/shard_map/ppermute | solution.py:38
  57.1 1.4 %collective-permute-done.7.c2 = bf16[128,768]{1,0:T(8,128)(2,1)S(1)} collective-permute-done((bf16[128,768]{1,0:T(8,128)(2,1)S(1)}, bf16[128,768]{1,0:T(8,128)(2,1)S(1)}, u32[]{:S(2)}, u32[]{:S(2)}) %collective-permute-start.7) | collective-permute-done | bytes 196640 | tf_op jit(solution)/shard_map/ppermute | solution.py:38
  58.7 2.1 %collective-permute-done.8.c3 = bf16[128,768]{1,0:T(8,128)(2,1)S(1)} collective-permute-done((bf16[128,768]{1,0:T(8,128)(2,1)S(1)}, bf16[128,768]{1,0:T(8,128)(2,1)S(1)}, u32[]{:S(2)}, u32[]{:S(2)}) %collective-permute-start.8) | collective-permute-done | bytes 196640 | tf_op jit(solution)/shard_map/ppermute | solution.py:38
  60.8 4.7 %shard_map.60 = f32[2,2048]{1,0:T(2,128)S(1)} custom-call(bf16[2048,768]{1,0:T(8,128)(2,1)S(1)} %copy-done, f32[1,2048]{1,0:T(1,128)S(1)} %bitcast.20, bf16[128,768]{1,0:T(8,128)(2,1)S(1)} %bitcast.19, bf16[128,768]{1,0:T(8,128)(2,1)S(1)} %collective-permute-done.6.c1, bf16[128,768]{1,0:T(8,128)(2,1)S(1)} %collective-permute-done.7.c2, ...), custom_call_target="tpu_custom_call" | custom-call | flops 3221225472 | bytes 8388608 | tf_op jit(solution)/shard_map/pallas_call | solution.py:118
  65.5 4.9 %collective-permute-start.10 = (f32[2,2048]{1,0:T(2,128)S(1)}, f32[2,2048]{1,0:T(2,128)S(1)}, u32[]{:S(2)}, u32[]{:S(2)}) collective-permute-start(f32[2,2048]{1,0:T(2,128)S(1)} %shard_map.60), channel_id=1, source_target_pairs={{0,1},{1,0},{2,3},{3,2},{4,5},{5,4},{6,7},{7,6},{8,9},{9,8},{10,11... | collective-permute-start | bytes 49160 | tf_op jit(solution)/shard_map/ppermute | solution.py:34
  70.4 0.8 collective-permute-done.10
  71.7 6.5 %shard_map.61 = f32[16,32]{1,0:T(8,128)S(1)} custom-call(bf16[2048,768]{1,0:T(8,128)(2,1)S(1)} %copy-done, f32[2,2048]{1,0:T(2,128)S(1)} %max.3.cover_ref, bf16[128,768]{1,0:T(8,128)(2,1)S(1)} %bitcast.15, bf16[128,768]{1,0:T(8,128)(2,1)} %collective-permute-done.11.c1, bf16[128,768]{1,0:T(8,128)(2,1)} %collective-permute-done.12.c2, ...), custom_call_target="tpu_custom_call" | custom-call | flops 3221225472 | bytes 8388608 | tf_op jit(solution)/shard_map/pallas_call | solution.py:118
  78.9 6.1 %all-to-all-start.1 = ((f32[128,1,4]{2,1,0:T(1,128)}), f32[128,1,4]{2,1,0:T(1,128)S(1)}, u32[]{:S(2)}, u32[]{:S(2)}) async-start(f32[128,1,4]{2,1,0:T(1,128)} %bitcast.10), calls=%async_computation.1 | async-start | bytes 131072 | tf_op jit(solution)/shard_map/all_to_all | solution.py:206
  85.6 10.0 %all-to-all-done.1 = f32[128,1,4]{2,1,0:T(1,128)S(1)} async-done(((f32[128,1,4]{2,1,0:T(1,128)}), f32[128,1,4]{2,1,0:T(1,128)S(1)}, u32[]{:S(2)}, u32[]{:S(2)}) %all-to-all-start.1) | async-done | bytes 2080 | tf_op jit(solution)/shard_map/all_to_all | solution.py:206
  (30 shorter events, 5.9 us)
Async XLA Ops:
  0.6 4.1 %copy-start = (bf16[2048,768]{1,0:T(8,128)(2,1)S(1)}, bf16[2048,768]{1,0:T(8,128)(2,1)}, u32[]{:S(2)}) copy-start(bf16[2048,768]{1,0:T(8,128)(2,1)} %own_ref.3) | copy-start | bytes 9437188
  0.6 60.2 %copy-start.1 = (f32[2048]{0:T(1024)S(1)}, f32[2048]{0:T(1024)}, u32[]{:S(2)}) copy-start(f32[2048]{0:T(1024)} %param.5) | copy-start | bytes 24580
  4.7 56.1 %collective-permute-start.9 = (bf16[2048,768]{1,0:T(8,128)(2,1)S(1)}, bf16[2048,768]{1,0:T(8,128)(2,1)}, u32[]{:S(2)}, u32[]{:S(2)}) collective-permute-start(bf16[2048,768]{1,0:T(8,128)(2,1)S(1)} %copy-done), channel_id=1, source_target_pairs={{0,1},{1,0},{2,3},{3,2},{4,5},{5,4},{6,7},{7,6},{8,9},{9,8},{10,11... | collective-permute-start | bytes 9437192 | tf_op jit(solution)/shard_map/ppermute | solution.py:34
  8.0 5.4 %collective-permute-start = (bf16[32,768]{1,0:T(8,128)(2,1)}, bf16[32,768]{1,0:T(8,128)(2,1)S(1)}, u32[]{:S(2)}, u32[]{:S(2)}) collective-permute-start(bf16[32,768]{1,0:T(8,128)(2,1)} %get-tuple-element.15), channel_id=1, source_target_pairs={{0,1},{1,0},{2,3},{3,2},{4,5},{5,4},{6,7},{7,6},{8,9},{9,8},{10,11... | collective-permute-start | bytes 147464 | tf_op jit(solution)/shard_map/ppermute | solution.py:34
  8.1 5.3 %collective-permute-start.1 = (bf16[32,768]{1,0:T(8,128)(2,1)}, bf16[32,768]{1,0:T(8,128)(2,1)S(1)}, u32[]{:S(2)}, u32[]{:S(2)}) collective-permute-start(bf16[32,768]{1,0:T(8,128)(2,1)} %get-tuple-element.16), channel_id=1, source_target_pairs={{0,16},{1,17},{2,18},{3,19},{4,20},{5,21},{6,22},{7,23},{8,24},{9,... | collective-permute-start | bytes 147464 | tf_op jit(solution)/shard_map/ppermute | solution.py:34
  9.3 6.0 %collective-permute-start.2 = (bf16[32,768]{1,0:T(8,128)(2,1)}, bf16[32,768]{1,0:T(8,128)(2,1)S(1)}, u32[]{:S(2)}, u32[]{:S(2)}) collective-permute-start(bf16[32,768]{1,0:T(8,128)(2,1)} %get-tuple-element.17), channel_id=1, source_target_pairs={{0,17},{1,16},{2,19},{3,18},{4,21},{5,20},{6,23},{7,22},{8,25},{9,... | collective-permute-start | bytes 147464 | tf_op jit(solution)/shard_map/ppermute | solution.py:34
  40.8 0.8 copy-start.2
  42.7 3.9 %collective-permute-start.3 = (bf16[64,768]{1,0:T(8,128)(2,1)S(1)}, bf16[64,768]{1,0:T(8,128)(2,1)S(1)}, u32[]{:S(2)}, u32[]{:S(2)}) collective-permute-start(bf16[64,768]{1,0:T(8,128)(2,1)S(1)} %get-tuple-element.23), channel_id=1, source_target_pairs={{0,32},{1,129},{2,34},{3,131},{4,36},{5,133},{6,38},{7,135},{8,40}... | collective-permute-start | bytes 294920 | tf_op jit(solution)/shard_map/ppermute | solution.py:38
  43.2 5.0 %collective-permute-start.4 = (bf16[64,768]{1,0:T(8,128)(2,1)S(1)}, bf16[64,768]{1,0:T(8,128)(2,1)S(1)}, u32[]{:S(2)}, u32[]{:S(2)}) collective-permute-start(bf16[64,768]{1,0:T(8,128)(2,1)S(1)} %get-tuple-element.23), channel_id=1, source_target_pairs={{0,64},{1,17},{2,66},{3,19},{4,68},{5,21},{6,70},{7,23},{8,72},{9,... | collective-permute-start | bytes 294920 | tf_op jit(solution)/shard_map/ppermute | solution.py:38
  44.7 4.7 %collective-permute-start.5 = (bf16[64,768]{1,0:T(8,128)(2,1)S(1)}, bf16[64,768]{1,0:T(8,128)(2,1)S(1)}, u32[]{:S(2)}, u32[]{:S(2)}) collective-permute-start(bf16[64,768]{1,0:T(8,128)(2,1)S(1)} %get-tuple-element.23), channel_id=1, source_target_pairs={{0,96},{1,145},{2,98},{3,147},{4,100},{5,149},{6,102},{7,151},{8,1... | collective-permute-start | bytes 294920 | tf_op jit(solution)/shard_map/ppermute | solution.py:38
  49.5 4.8 %collective-permute-start.6 = (bf16[128,768]{1,0:T(8,128)(2,1)S(1)}, bf16[128,768]{1,0:T(8,128)(2,1)S(1)}, u32[]{:S(2)}, u32[]{:S(2)}) collective-permute-start(bf16[128,768]{1,0:T(8,128)(2,1)S(1)} %bitcast.16), channel_id=1, source_target_pairs={{0,128},{1,33},{2,130},{3,35},{4,132},{5,37},{6,134},{7,39},{8,136... | collective-permute-start | bytes 589832 | tf_op jit(solution)/shard_map/ppermute | solution.py:38
  50.8 7.7 %collective-permute-start.7 = (bf16[128,768]{1,0:T(8,128)(2,1)S(1)}, bf16[128,768]{1,0:T(8,128)(2,1)S(1)}, u32[]{:S(2)}, u32[]{:S(2)}) collective-permute-start(bf16[128,768]{1,0:T(8,128)(2,1)S(1)} %bitcast.17), channel_id=1, source_target_pairs={{0,16},{1,65},{2,18},{3,67},{4,20},{5,69},{6,22},{7,71},{8,24},{9,... | collective-permute-start | bytes 589832 | tf_op jit(solution)/shard_map/ppermute | solution.py:38
  53.2 7.6 %collective-permute-start.8 = (bf16[128,768]{1,0:T(8,128)(2,1)S(1)}, bf16[128,768]{1,0:T(8,128)(2,1)S(1)}, u32[]{:S(2)}, u32[]{:S(2)}) collective-permute-start(bf16[128,768]{1,0:T(8,128)(2,1)S(1)} %bitcast.18), channel_id=1, source_target_pairs={{0,144},{1,97},{2,146},{3,99},{4,148},{5,101},{6,150},{7,103},{8,1... | collective-permute-start | bytes 589832 | tf_op jit(solution)/shard_map/ppermute | solution.py:38
  53.4 18.2 %collective-permute-start.11 = (bf16[128,768]{1,0:T(8,128)(2,1)S(1)}, bf16[128,768]{1,0:T(8,128)(2,1)}, u32[]{:S(2)}, u32[]{:S(2)}) collective-permute-start(bf16[128,768]{1,0:T(8,128)(2,1)S(1)} %bitcast.12), channel_id=1, source_target_pairs={{0,128},{1,33},{2,130},{3,35},{4,132},{5,37},{6,134},{7,39},{8,136... | collective-permute-start | bytes 589832 | tf_op jit(solution)/shard_map/ppermute | solution.py:38
  54.3 17.3 %collective-permute-start.12 = (bf16[128,768]{1,0:T(8,128)(2,1)S(1)}, bf16[128,768]{1,0:T(8,128)(2,1)}, u32[]{:S(2)}, u32[]{:S(2)}) collective-permute-start(bf16[128,768]{1,0:T(8,128)(2,1)S(1)} %bitcast.13), channel_id=1, source_target_pairs={{0,16},{1,65},{2,18},{3,67},{4,20},{5,69},{6,22},{7,71},{8,24},{9,... | collective-permute-start | bytes 589832 | tf_op jit(solution)/shard_map/ppermute | solution.py:38
  58.5 13.2 %collective-permute-start.13 = (bf16[128,768]{1,0:T(8,128)(2,1)S(1)}, bf16[128,768]{1,0:T(8,128)(2,1)}, u32[]{:S(2)}, u32[]{:S(2)}) collective-permute-start(bf16[128,768]{1,0:T(8,128)(2,1)S(1)} %bitcast.14), channel_id=1, source_target_pairs={{0,144},{1,97},{2,146},{3,99},{4,148},{5,101},{6,150},{7,103},{8,1... | collective-permute-start | bytes 589832 | tf_op jit(solution)/shard_map/ppermute | solution.py:38
  65.5 5.7 %collective-permute-start.10 = (f32[2,2048]{1,0:T(2,128)S(1)}, f32[2,2048]{1,0:T(2,128)S(1)}, u32[]{:S(2)}, u32[]{:S(2)}) collective-permute-start(f32[2,2048]{1,0:T(2,128)S(1)} %shard_map.60), channel_id=1, source_target_pairs={{0,1},{1,0},{2,3},{3,2},{4,5},{5,4},{6,7},{7,6},{8,9},{9,8},{10,11... | collective-permute-start | bytes 49160 | tf_op jit(solution)/shard_map/ppermute | solution.py:34
  78.9 16.7 %all-to-all-start.1 = ((f32[128,1,4]{2,1,0:T(1,128)}), f32[128,1,4]{2,1,0:T(1,128)S(1)}, u32[]{:S(2)}, u32[]{:S(2)}) async-start(f32[128,1,4]{2,1,0:T(1,128)} %bitcast.10), calls=%async_computation.1 | async-start | bytes 131072 | tf_op jit(solution)/shard_map/all_to_all | solution.py:206

commit v4 on v3

--- a/solution.py
+++ b/solution.py
@@ -13,7 +13,7 @@
 BLK = ("ylo", "x")
 CHIPS = ("ylo", "x", "yhi", "z")
 MOST = 4
-STEP = 512
+STEP = 256
 
 
 def place(y, x, z, core):
@@ -49,6 +49,22 @@
 
 def tile_sims(table, turned, start):
     return jnp.dot(table[pl.ds(start, STEP), :], turned[...], preferred_element_type=jnp.float32)
+
+
+def turn_kernel(c0, c1, c2, c3, turned):
+    turned_table((c0, c1, c2, c3), turned)
+
+
+def turned_pieces(pieces):
+    vmem = pl.BlockSpec(memory_space=pltpu.VMEM)
+    return pl.pallas_call(
+        turn_kernel,
+        out_shape=jax.ShapeDtypeStruct((pieces[0].shape[1], 512), jnp.bfloat16),
+        in_specs=[vmem] * 4,
+        out_specs=vmem,
+        compiler_params=pltpu.CompilerParams(vmem_limit_bytes=8 << 20),
+        cost_estimate=pl.CostEstimate(flops=1 << 20, bytes_accessed=2 << 20, transcendentals=0),
+    )(*pieces)
 
 
 def fetches(source, target, arrivals):
@@ -81,18 +97,16 @@
                 best_ref[t : t + 1, here] = row
 
 
-def gain_kernel(own_ref, cover_ref, c0, c1, c2, c3, partner_ref, gain_ref, partner, turned, arrivals):
-    rows, width = own_ref.shape
+def gain_kernel(cover_ref, turned, own_ref, partner_ref, gain_ref, own, partner, own_arrivals, arrivals):
+    rows, width = own.shape
     scale = 1.0 / width**0.5
-    copies = fetches(partner_ref, partner, arrivals)
-    for copy in copies:
+    copies = [fetches(own_ref, own, own_arrivals), fetches(partner_ref, partner, arrivals)]
+    for copy in copies[0] + copies[1]:
         copy.start()
-    turned_table((c0, c1, c2, c3), turned)
     total = jnp.zeros((8, 512), jnp.float32)
-    for t, table in enumerate((own_ref, partner)):
+    for t, table in enumerate((own, partner)):
         for k, start in enumerate(range(0, rows, STEP)):
-            if t == 1:
-                copies[k].wait()
+            copies[t][k].wait()
             sims = tile_sims(table, turned, start)
             for r in range(0, STEP, 128):
                 line = cover_ref[t : t + 1, pl.ds(start + r, 128)] * width**0.5
@@ -109,28 +123,26 @@
             y_mask = jnp.where(first, late, early)
             at = ((ylo ^ (y_mask & 1)) * 4 + (x ^ x_mask)) * 2 + (yhi ^ (y_mask >> 1))
             lane = late * 128 + early * 32
-            gain_ref[pl.ds(at, 1), :] = sums[:, lane : lane + 32]
-
-
-def on_chip(kernel, out, *operands):
-    rows, width = operands[0].shape
+            gain_ref[pl.ds(at * 8, 8), :] = jnp.broadcast_to(sums[:, lane : lane + 32], (8, 32))
+
+
+def on_chip(kernel, out, fetched, scratch, memory, *operands):
+    rows, width = operands[-1].shape
     vmem = pl.BlockSpec(memory_space=pltpu.VMEM)
     return pl.pallas_call(
         kernel,
         out_shape=jax.ShapeDtypeStruct(out, jnp.float32),
-        in_specs=[vmem] * (len(operands) - 1) + [pl.BlockSpec(memory_space=pl.ANY)],
+        in_specs=[vmem] * (len(operands) - fetched) + [pl.BlockSpec(memory_space=pl.ANY)] * fetched,
         out_specs=vmem,
-        scratch_shapes=[
-            pltpu.VMEM((rows, width), jnp.bfloat16),
-            pltpu.VMEM((width, 512), jnp.bfloat16),
-            pltpu.SemaphoreType.DMA((rows // STEP,)),
-        ],
-        compiler_params=pltpu.CompilerParams(vmem_limit_bytes=24 << 20),
+        scratch_shapes=[pltpu.VMEM((rows, width), jnp.bfloat16)] * fetched
+        + scratch
+        + [pltpu.SemaphoreType.DMA((rows // STEP,))] * fetched,
+        compiler_params=pltpu.CompilerParams(vmem_limit_bytes=memory << 20),
         cost_estimate=pl.CostEstimate(flops=4096 * 512 * 768 * 2, bytes_accessed=8 << 20, transcendentals=0),
     )(*operands)
 
 
-def pick_kernel(chosen_ref, cand_ref, table_ref, q0, q1, q2, q3, chosen_rows_ref, table, arrivals):
+def pick_kernel(chosen_ref, cand_ref, table_ref, kept_ref, given_ref, found_ref, table, arrivals):
     rows, width = table.shape
     copies = fetches(table_ref, table, arrivals)
     for copy in copies:
@@ -140,7 +152,7 @@
 
     lane = lax.broadcasted_iota(jnp.int32, (8, 128), 1)
     quarter = lane >> 5
-    source = ((yhi ^ (quarter >> 1)) << 6) | ((lane & 28) << 1) | ((core ^ (quarter & 1)) << 2) | (lane & 3)
+    source = ((yhi ^ (quarter & 1)) << 6) | ((lane & 28) << 1) | ((core ^ (quarter >> 1)) << 2) | (lane & 3)
     wanted = jnp.take_along_axis(jnp.broadcast_to(cand_ref[...], (8, 128)), source, axis=1) - base
     wanted = jnp.broadcast_to(wanted[:1], (128, 128)).T
 
@@ -154,18 +166,38 @@
         spots = jnp.where(row == s, least.astype(jnp.int32), spots)
 
     targets = jnp.concatenate([wanted, spots], axis=0)
-    total = jnp.zeros((136, width), jnp.float32)
     step = rows // len(copies)
     lanes = lax.broadcasted_iota(jnp.int32, (136, 128), 1)
+    total = jnp.zeros((136, width), jnp.float32)
     for k, copy in enumerate(copies):
         hits = [targets == lanes + (k * step + l) for l in range(0, step, 128)]
-        pick = jnp.concatenate([jnp.where(h, 1.0, 0.0) for h in hits], axis=1).astype(jnp.bfloat16)
+        pick = jnp.concatenate([jnp.where(h, 1.0, 0.0).astype(jnp.bfloat16) for h in hits], axis=1)
         copy.wait()
         total = total + jnp.dot(pick, table[pl.ds(k * step, step), :], preferred_element_type=jnp.float32)
-    picked = total.astype(jnp.bfloat16)
-    for k, out in enumerate((q0, q1, q2, q3)):
-        out[...] = picked[k * 32 : k * 32 + 32]
-    chosen_rows_ref[...] = total[128 : 128 + MOST].astype(jnp.bfloat16)
+    kept_ref[...] = total[:64].astype(jnp.bfloat16)
+    given_ref[...] = total[64:128].astype(jnp.bfloat16)
+    found_ref[...] = total[128 : 128 + MOST].astype(jnp.bfloat16)
+
+
+def settle_kernel(got_ref, block_ref):
+    total = got_ref[0, :32, :].astype(jnp.float32)
+    for z in range(1, 8):
+        total = total + got_ref[z, :32, :].astype(jnp.float32)
+    block_ref[:32, :] = total.astype(jnp.bfloat16)
+    found = [got_ref[z, 32:, :].astype(jnp.float32) for z in range(8)]
+    block_ref[32:, :] = jnp.concatenate(found, axis=0).astype(jnp.bfloat16)
+
+
+def settled(got):
+    vmem = pl.BlockSpec(memory_space=pltpu.VMEM)
+    return pl.pallas_call(
+        settle_kernel,
+        out_shape=jax.ShapeDtypeStruct((64, got.shape[2]), jnp.bfloat16),
+        in_specs=[vmem],
+        out_specs=vmem,
+        compiler_params=pltpu.CompilerParams(vmem_limit_bytes=8 << 20),
+        cost_estimate=pl.CostEstimate(flops=1 << 20, bytes_accessed=1 << 20, transcendentals=0),
+    )(got)
 
 
 def own_picks(chosen_index, candidate_index, embeddings):
@@ -173,11 +205,11 @@
     vmem = pl.BlockSpec(memory_space=pltpu.VMEM)
     return pl.pallas_call(
         pick_kernel,
-        out_shape=[jax.ShapeDtypeStruct((32, width), jnp.bfloat16)] * 4
+        out_shape=[jax.ShapeDtypeStruct((64, width), jnp.bfloat16)] * 2
         + [jax.ShapeDtypeStruct((MOST, width), jnp.bfloat16)],
         in_specs=[vmem, vmem, pl.BlockSpec(memory_space=pl.ANY)],
-        out_specs=[vmem] * 5,
-        scratch_shapes=[pltpu.VMEM((rows, width), jnp.bfloat16), pltpu.SemaphoreType.DMA((8,))],
+        out_specs=[vmem] * 3,
+        scratch_shapes=[pltpu.VMEM((rows, width), jnp.bfloat16), pltpu.SemaphoreType.DMA((4,))],
         compiler_params=pltpu.CompilerParams(vmem_limit_bytes=60 << 20),
         cost_estimate=pl.CostEstimate(flops=136 * 2048 * 768 * 2, bytes_accessed=4 << 20, transcendentals=0),
     )(chosen_index.reshape(4, 128), candidate_index.reshape(1, 128), embeddings)
@@ -185,26 +217,26 @@
 
 def local(embeddings, coverage, chosen_index, candidate_index):
     rows, width = embeddings.shape
-    q0, q1, q2, q3, found = own_picks(chosen_index, candidate_index, embeddings)
-    q1, q2, q3, later = lax.optimization_barrier((q1, q2, q3, embeddings))
+    kept, given, found = own_picks(chosen_index, candidate_index, embeddings)
+    half = kept + swap(given, 0, 1)
+    half, later = lax.optimization_barrier((half, embeddings))
     partner = swap(later, 0, 1)
-    quarter = q0 + swap(q1, 0, 1) + swap(q2, 2, 0) + swap(q3, 2, 1)
+    quarter = half[:32] + swap(half[32:], 2, 0)
     send = jnp.concatenate([quarter, found], axis=0)
     got = lax.all_to_all(jnp.broadcast_to(send, (8, 32 + MOST, width)), "z", 0, 0)
-    quarter = jnp.sum(got[:, :32].astype(jnp.float32), axis=0).astype(jnp.bfloat16)
-    near = got[:, 32:].reshape(8 * MOST, width)
-
-    block = jnp.concatenate([quarter, near], axis=0)
+    block = settled(got)
     line = jnp.stack([block] + [turn(block, s, True) for s in (1, 2, 3)])
     cands, chosen = line[:, :32].reshape(128, width), line[:, 32:].reshape(128, width)
     chosen = [chosen] + [turn(chosen, s, False) for s in (1, 2, 3)]
     cands = [cands] + [turn(cands, s, False) for s in (1, 2, 3)]
 
-    best = on_chip(best_kernel, (2, rows), embeddings, coverage.reshape(1, rows), *chosen, partner)
+    best = on_chip(best_kernel, (2, rows), 1, [pltpu.VMEM((width, 512), jnp.bfloat16)], 24, embeddings, coverage.reshape(1, rows), *chosen, partner)
+    turned = turned_pieces(cands)
     cover = jnp.maximum(best, swap(best, 0, 1)[::-1])
-    part = on_chip(gain_kernel, (16, 32), embeddings, cover, *cands, partner).reshape(128, 4)
-    parts = lax.all_to_all(part, CHIPS, 0, 0)
-    return cover[0], jnp.sum(parts, axis=0)
+    part = on_chip(gain_kernel, (128, 32), 2, [], 52, cover, turned, embeddings, partner)
+    parts = lax.all_to_all(part, CHIPS, 0, 0, tiled=True)
+    gains = lax.dynamic_slice_in_dim(jnp.sum(parts, axis=0), lax.axis_index("z") * 4, 4)
+    return cover[0], gains
 
 
 def solution(mesh):

time: 96.5 us -> 96.7 us (level)
  Pallas kernels: 15.2 us -> 19.3 us
  blocking collectives: 23.8 us -> 20.7 us
  waiting for transfers between devices: 21.6 us -> 23.6 us
  other arithmetic: 3.32 us -> 1.84 us
    pallas_call x2, Pallas kernels: 11.1 us -> 15 us  [on_chip(): pl.pallas_call(kernel, out_shape=jax.ShapeDtypeStruct(out, jnp.float32),...]
    all_to_all x1, blocking collectives: 23.8 us -> 20.7 us  [local(): lax.all_to_all(jnp.broadcast_to(send, (8, 32 + MOST, width)), 'z', 0, 0)]
    reduce_sum x2 -> x1, other arithmetic: 1.72 us -> 0.15 us  [local(): jnp.sum(parts, axis=0)]
    ppermute x9, waiting for transfers between devices: 7.11 us -> 8.6 us  [turn(): lax.ppermute(value, AXES, pairs_of(lambda y, x, z, c: (y, x ^ mask, z, c)...]
    ppermute x5 -> x4, starting transfers between devices: 11.9 us -> 11 us  [swap(): lax.ppermute(value, AXES, pairs_of(lambda y, x, z, c: (y ^ y_mask, x, z,...]
    ppermute x5 -> x4, waiting for transfers between devices: 4.52 us -> 4.99 us  [swap(): lax.ppermute(value, AXES, pairs_of(lambda y, x, z, c: (y ^ y_mask, x, z,...]
    pallas_call x1 -> x3, Pallas kernels: 4.04 us -> 4.27 us  [the longest x1 3.94 us: own_picks(): pl.pallas_call(pick_kernel, out_shape=[jax.ShapeDtypeStruct((64, width),...]
  transfers between devices with their start and end apart: 15 -> 14, of which waited for: 9 -> 9; matrix products, arithmetic and copies ran while one was open for 4% -> 1% of each run, Pallas kernels for 5% -> 8%
where the time goes in v4:
time: 96.7 us; the launch traced here: 96.5 us
  starting transfers between devices  28.6 us (30%)
  waiting for transfers between devices  23.6 us (24%)
  blocking collectives  20.7 us (21%)
  Pallas kernels  19.3 us (20%)
  other arithmetic  1.84 us (2%)
  local copies, waits for them, and re-layouts  1.65 us (2%)
    all_to_all x1, blocking collectives, local(): lax.all_to_all(jnp.broadcast_to(send, (8, 32 + MOST, width)), 'z', 0, 0)  20.7 us
    pallas_call x2, Pallas kernels, on_chip(): pl.pallas_call(kernel, out_shape=jax.ShapeDtypeStruct(out, jnp.float32),...  15 us
    ppermute x9, starting transfers between devices, turn(): lax.ppermute(value, AXES, pairs_of(lambda y, x, z, c: (y, x ^ mask, z, c)...  11.4 us
    ppermute x4, starting transfers between devices, swap(): lax.ppermute(value, AXES, pairs_of(lambda y, x, z, c: (y ^ y_mask, x, z,...  11 us
    all_to_all x1, waiting for transfers between devices, local(): parts = lax.all_to_all(part, CHIPS, 0, 0, tiled=True)  9.96 us
    ppermute x9, waiting for transfers between devices, turn(): lax.ppermute(value, AXES, pairs_of(lambda y, x, z, c: (y, x ^ mask, z, c)...  8.6 us
    all_to_all x1, starting transfers between devices, local(): parts = lax.all_to_all(part, CHIPS, 0, 0, tiled=True)  6.19 us
    ppermute x4, waiting for transfers between devices, swap(): lax.ppermute(value, AXES, pairs_of(lambda y, x, z, c: (y ^ y_mask, x, z,...  4.99 us
  transfers between devices with their start and end apart: 14, of which 9 were waited for; matrix products, arithmetic and copies ran while one was open for 1% of the time, Pallas kernels for 8%

profile of v4, /device:TPU:1, one launch (start us, length us, event | category | flops | bytes accessed | tf_op | source)
XLA Modules:
  0.0 96.5 jit_solution(7369801434390671390)
XLA Ops:
  0.7 3.9 %shard_map.59 = (bf16[64,768]{1,0:T(8,128)(2,1)}, bf16[64,768]{1,0:T(8,128)(2,1)}, bf16[4,768]{1,0:T(4,128)(2,1)}) custom-call(s32[4,128]{1,0:T(4,128)} %bitcast.27, s32[1,128]{1,0:T(1,128)} %bitcast.28, bf16[2048,768]{1,0:T(8,128)(2,1)} %own_ref.3), custom_call_target="tpu_custom_call" | custom-call | flops 427819008 | bytes 4194304 | tf_op jit(solution)/shard_map/pallas_call | solution.py:206
  4.6 3.3 %collective-permute-start = (bf16[64,768]{1,0:T(8,128)(2,1)}, bf16[64,768]{1,0:T(8,128)(2,1)S(1)}, u32[]{:S(2)}, u32[]{:S(2)}) collective-permute-start(bf16[64,768]{1,0:T(8,128)(2,1)} %get-tuple-element.8), channel_id=1, source_target_pairs={{0,1},{1,0},{2,3},{3,2},{4,5},{5,4},{6,7},{7,6},{8,9},{9,8},{10,11... | collective-permute-start | bytes 294920 | tf_op jit(solution)/shard_map/ppermute | solution.py:34
  7.9 1.2 %collective-permute-done = bf16[64,768]{1,0:T(8,128)(2,1)S(1)} collective-permute-done((bf16[64,768]{1,0:T(8,128)(2,1)}, bf16[64,768]{1,0:T(8,128)(2,1)S(1)}, u32[]{:S(2)}, u32[]{:S(2)}) %collective-permute-start) | collective-permute-done | bytes 98336 | tf_op jit(solution)/shard_map/ppermute | solution.py:34
  9.1 0.9 add.9
  10.5 1.2 %collective-permute-start.1 = (bf16[32,768]{1,0:T(8,128)(2,1)S(1)}, bf16[32,768]{1,0:T(8,128)(2,1)S(1)}, u32[]{:S(2)}, u32[]{:S(2)}) collective-permute-start(bf16[32,768]{1,0:T(8,128)(2,1)S(1)} %slice.16), channel_id=1, source_target_pairs={{0,16},{1,17},{2,18},{3,19},{4,20},{5,21},{6,22},{7,23},{8,24},{9,... | collective-permute-start | bytes 147464 | tf_op jit(solution)/shard_map/ppermute | solution.py:34
  11.6 3.3 %collective-permute-done.1 = bf16[32,768]{1,0:T(8,128)(2,1)S(1)} collective-permute-done((bf16[32,768]{1,0:T(8,128)(2,1)S(1)}, bf16[32,768]{1,0:T(8,128)(2,1)S(1)}, u32[]{:S(2)}, u32[]{:S(2)}) %collective-permute-start.1) | collective-permute-done | bytes 49184 | tf_op jit(solution)/shard_map/ppermute | solution.py:34
  14.9 0.7 pad_maximum_fusion.1
  15.7 20.7 %all_to_all.14.got_ref = bf16[8,36,768]{2,1,0:T(8,128)(2,1)S(1)} all-to-all(bf16[8,36,768]{2,1,0:T(8,128)(2,1)S(1)} %broadcast_in_dim.3), channel_id=1, replica_groups=mesh['ylo'=2,'x'=4,'yhi'=2,'z'=8,'core'=2] {'z'}, dimensions={0} | all-to-all | bytes 884736 | tf_op jit(solution)/shard_map/all_to_all | solution.py:226
  36.5 1.4 %collective-permute-start.2 = (bf16[64,768]{1,0:T(8,128)(2,1)S(1)}, bf16[64,768]{1,0:T(8,128)(2,1)S(1)}, u32[]{:S(2)}, u32[]{:S(2)}) collective-permute-start(bf16[64,768]{1,0:T(8,128)(2,1)S(1)} %shard_map.60), channel_id=1, source_target_pairs={{0,32},{1,129},{2,34},{3,131},{4,36},{5,133},{6,38},{7,135},{8,40}... | collective-permute-start | bytes 294920 | tf_op jit(solution)/shard_map/ppermute | solution.py:38
  37.8 2.6 %collective-permute-start.3 = (bf16[64,768]{1,0:T(8,128)(2,1)S(1)}, bf16[64,768]{1,0:T(8,128)(2,1)S(1)}, u32[]{:S(2)}, u32[]{:S(2)}) collective-permute-start(bf16[64,768]{1,0:T(8,128)(2,1)S(1)} %shard_map.60), channel_id=1, source_target_pairs={{0,64},{1,17},{2,66},{3,19},{4,68},{5,21},{6,70},{7,23},{8,72},{9,... | collective-permute-start | bytes 294920 | tf_op jit(solution)/shard_map/ppermute | solution.py:38
  40.5 3.0 %collective-permute-done.3 = bf16[64,768]{1,0:T(8,128)(2,1)S(1)} collective-permute-done((bf16[64,768]{1,0:T(8,128)(2,1)S(1)}, bf16[64,768]{1,0:T(8,128)(2,1)S(1)}, u32[]{:S(2)}, u32[]{:S(2)}) %collective-permute-start.3) | collective-permute-done | bytes 98336 | tf_op jit(solution)/shard_map/ppermute | solution.py:38
  43.5 1.6 %collective-permute-done.4 = bf16[64,768]{1,0:T(8,128)(2,1)S(1)} collective-permute-done((bf16[64,768]{1,0:T(8,128)(2,1)S(1)}, bf16[64,768]{1,0:T(8,128)(2,1)S(1)}, u32[]{:S(2)}, u32[]{:S(2)}) %collective-permute-start.4) | collective-permute-done | bytes 98336 | tf_op jit(solution)/shard_map/ppermute | solution.py:38
  45.2 1.4 %collective-permute-start.5 = (bf16[128,768]{1,0:T(8,128)(2,1)S(1)}, bf16[128,768]{1,0:T(8,128)(2,1)S(1)}, u32[]{:S(2)}, u32[]{:S(2)}) collective-permute-start(bf16[128,768]{1,0:T(8,128)(2,1)S(1)} %bitcast.18), channel_id=1, source_target_pairs={{0,128},{1,33},{2,130},{3,35},{4,132},{5,37},{6,134},{7,39},{8,136... | collective-permute-start | bytes 589832 | tf_op jit(solution)/shard_map/ppermute | solution.py:38
  46.7 2.6 %collective-permute-start.6 = (bf16[128,768]{1,0:T(8,128)(2,1)S(1)}, bf16[128,768]{1,0:T(8,128)(2,1)S(1)}, u32[]{:S(2)}, u32[]{:S(2)}) collective-permute-start(bf16[128,768]{1,0:T(8,128)(2,1)S(1)} %bitcast.19), channel_id=1, source_target_pairs={{0,16},{1,65},{2,18},{3,67},{4,20},{5,69},{6,22},{7,71},{8,24},{9,... | collective-permute-start | bytes 589832 | tf_op jit(solution)/shard_map/ppermute | solution.py:38
  49.8 3.3 %collective-permute-start.11 = (bf16[128,768]{1,0:T(8,128)(2,1)S(1)}, bf16[128,768]{1,0:T(8,128)(2,1)S(1)}, u32[]{:S(2)}, u32[]{:S(2)}) collective-permute-start(bf16[128,768]{1,0:T(8,128)(2,1)S(1)} %bitcast.14), channel_id=1, source_target_pairs={{0,16},{1,65},{2,18},{3,67},{4,20},{5,69},{6,22},{7,71},{8,24},{9,... | collective-permute-start | bytes 589832 | tf_op jit(solution)/shard_map/ppermute | solution.py:38
  53.1 1.4 %collective-permute-done.6.c2 = bf16[128,768]{1,0:T(8,128)(2,1)S(1)} collective-permute-done((bf16[128,768]{1,0:T(8,128)(2,1)S(1)}, bf16[128,768]{1,0:T(8,128)(2,1)S(1)}, u32[]{:S(2)}, u32[]{:S(2)}) %collective-permute-start.6) | collective-permute-done | bytes 196640 | tf_op jit(solution)/shard_map/ppermute | solution.py:38
  54.5 2.0 %collective-permute-done.7.c3 = bf16[128,768]{1,0:T(8,128)(2,1)S(1)} collective-permute-done((bf16[128,768]{1,0:T(8,128)(2,1)S(1)}, bf16[128,768]{1,0:T(8,128)(2,1)S(1)}, u32[]{:S(2)}, u32[]{:S(2)}) %collective-permute-start.7) | collective-permute-done | bytes 196640 | tf_op jit(solution)/shard_map/ppermute | solution.py:38
  56.6 7.2 %shard_map.61 = f32[2,2048]{1,0:T(2,128)S(1)} custom-call(bf16[2048,768]{1,0:T(8,128)(2,1)S(1)} %copy-done, f32[1,2048]{1,0:T(1,128)S(1)} %bitcast.22, bf16[128,768]{1,0:T(8,128)(2,1)S(1)} %bitcast.21, bf16[128,768]{1,0:T(8,128)(2,1)S(1)} %collective-permute-done.5.c1, bf16[128,768]{1,0:T(8,128)(2,1)S(1)} %collective-permute-done.6.c2, ...), custom_call_target="tpu_custom_call" | custom-call | flops 3221225472 | bytes 8388608 | tf_op jit(solution)/shard_map/pallas_call | solution.py:132
  63.8 6.1 %collective-permute-start.9 = (f32[2,2048]{1,0:T(2,128)S(1)}, f32[2,2048]{1,0:T(2,128)S(1)}, u32[]{:S(2)}, u32[]{:S(2)}) collective-permute-start(f32[2,2048]{1,0:T(2,128)S(1)} %shard_map.61), channel_id=1, source_target_pairs={{0,1},{1,0},{2,3},{3,2},{4,5},{5,4},{6,7},{7,6},{8,9},{9,8},{10,11... | collective-permute-start | bytes 49160 | tf_op jit(solution)/shard_map/ppermute | solution.py:34
  71.1 7.8 %shard_map.63 = f32[128,32]{1,0:T(8,128)} custom-call(f32[2,2048]{1,0:T(2,128)S(1)} %max.3.cover_ref, bf16[768,512]{1,0:T(8,128)(2,1)S(1)} %shard_map.62.turned, bf16[2048,768]{1,0:T(8,128)(2,1)} %own_ref.3, bf16[2048,768]{1,0:T(8,128)(2,1)} %copy-done.1), custom_call_target="tpu_custom_call" | custom-call | flops 3221225472 | bytes 8388608 | tf_op jit(solution)/shard_map/pallas_call | solution.py:132
  79.0 6.2 %all-to-all-start.1 = ((f32[128,1,32]{2,1,0:T(1,128)}), f32[128,1,32]{2,1,0:T(1,128)S(1)}, u32[]{:S(2)}, u32[]{:S(2)}) async-start(f32[128,1,32]{2,1,0:T(1,128)} %bitcast.11), calls=%async_computation.1 | async-start | bytes 131072 | tf_op jit(solution)/shard_map/all_to_all | solution.py:237
  85.2 0.6 slice.21
  85.8 10.0 %all-to-all-done.1 = f32[128,1,32]{2,1,0:T(1,128)S(1)} async-done(((f32[128,1,32]{2,1,0:T(1,128)}), f32[128,1,32]{2,1,0:T(1,128)S(1)}, u32[]{:S(2)}, u32[]{:S(2)}) %all-to-all-start.1) | async-done | bytes 16416 | tf_op jit(solution)/shard_map/all_to_all | solution.py:237
  95.9 0.6 dynamic_slice.3
  (28 shorter events, 2.6 us)
Async XLA Ops:
  0.6 9.4 %copy-start = (bf16[2048,768]{1,0:T(8,128)(2,1)S(1)}, bf16[2048,768]{1,0:T(8,128)(2,1)}, u32[]{:S(2)}) copy-start(bf16[2048,768]{1,0:T(8,128)(2,1)} %own_ref.3) | copy-start | bytes 9437188
  0.6 55.9 %copy-start.2 = (f32[2048]{0:T(1024)S(1)}, f32[2048]{0:T(1024)}, u32[]{:S(2)}) copy-start(f32[2048]{0:T(1024)} %param.5) | copy-start | bytes 24580
  4.6 4.5 %collective-permute-start = (bf16[64,768]{1,0:T(8,128)(2,1)}, bf16[64,768]{1,0:T(8,128)(2,1)S(1)}, u32[]{:S(2)}, u32[]{:S(2)}) collective-permute-start(bf16[64,768]{1,0:T(8,128)(2,1)} %get-tuple-element.8), channel_id=1, source_target_pairs={{0,1},{1,0},{2,3},{3,2},{4,5},{5,4},{6,7},{7,6},{8,9},{9,8},{10,11... | collective-permute-start | bytes 294920 | tf_op jit(solution)/shard_map/ppermute | solution.py:34
  10.0 46.5 %collective-permute-start.8 = (bf16[2048,768]{1,0:T(8,128)(2,1)S(1)}, bf16[2048,768]{1,0:T(8,128)(2,1)S(1)}, u32[]{:S(2)}, u32[]{:S(2)}) collective-permute-start(bf16[2048,768]{1,0:T(8,128)(2,1)S(1)} %copy-done), channel_id=1, source_target_pairs={{0,1},{1,0},{2,3},{3,2},{4,5},{5,4},{6,7},{7,6},{8,9},{9,8},{10,11... | collective-permute-start | bytes 9437192 | tf_op jit(solution)/shard_map/ppermute | solution.py:34
  10.5 4.4 %collective-permute-start.1 = (bf16[32,768]{1,0:T(8,128)(2,1)S(1)}, bf16[32,768]{1,0:T(8,128)(2,1)S(1)}, u32[]{:S(2)}, u32[]{:S(2)}) collective-permute-start(bf16[32,768]{1,0:T(8,128)(2,1)S(1)} %slice.16), channel_id=1, source_target_pairs={{0,16},{1,17},{2,18},{3,19},{4,20},{5,21},{6,22},{7,23},{8,24},{9,... | collective-permute-start | bytes 147464 | tf_op jit(solution)/shard_map/ppermute | solution.py:34
  36.5 4.0 %collective-permute-start.2 = (bf16[64,768]{1,0:T(8,128)(2,1)S(1)}, bf16[64,768]{1,0:T(8,128)(2,1)S(1)}, u32[]{:S(2)}, u32[]{:S(2)}) collective-permute-start(bf16[64,768]{1,0:T(8,128)(2,1)S(1)} %shard_map.60), channel_id=1, source_target_pairs={{0,32},{1,129},{2,34},{3,131},{4,36},{5,133},{6,38},{7,135},{8,40}... | collective-permute-start | bytes 294920 | tf_op jit(solution)/shard_map/ppermute | solution.py:38
  37.8 5.7 %collective-permute-start.3 = (bf16[64,768]{1,0:T(8,128)(2,1)S(1)}, bf16[64,768]{1,0:T(8,128)(2,1)S(1)}, u32[]{:S(2)}, u32[]{:S(2)}) collective-permute-start(bf16[64,768]{1,0:T(8,128)(2,1)S(1)} %shard_map.60), channel_id=1, source_target_pairs={{0,64},{1,17},{2,66},{3,19},{4,68},{5,21},{6,70},{7,23},{8,72},{9,... | collective-permute-start | bytes 294920 | tf_op jit(solution)/shard_map/ppermute | solution.py:38
  40.5 4.7 %collective-permute-start.4 = (bf16[64,768]{1,0:T(8,128)(2,1)S(1)}, bf16[64,768]{1,0:T(8,128)(2,1)S(1)}, u32[]{:S(2)}, u32[]{:S(2)}) collective-permute-start(bf16[64,768]{1,0:T(8,128)(2,1)S(1)} %shard_map.60), channel_id=1, source_target_pairs={{0,96},{1,145},{2,98},{3,147},{4,100},{5,149},{6,102},{7,151},{8,1... | collective-permute-start | bytes 294920 | tf_op jit(solution)/shard_map/ppermute | solution.py:38
  45.2 4.6 %collective-permute-start.5 = (bf16[128,768]{1,0:T(8,128)(2,1)S(1)}, bf16[128,768]{1,0:T(8,128)(2,1)S(1)}, u32[]{:S(2)}, u32[]{:S(2)}) collective-permute-start(bf16[128,768]{1,0:T(8,128)(2,1)S(1)} %bitcast.18), channel_id=1, source_target_pairs={{0,128},{1,33},{2,130},{3,35},{4,132},{5,37},{6,134},{7,39},{8,136... | collective-permute-start | bytes 589832 | tf_op jit(solution)/shard_map/ppermute | solution.py:38
  46.7 7.9 %collective-permute-start.6 = (bf16[128,768]{1,0:T(8,128)(2,1)S(1)}, bf16[128,768]{1,0:T(8,128)(2,1)S(1)}, u32[]{:S(2)}, u32[]{:S(2)}) collective-permute-start(bf16[128,768]{1,0:T(8,128)(2,1)S(1)} %bitcast.19), channel_id=1, source_target_pairs={{0,16},{1,65},{2,18},{3,67},{4,20},{5,69},{6,22},{7,71},{8,24},{9,... | collective-permute-start | bytes 589832 | tf_op jit(solution)/shard_map/ppermute | solution.py:38
  49.3 7.3 %collective-permute-start.7 = (bf16[128,768]{1,0:T(8,128)(2,1)S(1)}, bf16[128,768]{1,0:T(8,128)(2,1)S(1)}, u32[]{:S(2)}, u32[]{:S(2)}) collective-permute-start(bf16[128,768]{1,0:T(8,128)(2,1)S(1)} %bitcast.20), channel_id=1, source_target_pairs={{0,144},{1,97},{2,146},{3,99},{4,148},{5,101},{6,150},{7,103},{8,1... | collective-permute-start | bytes 589832 | tf_op jit(solution)/shard_map/ppermute | solution.py:38
  49.3 20.6 %collective-permute-start.10 = (bf16[128,768]{1,0:T(8,128)(2,1)S(1)}, bf16[128,768]{1,0:T(8,128)(2,1)S(1)}, u32[]{:S(2)}, u32[]{:S(2)}) collective-permute-start(bf16[128,768]{1,0:T(8,128)(2,1)S(1)} %bitcast.13), channel_id=1, source_target_pairs={{0,128},{1,33},{2,130},{3,35},{4,132},{5,37},{6,134},{7,39},{8,136... | collective-permute-start | bytes 589832 | tf_op jit(solution)/shard_map/ppermute | solution.py:38
  49.8 20.0 %collective-permute-start.11 = (bf16[128,768]{1,0:T(8,128)(2,1)S(1)}, bf16[128,768]{1,0:T(8,128)(2,1)S(1)}, u32[]{:S(2)}, u32[]{:S(2)}) collective-permute-start(bf16[128,768]{1,0:T(8,128)(2,1)S(1)} %bitcast.14), channel_id=1, source_target_pairs={{0,16},{1,65},{2,18},{3,67},{4,20},{5,69},{6,22},{7,71},{8,24},{9,... | collective-permute-start | bytes 589832 | tf_op jit(solution)/shard_map/ppermute | solution.py:38
  54.5 15.4 %collective-permute-start.12 = (bf16[128,768]{1,0:T(8,128)(2,1)S(1)}, bf16[128,768]{1,0:T(8,128)(2,1)S(1)}, u32[]{:S(2)}, u32[]{:S(2)}) collective-permute-start(bf16[128,768]{1,0:T(8,128)(2,1)S(1)} %bitcast.15), channel_id=1, source_target_pairs={{0,144},{1,97},{2,146},{3,99},{4,148},{5,101},{6,150},{7,103},{8,1... | collective-permute-start | bytes 589832 | tf_op jit(solution)/shard_map/ppermute | solution.py:38
  56.5 7.2 %copy-start.1 = (bf16[2048,768]{1,0:T(8,128)(2,1)}, bf16[2048,768]{1,0:T(8,128)(2,1)S(1)}, u32[]{:S(2)}) copy-start(bf16[2048,768]{1,0:T(8,128)(2,1)S(1)} %collective-permute-done.8.partner_ref) | copy-start | bytes 9437188
  63.8 6.9 %collective-permute-start.9 = (f32[2,2048]{1,0:T(2,128)S(1)}, f32[2,2048]{1,0:T(2,128)S(1)}, u32[]{:S(2)}, u32[]{:S(2)}) collective-permute-start(f32[2,2048]{1,0:T(2,128)S(1)} %shard_map.61), channel_id=1, source_target_pairs={{0,1},{1,0},{2,3},{3,2},{4,5},{5,4},{6,7},{7,6},{8,9},{9,8},{10,11... | collective-permute-start | bytes 49160 | tf_op jit(solution)/shard_map/ppermute | solution.py:34
  79.0 16.8 %all-to-all-start.1 = ((f32[128,1,32]{2,1,0:T(1,128)}), f32[128,1,32]{2,1,0:T(1,128)S(1)}, u32[]{:S(2)}, u32[]{:S(2)}) async-start(f32[128,1,32]{2,1,0:T(1,128)} %bitcast.11), calls=%async_computation.1 | async-start | bytes 131072 | tf_op jit(solution)/shard_map/all_to_all | solution.py:237

commit v5 on v4

--- a/solution.py
+++ b/solution.py
@@ -13,7 +13,7 @@
 BLK = ("ylo", "x")
 CHIPS = ("ylo", "x", "yhi", "z")
 MOST = 4
-STEP = 256
+STEP = 512
 
 
 def place(y, x, z, core):
@@ -76,17 +76,12 @@
     ]
 
 
-def best_kernel(own_ref, coverage_ref, c0, c1, c2, c3, partner_ref, best_ref, partner, turned, arrivals):
+def best_kernel(own_ref, coverage_ref, c0, c1, c2, c3, partner_ref, best_ref, turned):
     rows, width = own_ref.shape
     scale = 1.0 / width**0.5
-    copies = fetches(partner_ref, partner, arrivals)
-    for copy in copies:
-        copy.start()
     turned_table((c0, c1, c2, c3), turned)
-    for t, table in enumerate((own_ref, partner)):
-        for k, start in enumerate(range(0, rows, STEP)):
-            if t == 1:
-                copies[k].wait()
+    for t, table in enumerate((own_ref, partner_ref)):
+        for start in range(0, rows, STEP):
             sims = tile_sims(table, turned, start)
             top = functools.reduce(jnp.maximum, [sims[:, l : l + 128] for l in range(0, 512, 128)])
             for r in range(0, STEP, 128):
@@ -97,20 +92,19 @@
                 best_ref[t : t + 1, here] = row
 
 
-def gain_kernel(cover_ref, turned, own_ref, partner_ref, gain_ref, own, partner, own_arrivals, arrivals):
-    rows, width = own.shape
+def gain_kernel(own_ref, best_ref, other_ref, turned, partner_ref, gain_ref, cover_ref):
+    rows, width = own_ref.shape
     scale = 1.0 / width**0.5
-    copies = [fetches(own_ref, own, own_arrivals), fetches(partner_ref, partner, arrivals)]
-    for copy in copies[0] + copies[1]:
-        copy.start()
     total = jnp.zeros((8, 512), jnp.float32)
-    for t, table in enumerate((own, partner)):
-        for k, start in enumerate(range(0, rows, STEP)):
-            copies[t][k].wait()
+    for t, table in enumerate((own_ref, partner_ref)):
+        for start in range(0, rows, STEP):
             sims = tile_sims(table, turned, start)
             for r in range(0, STEP, 128):
-                line = cover_ref[t : t + 1, pl.ds(start + r, 128)] * width**0.5
-                floor = jnp.broadcast_to(line, (128, 128)).T
+                here = pl.ds(start + r, 128)
+                line = jnp.maximum(best_ref[t : t + 1, here], other_ref[1 - t : 2 - t, here])
+                if t == 0:
+                    cover_ref[:, here] = line
+                floor = jnp.broadcast_to(line * width**0.5, (128, 128)).T
                 over = jnp.maximum(sims[r : r + 128] - jnp.concatenate([floor] * 4, axis=1), 0.0)
                 total = total + jnp.sum(over.reshape(16, 8, 512), axis=0)
     sums = jnp.sum(total, axis=0, keepdims=True) * scale
@@ -126,18 +120,15 @@
             gain_ref[pl.ds(at * 8, 8), :] = jnp.broadcast_to(sums[:, lane : lane + 32], (8, 32))
 
 
-def on_chip(kernel, out, fetched, scratch, memory, *operands):
-    rows, width = operands[-1].shape
+def on_chip(kernel, outs, scratch, *operands):
     vmem = pl.BlockSpec(memory_space=pltpu.VMEM)
     return pl.pallas_call(
         kernel,
-        out_shape=jax.ShapeDtypeStruct(out, jnp.float32),
-        in_specs=[vmem] * (len(operands) - fetched) + [pl.BlockSpec(memory_space=pl.ANY)] * fetched,
-        out_specs=vmem,
-        scratch_shapes=[pltpu.VMEM((rows, width), jnp.bfloat16)] * fetched
-        + scratch
-        + [pltpu.SemaphoreType.DMA((rows // STEP,))] * fetched,
-        compiler_params=pltpu.CompilerParams(vmem_limit_bytes=memory << 20),
+        out_shape=[jax.ShapeDtypeStruct(out, jnp.float32) for out in outs],
+        in_specs=[vmem] * len(operands),
+        out_specs=[vmem] * len(outs),
+        scratch_shapes=scratch,
+        compiler_params=pltpu.CompilerParams(vmem_limit_bytes=16 << 20),
         cost_estimate=pl.CostEstimate(flops=4096 * 512 * 768 * 2, bytes_accessed=8 << 20, transcendentals=0),
     )(*operands)
 
@@ -230,10 +221,11 @@
     chosen = [chosen] + [turn(chosen, s, False) for s in (1, 2, 3)]
     cands = [cands] + [turn(cands, s, False) for s in (1, 2, 3)]
 
-    best = on_chip(best_kernel, (2, rows), 1, [pltpu.VMEM((width, 512), jnp.bfloat16)], 24, embeddings, coverage.reshape(1, rows), *chosen, partner)
+    table = [pltpu.VMEM((width, 512), jnp.bfloat16)]
+    best = on_chip(best_kernel, [(2, rows)], table, embeddings, coverage.reshape(1, rows), *chosen, partner)[0]
+    other = swap(best, 0, 1)
     turned = turned_pieces(cands)
-    cover = jnp.maximum(best, swap(best, 0, 1)[::-1])
-    part = on_chip(gain_kernel, (128, 32), 2, [], 52, cover, turned, embeddings, partner)
+    part, cover = on_chip(gain_kernel, [(128, 32), (1, rows)], [], embeddings, best, other, turned, partner)
     parts = lax.all_to_all(part, CHIPS, 0, 0, tiled=True)
     gains = lax.dynamic_slice_in_dim(jnp.sum(parts, axis=0), lax.axis_index("z") * 4, 4)
     return cover[0], gains

time: 96.7 us -> 88.9 us (0.919)
  Pallas kernels: 19.3 us -> 12 us
  local copies, waits for them, and re-layouts: 1.65 us -> 0.66 us
    pallas_call x2, Pallas kernels: 15 us -> 7.78 us  [on_chip(): pl.pallas_call(kernel, out_shape=[jax.ShapeDtypeStruct(out, jnp.float32)...]
  transfers between devices with their start and end apart: 14 -> 14, of which waited for: 9 -> 9; matrix products, arithmetic and copies ran while one was open for 1% -> 1% of each run, Pallas kernels for 8% -> 4%
where the time goes in v5:
time: 88.9 us; the launch traced here: 88.6 us
  starting transfers between devices  28.5 us (32%)
  waiting for transfers between devices  24.1 us (27%)
  blocking collectives  20.7 us (23%)
  Pallas kernels  12 us (13%)
  other arithmetic  1.83 us (2%)
    all_to_all x1, blocking collectives, local(): lax.all_to_all(jnp.broadcast_to(send, (8, 32 + MOST, width)), 'z', 0, 0)  20.7 us
    ppermute x9, starting transfers between devices, turn(): lax.ppermute(value, AXES, pairs_of(lambda y, x, z, c: (y, x ^ mask, z, c)...  11.4 us
    ppermute x4, starting transfers between devices, swap(): lax.ppermute(value, AXES, pairs_of(lambda y, x, z, c: (y ^ y_mask, x, z,...  11 us
    all_to_all x1, waiting for transfers between devices, local(): parts = lax.all_to_all(part, CHIPS, 0, 0, tiled=True)  10.5 us
    ppermute x9, waiting for transfers between devices, turn(): lax.ppermute(value, AXES, pairs_of(lambda y, x, z, c: (y, x ^ mask, z, c)...  8.6 us
    pallas_call x2, Pallas kernels, on_chip(): pl.pallas_call(kernel, out_shape=[jax.ShapeDtypeStruct(out, jnp.float32)...  7.78 us
    all_to_all x1, starting transfers between devices, local(): parts = lax.all_to_all(part, CHIPS, 0, 0, tiled=True)  6.06 us
    ppermute x4, waiting for transfers between devices, swap(): lax.ppermute(value, AXES, pairs_of(lambda y, x, z, c: (y ^ y_mask, x, z,...  4.99 us
  transfers between devices with their start and end apart: 14, of which 9 were waited for; matrix products, arithmetic and copies ran while one was open for 1% of the time, Pallas kernels for 4%

profile of v5, /device:TPU:1, one launch (start us, length us, event | category | flops | bytes accessed | tf_op | source)
XLA Modules:
  0.0 88.6 jit_solution(9171888835851955758)
XLA Ops:
  0.7 3.9 %shard_map.59 = (bf16[64,768]{1,0:T(8,128)(2,1)}, bf16[64,768]{1,0:T(8,128)(2,1)}, bf16[4,768]{1,0:T(4,128)(2,1)}) custom-call(s32[4,128]{1,0:T(4,128)} %bitcast.26, s32[1,128]{1,0:T(1,128)} %bitcast.27, bf16[2048,768]{1,0:T(8,128)(2,1)} %own_ref.3), custom_call_target="tpu_custom_call" | custom-call | flops 427819008 | bytes 4194304 | tf_op jit(solution)/shard_map/pallas_call | solution.py:197
  4.6 3.3 %collective-permute-start = (bf16[64,768]{1,0:T(8,128)(2,1)}, bf16[64,768]{1,0:T(8,128)(2,1)S(1)}, u32[]{:S(2)}, u32[]{:S(2)}) collective-permute-start(bf16[64,768]{1,0:T(8,128)(2,1)} %get-tuple-element.10), channel_id=1, source_target_pairs={{0,1},{1,0},{2,3},{3,2},{4,5},{5,4},{6,7},{7,6},{8,9},{9,8},{10,11... | collective-permute-start | bytes 294920 | tf_op jit(solution)/shard_map/ppermute | solution.py:34
  7.9 1.2 %collective-permute-done = bf16[64,768]{1,0:T(8,128)(2,1)S(1)} collective-permute-done((bf16[64,768]{1,0:T(8,128)(2,1)}, bf16[64,768]{1,0:T(8,128)(2,1)S(1)}, u32[]{:S(2)}, u32[]{:S(2)}) %collective-permute-start) | collective-permute-done | bytes 98336 | tf_op jit(solution)/shard_map/ppermute | solution.py:34
  9.1 0.9 %add.9 = bf16[64,768]{1,0:T(8,128)(2,1)S(1)} add(bf16[64,768]{1,0:T(8,128)(2,1)} %get-tuple-element.9, bf16[64,768]{1,0:T(8,128)(2,1)S(1)} %collective-permute-done) | non-fusion elementwise | flops 49152 | bytes 294912 | tf_op jit(solution)/shard_map/add | solution.py:212
  10.5 1.2 %collective-permute-start.1 = (bf16[32,768]{1,0:T(8,128)(2,1)S(1)}, bf16[32,768]{1,0:T(8,128)(2,1)S(1)}, u32[]{:S(2)}, u32[]{:S(2)}) collective-permute-start(bf16[32,768]{1,0:T(8,128)(2,1)S(1)} %slice.13), channel_id=1, source_target_pairs={{0,16},{1,17},{2,18},{3,19},{4,20},{5,21},{6,22},{7,23},{8,24},{9,... | collective-permute-start | bytes 147464 | tf_op jit(solution)/shard_map/ppermute | solution.py:34
  11.6 3.3 %collective-permute-done.1 = bf16[32,768]{1,0:T(8,128)(2,1)S(1)} collective-permute-done((bf16[32,768]{1,0:T(8,128)(2,1)S(1)}, bf16[32,768]{1,0:T(8,128)(2,1)S(1)}, u32[]{:S(2)}, u32[]{:S(2)}) %collective-permute-start.1) | collective-permute-done | bytes 49184 | tf_op jit(solution)/shard_map/ppermute | solution.py:34
  14.9 0.7 pad_maximum_fusion.1
  15.7 20.7 %all_to_all.14.got_ref = bf16[8,36,768]{2,1,0:T(8,128)(2,1)S(1)} all-to-all(bf16[8,36,768]{2,1,0:T(8,128)(2,1)S(1)} %broadcast_in_dim.3), channel_id=1, replica_groups=mesh['ylo'=2,'x'=4,'yhi'=2,'z'=8,'core'=2] {'z'}, dimensions={0} | all-to-all | bytes 884736 | tf_op jit(solution)/shard_map/all_to_all | solution.py:217
  36.5 1.4 %collective-permute-start.2 = (bf16[64,768]{1,0:T(8,128)(2,1)S(1)}, bf16[64,768]{1,0:T(8,128)(2,1)S(1)}, u32[]{:S(2)}, u32[]{:S(2)}) collective-permute-start(bf16[64,768]{1,0:T(8,128)(2,1)S(1)} %shard_map.60), channel_id=1, source_target_pairs={{0,32},{1,129},{2,34},{3,131},{4,36},{5,133},{6,38},{7,135},{8,40}... | collective-permute-start | bytes 294920 | tf_op jit(solution)/shard_map/ppermute | solution.py:38
  37.8 2.6 %collective-permute-start.3 = (bf16[64,768]{1,0:T(8,128)(2,1)S(1)}, bf16[64,768]{1,0:T(8,128)(2,1)S(1)}, u32[]{:S(2)}, u32[]{:S(2)}) collective-permute-start(bf16[64,768]{1,0:T(8,128)(2,1)S(1)} %shard_map.60), channel_id=1, source_target_pairs={{0,64},{1,17},{2,66},{3,19},{4,68},{5,21},{6,70},{7,23},{8,72},{9,... | collective-permute-start | bytes 294920 | tf_op jit(solution)/shard_map/ppermute | solution.py:38
  40.5 3.0 %collective-permute-done.3 = bf16[64,768]{1,0:T(8,128)(2,1)S(1)} collective-permute-done((bf16[64,768]{1,0:T(8,128)(2,1)S(1)}, bf16[64,768]{1,0:T(8,128)(2,1)S(1)}, u32[]{:S(2)}, u32[]{:S(2)}) %collective-permute-start.3) | collective-permute-done | bytes 98336 | tf_op jit(solution)/shard_map/ppermute | solution.py:38
  43.5 1.6 %collective-permute-done.4 = bf16[64,768]{1,0:T(8,128)(2,1)S(1)} collective-permute-done((bf16[64,768]{1,0:T(8,128)(2,1)S(1)}, bf16[64,768]{1,0:T(8,128)(2,1)S(1)}, u32[]{:S(2)}, u32[]{:S(2)}) %collective-permute-start.4) | collective-permute-done | bytes 98336 | tf_op jit(solution)/shard_map/ppermute | solution.py:38
  45.2 1.4 %collective-permute-start.5 = (bf16[128,768]{1,0:T(8,128)(2,1)S(1)}, bf16[128,768]{1,0:T(8,128)(2,1)S(1)}, u32[]{:S(2)}, u32[]{:S(2)}) collective-permute-start(bf16[128,768]{1,0:T(8,128)(2,1)S(1)} %bitcast.18), channel_id=1, source_target_pairs={{0,128},{1,33},{2,130},{3,35},{4,132},{5,37},{6,134},{7,39},{8,136... | collective-permute-start | bytes 589832 | tf_op jit(solution)/shard_map/ppermute | solution.py:38
  46.7 2.6 %collective-permute-start.6 = (bf16[128,768]{1,0:T(8,128)(2,1)S(1)}, bf16[128,768]{1,0:T(8,128)(2,1)S(1)}, u32[]{:S(2)}, u32[]{:S(2)}) collective-permute-start(bf16[128,768]{1,0:T(8,128)(2,1)S(1)} %bitcast.19), channel_id=1, source_target_pairs={{0,16},{1,65},{2,18},{3,67},{4,20},{5,69},{6,22},{7,71},{8,24},{9,... | collective-permute-start | bytes 589832 | tf_op jit(solution)/shard_map/ppermute | solution.py:38
  49.8 3.3 %collective-permute-start.11 = (bf16[128,768]{1,0:T(8,128)(2,1)S(1)}, bf16[128,768]{1,0:T(8,128)(2,1)S(1)}, u32[]{:S(2)}, u32[]{:S(2)}) collective-permute-start(bf16[128,768]{1,0:T(8,128)(2,1)S(1)} %bitcast.14), channel_id=1, source_target_pairs={{0,16},{1,65},{2,18},{3,67},{4,20},{5,69},{6,22},{7,71},{8,24},{9,... | collective-permute-start | bytes 589832 | tf_op jit(solution)/shard_map/ppermute | solution.py:38
  53.1 1.4 %collective-permute-done.6.c2 = bf16[128,768]{1,0:T(8,128)(2,1)S(1)} collective-permute-done((bf16[128,768]{1,0:T(8,128)(2,1)S(1)}, bf16[128,768]{1,0:T(8,128)(2,1)S(1)}, u32[]{:S(2)}, u32[]{:S(2)}) %collective-permute-start.6) | collective-permute-done | bytes 196640 | tf_op jit(solution)/shard_map/ppermute | solution.py:38
  54.5 2.0 %collective-permute-done.7.c3 = bf16[128,768]{1,0:T(8,128)(2,1)S(1)} collective-permute-done((bf16[128,768]{1,0:T(8,128)(2,1)S(1)}, bf16[128,768]{1,0:T(8,128)(2,1)S(1)}, u32[]{:S(2)}, u32[]{:S(2)}) %collective-permute-start.7) | collective-permute-done | bytes 196640 | tf_op jit(solution)/shard_map/ppermute | solution.py:38
  56.5 3.6 %shard_map.61.best_ref = f32[2,2048]{1,0:T(2,128)S(1)} custom-call(bf16[2048,768]{1,0:T(8,128)(2,1)S(1)} %copy-done, f32[1,2048]{1,0:T(1,128)S(1)} %bitcast.22, bf16[128,768]{1,0:T(8,128)(2,1)S(1)} %bitcast.21, bf16[128,768]{1,0:T(8,128)(2,1)S(1)} %collective-permute-done.5.c1, bf16[128,768]{1,0:T(8,128)(2,1)S(1)} %collective-permute-done.6.c2, ...), custom_call_target="tpu_custom_call" | custom-call | flops 3221225472 | bytes 8388608 | tf_op jit(solution)/shard_map/pallas_call | solution.py:125
  60.2 6.1 %collective-permute-start.9 = (f32[2,2048]{1,0:T(2,128)S(1)}, f32[2,2048]{1,0:T(2,128)S(1)}, u32[]{:S(2)}, u32[]{:S(2)}) collective-permute-start(f32[2,2048]{1,0:T(2,128)S(1)} %shard_map.61.best_ref), channel_id=1, source_target_pairs={{0,1},{1,0},{2,3},{3,2},{4,5},{5,4},{6,7},{7,6},{8,9},{9,8},{10,11... | collective-permute-start | bytes 49160 | tf_op jit(solution)/shard_map/ppermute | solution.py:34
  66.5 0.6 collective-permute-done.9.other_ref
  67.1 4.1 %shard_map.63 = (f32[128,32]{1,0:T(8,128)}, f32[1,2048]{1,0:T(1,128)}) custom-call(bf16[2048,768]{1,0:T(8,128)(2,1)S(1)} %copy-done, f32[2,2048]{1,0:T(2,128)S(1)} %shard_map.61.best_ref, f32[2,2048]{1,0:T(2,128)S(1)} %collective-permute-done.9.other_ref, bf16[768,512]{1,0:T(8,128)(2,1)S(1)} %shard_map.62.turned, ...), custom_call_target="tpu_custom_call" | custom-call | flops 3221225472 | bytes 8388608 | tf_op jit(solution)/shard_map/pallas_call | solution.py:125
  71.3 6.1 %all-to-all-start.1 = ((f32[128,1,32]{2,1,0:T(1,128)}), f32[128,1,32]{2,1,0:T(1,128)S(1)}, u32[]{:S(2)}, u32[]{:S(2)}) async-start(f32[128,1,32]{2,1,0:T(1,128)} %bitcast.11), calls=%async_computation.1 | async-start | bytes 131072 | tf_op jit(solution)/shard_map/all_to_all | solution.py:229
  77.3 10.5 %all-to-all-done.1 = f32[128,1,32]{2,1,0:T(1,128)S(1)} async-done(((f32[128,1,32]{2,1,0:T(1,128)}), f32[128,1,32]{2,1,0:T(1,128)S(1)}, u32[]{:S(2)}, u32[]{:S(2)}) %all-to-all-start.1) | async-done | bytes 16416 | tf_op jit(solution)/shard_map/all_to_all | solution.py:229
  88.0 0.6 dynamic_slice.3
  (23 shorter events, 1.6 us)
Async XLA Ops:
  0.6 9.4 %copy-start = (bf16[2048,768]{1,0:T(8,128)(2,1)S(1)}, bf16[2048,768]{1,0:T(8,128)(2,1)}, u32[]{:S(2)}) copy-start(bf16[2048,768]{1,0:T(8,128)(2,1)} %own_ref.3) | copy-start | bytes 9437188
  0.6 55.9 %copy-start.1 = (f32[2048]{0:T(1024)S(1)}, f32[2048]{0:T(1024)}, u32[]{:S(2)}) copy-start(f32[2048]{0:T(1024)} %param.5) | copy-start | bytes 24580
  4.6 4.5 %collective-permute-start = (bf16[64,768]{1,0:T(8,128)(2,1)}, bf16[64,768]{1,0:T(8,128)(2,1)S(1)}, u32[]{:S(2)}, u32[]{:S(2)}) collective-permute-start(bf16[64,768]{1,0:T(8,128)(2,1)} %get-tuple-element.10), channel_id=1, source_target_pairs={{0,1},{1,0},{2,3},{3,2},{4,5},{5,4},{6,7},{7,6},{8,9},{9,8},{10,11... | collective-permute-start | bytes 294920 | tf_op jit(solution)/shard_map/ppermute | solution.py:34
  10.0 46.5 %collective-permute-start.8 = (bf16[2048,768]{1,0:T(8,128)(2,1)S(1)}, bf16[2048,768]{1,0:T(8,128)(2,1)S(1)}, u32[]{:S(2)}, u32[]{:S(2)}) collective-permute-start(bf16[2048,768]{1,0:T(8,128)(2,1)S(1)} %copy-done), channel_id=1, source_target_pairs={{0,1},{1,0},{2,3},{3,2},{4,5},{5,4},{6,7},{7,6},{8,9},{9,8},{10,11... | collective-permute-start | bytes 9437192 | tf_op jit(solution)/shard_map/ppermute | solution.py:34
  10.5 4.4 %collective-permute-start.1 = (bf16[32,768]{1,0:T(8,128)(2,1)S(1)}, bf16[32,768]{1,0:T(8,128)(2,1)S(1)}, u32[]{:S(2)}, u32[]{:S(2)}) collective-permute-start(bf16[32,768]{1,0:T(8,128)(2,1)S(1)} %slice.13), channel_id=1, source_target_pairs={{0,16},{1,17},{2,18},{3,19},{4,20},{5,21},{6,22},{7,23},{8,24},{9,... | collective-permute-start | bytes 147464 | tf_op jit(solution)/shard_map/ppermute | solution.py:34
  36.5 4.0 %collective-permute-start.2 = (bf16[64,768]{1,0:T(8,128)(2,1)S(1)}, bf16[64,768]{1,0:T(8,128)(2,1)S(1)}, u32[]{:S(2)}, u32[]{:S(2)}) collective-permute-start(bf16[64,768]{1,0:T(8,128)(2,1)S(1)} %shard_map.60), channel_id=1, source_target_pairs={{0,32},{1,129},{2,34},{3,131},{4,36},{5,133},{6,38},{7,135},{8,40}... | collective-permute-start | bytes 294920 | tf_op jit(solution)/shard_map/ppermute | solution.py:38
  37.8 5.7 %collective-permute-start.3 = (bf16[64,768]{1,0:T(8,128)(2,1)S(1)}, bf16[64,768]{1,0:T(8,128)(2,1)S(1)}, u32[]{:S(2)}, u32[]{:S(2)}) collective-permute-start(bf16[64,768]{1,0:T(8,128)(2,1)S(1)} %shard_map.60), channel_id=1, source_target_pairs={{0,64},{1,17},{2,66},{3,19},{4,68},{5,21},{6,70},{7,23},{8,72},{9,... | collective-permute-start | bytes 294920 | tf_op jit(solution)/shard_map/ppermute | solution.py:38
  40.5 4.7 %collective-permute-start.4 = (bf16[64,768]{1,0:T(8,128)(2,1)S(1)}, bf16[64,768]{1,0:T(8,128)(2,1)S(1)}, u32[]{:S(2)}, u32[]{:S(2)}) collective-permute-start(bf16[64,768]{1,0:T(8,128)(2,1)S(1)} %shard_map.60), channel_id=1, source_target_pairs={{0,96},{1,145},{2,98},{3,147},{4,100},{5,149},{6,102},{7,151},{8,1... | collective-permute-start | bytes 294920 | tf_op jit(solution)/shard_map/ppermute | solution.py:38
  45.2 4.6 %collective-permute-start.5 = (bf16[128,768]{1,0:T(8,128)(2,1)S(1)}, bf16[128,768]{1,0:T(8,128)(2,1)S(1)}, u32[]{:S(2)}, u32[]{:S(2)}) collective-permute-start(bf16[128,768]{1,0:T(8,128)(2,1)S(1)} %bitcast.18), channel_id=1, source_target_pairs={{0,128},{1,33},{2,130},{3,35},{4,132},{5,37},{6,134},{7,39},{8,136... | collective-permute-start | bytes 589832 | tf_op jit(solution)/shard_map/ppermute | solution.py:38
  46.7 7.9 %collective-permute-start.6 = (bf16[128,768]{1,0:T(8,128)(2,1)S(1)}, bf16[128,768]{1,0:T(8,128)(2,1)S(1)}, u32[]{:S(2)}, u32[]{:S(2)}) collective-permute-start(bf16[128,768]{1,0:T(8,128)(2,1)S(1)} %bitcast.19), channel_id=1, source_target_pairs={{0,16},{1,65},{2,18},{3,67},{4,20},{5,69},{6,22},{7,71},{8,24},{9,... | collective-permute-start | bytes 589832 | tf_op jit(solution)/shard_map/ppermute | solution.py:38
  49.3 7.3 %collective-permute-start.7 = (bf16[128,768]{1,0:T(8,128)(2,1)S(1)}, bf16[128,768]{1,0:T(8,128)(2,1)S(1)}, u32[]{:S(2)}, u32[]{:S(2)}) collective-permute-start(bf16[128,768]{1,0:T(8,128)(2,1)S(1)} %bitcast.20), channel_id=1, source_target_pairs={{0,144},{1,97},{2,146},{3,99},{4,148},{5,101},{6,150},{7,103},{8,1... | collective-permute-start | bytes 589832 | tf_op jit(solution)/shard_map/ppermute | solution.py:38
  49.3 17.0 %collective-permute-start.10 = (bf16[128,768]{1,0:T(8,128)(2,1)S(1)}, bf16[128,768]{1,0:T(8,128)(2,1)S(1)}, u32[]{:S(2)}, u32[]{:S(2)}) collective-permute-start(bf16[128,768]{1,0:T(8,128)(2,1)S(1)} %bitcast.13), channel_id=1, source_target_pairs={{0,128},{1,33},{2,130},{3,35},{4,132},{5,37},{6,134},{7,39},{8,136... | collective-permute-start | bytes 589832 | tf_op jit(solution)/shard_map/ppermute | solution.py:38
  49.8 16.4 %collective-permute-start.11 = (bf16[128,768]{1,0:T(8,128)(2,1)S(1)}, bf16[128,768]{1,0:T(8,128)(2,1)S(1)}, u32[]{:S(2)}, u32[]{:S(2)}) collective-permute-start(bf16[128,768]{1,0:T(8,128)(2,1)S(1)} %bitcast.14), channel_id=1, source_target_pairs={{0,16},{1,65},{2,18},{3,67},{4,20},{5,69},{6,22},{7,71},{8,24},{9,... | collective-permute-start | bytes 589832 | tf_op jit(solution)/shard_map/ppermute | solution.py:38
  54.5 11.8 %collective-permute-start.12 = (bf16[128,768]{1,0:T(8,128)(2,1)S(1)}, bf16[128,768]{1,0:T(8,128)(2,1)S(1)}, u32[]{:S(2)}, u32[]{:S(2)}) collective-permute-start(bf16[128,768]{1,0:T(8,128)(2,1)S(1)} %bitcast.15), channel_id=1, source_target_pairs={{0,144},{1,97},{2,146},{3,99},{4,148},{5,101},{6,150},{7,103},{8,1... | collective-permute-start | bytes 589832 | tf_op jit(solution)/shard_map/ppermute | solution.py:38
  60.2 6.9 %collective-permute-start.9 = (f32[2,2048]{1,0:T(2,128)S(1)}, f32[2,2048]{1,0:T(2,128)S(1)}, u32[]{:S(2)}, u32[]{:S(2)}) collective-permute-start(f32[2,2048]{1,0:T(2,128)S(1)} %shard_map.61.best_ref), channel_id=1, source_target_pairs={{0,1},{1,0},{2,3},{3,2},{4,5},{5,4},{6,7},{7,6},{8,9},{9,8},{10,11... | collective-permute-start | bytes 49160 | tf_op jit(solution)/shard_map/ppermute | solution.py:34
  71.3 16.6 %all-to-all-start.1 = ((f32[128,1,32]{2,1,0:T(1,128)}), f32[128,1,32]{2,1,0:T(1,128)S(1)}, u32[]{:S(2)}, u32[]{:S(2)}) async-start(f32[128,1,32]{2,1,0:T(1,128)} %bitcast.11), calls=%async_computation.1 | async-start | bytes 131072 | tf_op jit(solution)/shard_map/all_to_all | solution.py:229

commit v6 on v5

--- a/solution.py
+++ b/solution.py
@@ -65,15 +65,6 @@
         compiler_params=pltpu.CompilerParams(vmem_limit_bytes=8 << 20),
         cost_estimate=pl.CostEstimate(flops=1 << 20, bytes_accessed=2 << 20, transcendentals=0),
     )(*pieces)
-
-
-def fetches(source, target, arrivals):
-    step = target.shape[0] // arrivals.shape[0]
-    parts = [pl.ds(k * step, step) for k in range(arrivals.shape[0])]
-    return [
-        pltpu.make_async_copy(source.at[at, :], target.at[at, :], arrivals.at[k])
-        for k, at in enumerate(parts)
-    ]
 
 
 def best_kernel(own_ref, coverage_ref, c0, c1, c2, c3, partner_ref, best_ref, turned):
@@ -133,11 +124,8 @@
     )(*operands)
 
 
-def pick_kernel(chosen_ref, cand_ref, table_ref, kept_ref, given_ref, found_ref, table, arrivals):
+def pick_kernel(chosen_ref, cand_ref, table, kept_ref, given_ref, found_ref):
     rows, width = table.shape
-    copies = fetches(table_ref, table, arrivals)
-    for copy in copies:
-        copy.start()
     core, yhi = lax.axis_index("core"), lax.axis_index("yhi")
     base = lax.axis_index(AXES) * rows
 
@@ -157,13 +145,12 @@
         spots = jnp.where(row == s, least.astype(jnp.int32), spots)
 
     targets = jnp.concatenate([wanted, spots], axis=0)
-    step = rows // len(copies)
+    step = 512
     lanes = lax.broadcasted_iota(jnp.int32, (136, 128), 1)
     total = jnp.zeros((136, width), jnp.float32)
-    for k, copy in enumerate(copies):
+    for k in range(rows // step):
         hits = [targets == lanes + (k * step + l) for l in range(0, step, 128)]
         pick = jnp.concatenate([jnp.where(h, 1.0, 0.0).astype(jnp.bfloat16) for h in hits], axis=1)
-        copy.wait()
         total = total + jnp.dot(pick, table[pl.ds(k * step, step), :], preferred_element_type=jnp.float32)
     kept_ref[...] = total[:64].astype(jnp.bfloat16)
     given_ref[...] = total[64:128].astype(jnp.bfloat16)
@@ -198,10 +185,9 @@
         pick_kernel,
         out_shape=[jax.ShapeDtypeStruct((64, width), jnp.bfloat16)] * 2
         + [jax.ShapeDtypeStruct((MOST, width), jnp.bfloat16)],
-        in_specs=[vmem, vmem, pl.BlockSpec(memory_space=pl.ANY)],
+        in_specs=[vmem] * 3,
         out_specs=[vmem] * 3,
-        scratch_shapes=[pltpu.VMEM((rows, width), jnp.bfloat16), pltpu.SemaphoreType.DMA((4,))],
-        compiler_params=pltpu.CompilerParams(vmem_limit_bytes=60 << 20),
+        compiler_params=pltpu.CompilerParams(vmem_limit_bytes=40 << 20),
         cost_estimate=pl.CostEstimate(flops=136 * 2048 * 768 * 2, bytes_accessed=4 << 20, transcendentals=0),
     )(chosen_index.reshape(4, 128), candidate_index.reshape(1, 128), embeddings)
 

time: 88.9 us -> 87.4 us (0.983)
  local copies, waits for them, and re-layouts: 0.66 us -> 3.87 us
  Pallas kernels: 12 us -> 9.03 us
  other arithmetic: 1.83 us -> 0.25 us
    unnamed x4 -> x8, local copies, waits for them, and re-layouts: 0.01 us -> 3.22 us
    pallas_call x1, Pallas kernels: 3.94 us -> 0.93 us  [own_picks(): pl.pallas_call(pick_kernel, out_shape=[jax.ShapeDtypeStruct((64, width),...]
    add x1, other arithmetic: 0.92 us -> 0.03 us  [local(): half = kept + swap(given, 0, 1)]
  transfers between devices with their start and end apart: 14 -> 14, of which waited for: 9 -> 9; matrix products, arithmetic and copies ran while one was open for 1% -> 0% of each run, Pallas kernels for 4% -> 5%
where the time goes in v6:
time: 87.4 us; the launch traced here: 87.2 us
  starting transfers between devices  28.6 us (33%)
  waiting for transfers between devices  24 us (27%)
  blocking collectives  20.7 us (24%)
  Pallas kernels  9.03 us (10%)
  local copies, waits for them, and re-layouts  3.87 us (4%)
    all_to_all x1, blocking collectives, local(): lax.all_to_all(jnp.broadcast_to(send, (8, 32 + MOST, width)), 'z', 0, 0)  20.7 us
    ppermute x9, starting transfers between devices, turn(): lax.ppermute(value, AXES, pairs_of(lambda y, x, z, c: (y, x ^ mask, z, c)...  11.4 us
    ppermute x4, starting transfers between devices, swap(): lax.ppermute(value, AXES, pairs_of(lambda y, x, z, c: (y ^ y_mask, x, z,...  11 us
    all_to_all x1, waiting for transfers between devices, local(): parts = lax.all_to_all(part, CHIPS, 0, 0, tiled=True)  10.6 us
    ppermute x9, waiting for transfers between devices, turn(): lax.ppermute(value, AXES, pairs_of(lambda y, x, z, c: (y, x ^ mask, z, c)...  8.6 us
    pallas_call x2, Pallas kernels, on_chip(): pl.pallas_call(kernel, out_shape=[jax.ShapeDtypeStruct(out, jnp.float32)...  7.78 us
    all_to_all x1, starting transfers between devices, local(): parts = lax.all_to_all(part, CHIPS, 0, 0, tiled=True)  6.17 us
    ppermute x4, waiting for transfers between devices, swap(): lax.ppermute(value, AXES, pairs_of(lambda y, x, z, c: (y ^ y_mask, x, z,...  4.78 us
  transfers between devices with their start and end apart: 14, of which 9 were waited for; matrix products, arithmetic and copies ran while one was open for 0% of the time, Pallas kernels for 5%

profile of v6, /device:TPU:1, one launch (start us, length us, event | category | flops | bytes accessed | tf_op | source)
XLA Modules:
  0.0 87.2 jit_solution(15393025964882846375)
XLA Ops:
  0.6 1.9 %copy-done = bf16[2048,768]{1,0:T(8,128)(2,1)S(1)} copy-done((bf16[2048,768]{1,0:T(8,128)(2,1)S(1)}, bf16[2048,768]{1,0:T(8,128)(2,1)}, u32[]{:S(2)}) %copy-start) | copy-done | bytes 3145752
  2.5 0.7 copy-done.1
  3.2 0.7 copy-done.2
  3.9 0.9 %shard_map.59 = (bf16[64,768]{1,0:T(8,128)(2,1)S(1)}, bf16[64,768]{1,0:T(8,128)(2,1)S(1)}, bf16[4,768]{1,0:T(4,128)(2,1)S(1)}) custom-call(s32[4,128]{1,0:T(4,128)S(1)} %bitcast.22, s32[1,128]{1,0:T(1,128)S(1)} %bitcast.23, bf16[2048,768]{1,0:T(8,128)(2,1)S(1)} %copy-done), custom_call_target="tpu_custom_call" | custom-call | flops 427819008 | bytes 4194304 | tf_op jit(solution)/shard_map/pallas_call | solution.py:184
  4.8 3.3 %collective-permute-start = (bf16[64,768]{1,0:T(8,128)(2,1)S(1)}, bf16[64,768]{1,0:T(8,128)(2,1)S(1)}, u32[]{:S(2)}, u32[]{:S(2)}) collective-permute-start(bf16[64,768]{1,0:T(8,128)(2,1)S(1)} %get-tuple-element.10), channel_id=1, source_target_pairs={{0,1},{1,0},{2,3},{3,2},{4,5},{5,4},{6,7},{7,6},{8,9},{9,8},{10,11... | collective-permute-start | bytes 294920 | tf_op jit(solution)/shard_map/ppermute | solution.py:34
  8.1 0.9 %collective-permute-done = bf16[64,768]{1,0:T(8,128)(2,1)S(1)} collective-permute-done((bf16[64,768]{1,0:T(8,128)(2,1)S(1)}, bf16[64,768]{1,0:T(8,128)(2,1)S(1)}, u32[]{:S(2)}, u32[]{:S(2)}) %collective-permute-start) | collective-permute-done | bytes 98336 | tf_op jit(solution)/shard_map/ppermute | solution.py:34
  9.6 1.2 %collective-permute-start.1 = (bf16[32,768]{1,0:T(8,128)(2,1)S(1)}, bf16[32,768]{1,0:T(8,128)(2,1)S(1)}, u32[]{:S(2)}, u32[]{:S(2)}) collective-permute-start(bf16[32,768]{1,0:T(8,128)(2,1)S(1)} %slice.13), channel_id=1, source_target_pairs={{0,16},{1,17},{2,18},{3,19},{4,20},{5,21},{6,22},{7,23},{8,24},{9,... | collective-permute-start | bytes 147464 | tf_op jit(solution)/shard_map/ppermute | solution.py:34
  10.7 3.3 %collective-permute-done.1 = bf16[32,768]{1,0:T(8,128)(2,1)S(1)} collective-permute-done((bf16[32,768]{1,0:T(8,128)(2,1)S(1)}, bf16[32,768]{1,0:T(8,128)(2,1)S(1)}, u32[]{:S(2)}, u32[]{:S(2)}) %collective-permute-start.1) | collective-permute-done | bytes 49184 | tf_op jit(solution)/shard_map/ppermute | solution.py:34
  14.1 20.7 %all_to_all.14.got_ref = bf16[8,36,768]{2,1,0:T(8,128)(2,1)S(1)} all-to-all(bf16[8,36,768]{2,1,0:T(8,128)(2,1)S(1)} %broadcast_in_dim.3), channel_id=1, replica_groups=mesh['ylo'=2,'x'=4,'yhi'=2,'z'=8,'core'=2] {'z'}, dimensions={0} | all-to-all | bytes 884736 | tf_op jit(solution)/shard_map/all_to_all | solution.py:203
  34.9 1.4 %collective-permute-start.2 = (bf16[64,768]{1,0:T(8,128)(2,1)S(1)}, bf16[64,768]{1,0:T(8,128)(2,1)S(1)}, u32[]{:S(2)}, u32[]{:S(2)}) collective-permute-start(bf16[64,768]{1,0:T(8,128)(2,1)S(1)} %shard_map.60), channel_id=1, source_target_pairs={{0,32},{1,129},{2,34},{3,131},{4,36},{5,133},{6,38},{7,135},{8,40}... | collective-permute-start | bytes 294920 | tf_op jit(solution)/shard_map/ppermute | solution.py:38
  36.2 2.6 %collective-permute-start.3 = (bf16[64,768]{1,0:T(8,128)(2,1)S(1)}, bf16[64,768]{1,0:T(8,128)(2,1)S(1)}, u32[]{:S(2)}, u32[]{:S(2)}) collective-permute-start(bf16[64,768]{1,0:T(8,128)(2,1)S(1)} %shard_map.60), channel_id=1, source_target_pairs={{0,64},{1,17},{2,66},{3,19},{4,68},{5,21},{6,70},{7,23},{8,72},{9,... | collective-permute-start | bytes 294920 | tf_op jit(solution)/shard_map/ppermute | solution.py:38
  38.9 3.0 %collective-permute-done.3 = bf16[64,768]{1,0:T(8,128)(2,1)S(1)} collective-permute-done((bf16[64,768]{1,0:T(8,128)(2,1)S(1)}, bf16[64,768]{1,0:T(8,128)(2,1)S(1)}, u32[]{:S(2)}, u32[]{:S(2)}) %collective-permute-start.3) | collective-permute-done | bytes 98336 | tf_op jit(solution)/shard_map/ppermute | solution.py:38
  41.9 1.6 %collective-permute-done.4 = bf16[64,768]{1,0:T(8,128)(2,1)S(1)} collective-permute-done((bf16[64,768]{1,0:T(8,128)(2,1)S(1)}, bf16[64,768]{1,0:T(8,128)(2,1)S(1)}, u32[]{:S(2)}, u32[]{:S(2)}) %collective-permute-start.4) | collective-permute-done | bytes 98336 | tf_op jit(solution)/shard_map/ppermute | solution.py:38
  43.6 1.4 %collective-permute-start.5 = (bf16[128,768]{1,0:T(8,128)(2,1)S(1)}, bf16[128,768]{1,0:T(8,128)(2,1)S(1)}, u32[]{:S(2)}, u32[]{:S(2)}) collective-permute-start(bf16[128,768]{1,0:T(8,128)(2,1)S(1)} %bitcast.18), channel_id=1, source_target_pairs={{0,128},{1,33},{2,130},{3,35},{4,132},{5,37},{6,134},{7,39},{8,136... | collective-permute-start | bytes 589832 | tf_op jit(solution)/shard_map/ppermute | solution.py:38
  45.1 2.6 %collective-permute-start.6 = (bf16[128,768]{1,0:T(8,128)(2,1)S(1)}, bf16[128,768]{1,0:T(8,128)(2,1)S(1)}, u32[]{:S(2)}, u32[]{:S(2)}) collective-permute-start(bf16[128,768]{1,0:T(8,128)(2,1)S(1)} %bitcast.19), channel_id=1, source_target_pairs={{0,16},{1,65},{2,18},{3,67},{4,20},{5,69},{6,22},{7,71},{8,24},{9,... | collective-permute-start | bytes 589832 | tf_op jit(solution)/shard_map/ppermute | solution.py:38
  48.2 3.3 %collective-permute-start.11 = (bf16[128,768]{1,0:T(8,128)(2,1)S(1)}, bf16[128,768]{1,0:T(8,128)(2,1)S(1)}, u32[]{:S(2)}, u32[]{:S(2)}) collective-permute-start(bf16[128,768]{1,0:T(8,128)(2,1)S(1)} %bitcast.14), channel_id=1, source_target_pairs={{0,16},{1,65},{2,18},{3,67},{4,20},{5,69},{6,22},{7,71},{8,24},{9,... | collective-permute-start | bytes 589832 | tf_op jit(solution)/shard_map/ppermute | solution.py:38
  51.5 1.4 %collective-permute-done.6.c2 = bf16[128,768]{1,0:T(8,128)(2,1)S(1)} collective-permute-done((bf16[128,768]{1,0:T(8,128)(2,1)S(1)}, bf16[128,768]{1,0:T(8,128)(2,1)S(1)}, u32[]{:S(2)}, u32[]{:S(2)}) %collective-permute-start.6) | collective-permute-done | bytes 196640 | tf_op jit(solution)/shard_map/ppermute | solution.py:38
  52.9 2.0 %collective-permute-done.7.c3 = bf16[128,768]{1,0:T(8,128)(2,1)S(1)} collective-permute-done((bf16[128,768]{1,0:T(8,128)(2,1)S(1)}, bf16[128,768]{1,0:T(8,128)(2,1)S(1)}, u32[]{:S(2)}, u32[]{:S(2)}) %collective-permute-start.7) | collective-permute-done | bytes 196640 | tf_op jit(solution)/shard_map/ppermute | solution.py:38
  55.0 3.6 %shard_map.61.best_ref = f32[2,2048]{1,0:T(2,128)S(1)} custom-call(bf16[2048,768]{1,0:T(8,128)(2,1)S(1)} %copy-done, f32[1,2048]{1,0:T(1,128)S(1)} %bitcast.24, bf16[128,768]{1,0:T(8,128)(2,1)S(1)} %bitcast.21, bf16[128,768]{1,0:T(8,128)(2,1)S(1)} %collective-permute-done.5.c1, bf16[128,768]{1,0:T(8,128)(2,1)S(1)} %collective-permute-done.6.c2, ...), custom_call_target="tpu_custom_call" | custom-call | flops 3221225472 | bytes 8388608 | tf_op jit(solution)/shard_map/pallas_call | solution.py:116
  58.6 6.1 %collective-permute-start.9 = (f32[2,2048]{1,0:T(2,128)S(1)}, f32[2,2048]{1,0:T(2,128)S(1)}, u32[]{:S(2)}, u32[]{:S(2)}) collective-permute-start(f32[2,2048]{1,0:T(2,128)S(1)} %shard_map.61.best_ref), channel_id=1, source_target_pairs={{0,1},{1,0},{2,3},{3,2},{4,5},{5,4},{6,7},{7,6},{8,9},{9,8},{10,11... | collective-permute-start | bytes 49160 | tf_op jit(solution)/shard_map/ppermute | solution.py:34
  65.5 4.1 %shard_map.63 = (f32[128,32]{1,0:T(8,128)}, f32[1,2048]{1,0:T(1,128)}) custom-call(bf16[2048,768]{1,0:T(8,128)(2,1)S(1)} %copy-done, f32[2,2048]{1,0:T(2,128)S(1)} %shard_map.61.best_ref, f32[2,2048]{1,0:T(2,128)S(1)} %collective-permute-done.9.other_ref, bf16[768,512]{1,0:T(8,128)(2,1)S(1)} %shard_map.62.turned, ...), custom_call_target="tpu_custom_call" | custom-call | flops 3221225472 | bytes 8388608 | tf_op jit(solution)/shard_map/pallas_call | solution.py:116
  69.7 6.2 %all-to-all-start.1 = ((f32[128,1,32]{2,1,0:T(1,128)}), f32[128,1,32]{2,1,0:T(1,128)S(1)}, u32[]{:S(2)}, u32[]{:S(2)}) async-start(f32[128,1,32]{2,1,0:T(1,128)} %bitcast.11), calls=%async_computation.1 | async-start | bytes 131072 | tf_op jit(solution)/shard_map/all_to_all | solution.py:215
  75.8 10.6 %all-to-all-done.1 = f32[128,1,32]{2,1,0:T(1,128)S(1)} async-done(((f32[128,1,32]{2,1,0:T(1,128)}), f32[128,1,32]{2,1,0:T(1,128)S(1)}, u32[]{:S(2)}, u32[]{:S(2)}) %all-to-all-start.1) | async-done | bytes 16416 | tf_op jit(solution)/shard_map/all_to_all | solution.py:215
  86.6 0.6 dynamic_slice.3
  (27 shorter events, 2.2 us)
Async XLA Ops:
  0.6 1.9 %copy-start = (bf16[2048,768]{1,0:T(8,128)(2,1)S(1)}, bf16[2048,768]{1,0:T(8,128)(2,1)}, u32[]{:S(2)}) copy-start(bf16[2048,768]{1,0:T(8,128)(2,1)} %own_ref.3) | copy-start | bytes 9437188
  2.5 0.7 copy-start.1
  3.2 0.7 copy-start.2
  3.9 51.1 %copy-start.3 = (f32[2048]{0:T(1024)S(1)}, f32[2048]{0:T(1024)}, u32[]{:S(2)}) copy-start(f32[2048]{0:T(1024)} %param.5) | copy-start | bytes 24580
  4.8 4.3 %collective-permute-start = (bf16[64,768]{1,0:T(8,128)(2,1)S(1)}, bf16[64,768]{1,0:T(8,128)(2,1)S(1)}, u32[]{:S(2)}, u32[]{:S(2)}) collective-permute-start(bf16[64,768]{1,0:T(8,128)(2,1)S(1)} %get-tuple-element.10), channel_id=1, source_target_pairs={{0,1},{1,0},{2,3},{3,2},{4,5},{5,4},{6,7},{7,6},{8,9},{9,8},{10,11... | collective-permute-start | bytes 294920 | tf_op jit(solution)/shard_map/ppermute | solution.py:34
  9.1 45.8 %collective-permute-start.8 = (bf16[2048,768]{1,0:T(8,128)(2,1)S(1)}, bf16[2048,768]{1,0:T(8,128)(2,1)S(1)}, u32[]{:S(2)}, u32[]{:S(2)}) collective-permute-start(bf16[2048,768]{1,0:T(8,128)(2,1)S(1)} %copy-done), channel_id=1, source_target_pairs={{0,1},{1,0},{2,3},{3,2},{4,5},{5,4},{6,7},{7,6},{8,9},{9,8},{10,11... | collective-permute-start | bytes 9437192 | tf_op jit(solution)/shard_map/ppermute | solution.py:34
  9.6 4.4 %collective-permute-start.1 = (bf16[32,768]{1,0:T(8,128)(2,1)S(1)}, bf16[32,768]{1,0:T(8,128)(2,1)S(1)}, u32[]{:S(2)}, u32[]{:S(2)}) collective-permute-start(bf16[32,768]{1,0:T(8,128)(2,1)S(1)} %slice.13), channel_id=1, source_target_pairs={{0,16},{1,17},{2,18},{3,19},{4,20},{5,21},{6,22},{7,23},{8,24},{9,... | collective-permute-start | bytes 147464 | tf_op jit(solution)/shard_map/ppermute | solution.py:34
  34.9 4.0 %collective-permute-start.2 = (bf16[64,768]{1,0:T(8,128)(2,1)S(1)}, bf16[64,768]{1,0:T(8,128)(2,1)S(1)}, u32[]{:S(2)}, u32[]{:S(2)}) collective-permute-start(bf16[64,768]{1,0:T(8,128)(2,1)S(1)} %shard_map.60), channel_id=1, source_target_pairs={{0,32},{1,129},{2,34},{3,131},{4,36},{5,133},{6,38},{7,135},{8,40}... | collective-permute-start | bytes 294920 | tf_op jit(solution)/shard_map/ppermute | solution.py:38
  36.2 5.7 %collective-permute-start.3 = (bf16[64,768]{1,0:T(8,128)(2,1)S(1)}, bf16[64,768]{1,0:T(8,128)(2,1)S(1)}, u32[]{:S(2)}, u32[]{:S(2)}) collective-permute-start(bf16[64,768]{1,0:T(8,128)(2,1)S(1)} %shard_map.60), channel_id=1, source_target_pairs={{0,64},{1,17},{2,66},{3,19},{4,68},{5,21},{6,70},{7,23},{8,72},{9,... | collective-permute-start | bytes 294920 | tf_op jit(solution)/shard_map/ppermute | solution.py:38
  38.9 4.7 %collective-permute-start.4 = (bf16[64,768]{1,0:T(8,128)(2,1)S(1)}, bf16[64,768]{1,0:T(8,128)(2,1)S(1)}, u32[]{:S(2)}, u32[]{:S(2)}) collective-permute-start(bf16[64,768]{1,0:T(8,128)(2,1)S(1)} %shard_map.60), channel_id=1, source_target_pairs={{0,96},{1,145},{2,98},{3,147},{4,100},{5,149},{6,102},{7,151},{8,1... | collective-permute-start | bytes 294920 | tf_op jit(solution)/shard_map/ppermute | solution.py:38
  43.6 4.6 %collective-permute-start.5 = (bf16[128,768]{1,0:T(8,128)(2,1)S(1)}, bf16[128,768]{1,0:T(8,128)(2,1)S(1)}, u32[]{:S(2)}, u32[]{:S(2)}) collective-permute-start(bf16[128,768]{1,0:T(8,128)(2,1)S(1)} %bitcast.18), channel_id=1, source_target_pairs={{0,128},{1,33},{2,130},{3,35},{4,132},{5,37},{6,134},{7,39},{8,136... | collective-permute-start | bytes 589832 | tf_op jit(solution)/shard_map/ppermute | solution.py:38
  45.1 7.9 %collective-permute-start.6 = (bf16[128,768]{1,0:T(8,128)(2,1)S(1)}, bf16[128,768]{1,0:T(8,128)(2,1)S(1)}, u32[]{:S(2)}, u32[]{:S(2)}) collective-permute-start(bf16[128,768]{1,0:T(8,128)(2,1)S(1)} %bitcast.19), channel_id=1, source_target_pairs={{0,16},{1,65},{2,18},{3,67},{4,20},{5,69},{6,22},{7,71},{8,24},{9,... | collective-permute-start | bytes 589832 | tf_op jit(solution)/shard_map/ppermute | solution.py:38
  47.7 7.3 %collective-permute-start.7 = (bf16[128,768]{1,0:T(8,128)(2,1)S(1)}, bf16[128,768]{1,0:T(8,128)(2,1)S(1)}, u32[]{:S(2)}, u32[]{:S(2)}) collective-permute-start(bf16[128,768]{1,0:T(8,128)(2,1)S(1)} %bitcast.20), channel_id=1, source_target_pairs={{0,144},{1,97},{2,146},{3,99},{4,148},{5,101},{6,150},{7,103},{8,1... | collective-permute-start | bytes 589832 | tf_op jit(solution)/shard_map/ppermute | solution.py:38
  47.7 17.0 %collective-permute-start.10 = (bf16[128,768]{1,0:T(8,128)(2,1)S(1)}, bf16[128,768]{1,0:T(8,128)(2,1)S(1)}, u32[]{:S(2)}, u32[]{:S(2)}) collective-permute-start(bf16[128,768]{1,0:T(8,128)(2,1)S(1)} %bitcast.13), channel_id=1, source_target_pairs={{0,128},{1,33},{2,130},{3,35},{4,132},{5,37},{6,134},{7,39},{8,136... | collective-permute-start | bytes 589832 | tf_op jit(solution)/shard_map/ppermute | solution.py:38
  48.2 16.4 %collective-permute-start.11 = (bf16[128,768]{1,0:T(8,128)(2,1)S(1)}, bf16[128,768]{1,0:T(8,128)(2,1)S(1)}, u32[]{:S(2)}, u32[]{:S(2)}) collective-permute-start(bf16[128,768]{1,0:T(8,128)(2,1)S(1)} %bitcast.14), channel_id=1, source_target_pairs={{0,16},{1,65},{2,18},{3,67},{4,20},{5,69},{6,22},{7,71},{8,24},{9,... | collective-permute-start | bytes 589832 | tf_op jit(solution)/shard_map/ppermute | solution.py:38
  52.9 11.8 %collective-permute-start.12 = (bf16[128,768]{1,0:T(8,128)(2,1)S(1)}, bf16[128,768]{1,0:T(8,128)(2,1)S(1)}, u32[]{:S(2)}, u32[]{:S(2)}) collective-permute-start(bf16[128,768]{1,0:T(8,128)(2,1)S(1)} %bitcast.15), channel_id=1, source_target_pairs={{0,144},{1,97},{2,146},{3,99},{4,148},{5,101},{6,150},{7,103},{8,1... | collective-permute-start | bytes 589832 | tf_op jit(solution)/shard_map/ppermute | solution.py:38
  58.6 6.9 %collective-permute-start.9 = (f32[2,2048]{1,0:T(2,128)S(1)}, f32[2,2048]{1,0:T(2,128)S(1)}, u32[]{:S(2)}, u32[]{:S(2)}) collective-permute-start(f32[2,2048]{1,0:T(2,128)S(1)} %shard_map.61.best_ref), channel_id=1, source_target_pairs={{0,1},{1,0},{2,3},{3,2},{4,5},{5,4},{6,7},{7,6},{8,9},{9,8},{10,11... | collective-permute-start | bytes 49160 | tf_op jit(solution)/shard_map/ppermute | solution.py:34
  69.7 16.8 %all-to-all-start.1 = ((f32[128,1,32]{2,1,0:T(1,128)}), f32[128,1,32]{2,1,0:T(1,128)S(1)}, u32[]{:S(2)}, u32[]{:S(2)}) async-start(f32[128,1,32]{2,1,0:T(1,128)} %bitcast.11), calls=%async_computation.1 | async-start | bytes 131072 | tf_op jit(solution)/shard_map/all_to_all | solution.py:215

commit v7 on v6

--- a/solution.py
+++ b/solution.py
@@ -124,18 +124,17 @@
     )(*operands)
 
 
-def pick_kernel(chosen_ref, cand_ref, table, kept_ref, given_ref, found_ref):
-    rows, width = table.shape
+def spot_kernel(rows, index_ref, targets_ref):
     core, yhi = lax.axis_index("core"), lax.axis_index("yhi")
     base = lax.axis_index(AXES) * rows
 
     lane = lax.broadcasted_iota(jnp.int32, (8, 128), 1)
     quarter = lane >> 5
     source = ((yhi ^ (quarter & 1)) << 6) | ((lane & 28) << 1) | ((core ^ (quarter >> 1)) << 2) | (lane & 3)
-    wanted = jnp.take_along_axis(jnp.broadcast_to(cand_ref[...], (8, 128)), source, axis=1) - base
+    wanted = jnp.take_along_axis(jnp.broadcast_to(index_ref[4:5, :], (8, 128)), source, axis=1) - base
     wanted = jnp.broadcast_to(wanted[:1], (128, 128)).T
 
-    left = chosen_ref[...] - base
+    left = index_ref[:4, :] - base
     left = jnp.where((left >= 0) & (left < rows), left, rows).astype(jnp.float32)
     row = lax.broadcasted_iota(jnp.int32, (8, 128), 0)
     spots = jnp.full((8, 128), -1, jnp.int32)
@@ -144,7 +143,13 @@
         left = jnp.where(left == least, float(rows), left)
         spots = jnp.where(row == s, least.astype(jnp.int32), spots)
 
-    targets = jnp.concatenate([wanted, spots], axis=0)
+    targets_ref[:128, :] = wanted
+    targets_ref[128:, :] = spots
+
+
+def pick_kernel(targets_ref, table, kept_ref, given_ref, found_ref):
+    rows, width = table.shape
+    targets = targets_ref[...]
     step = 512
     lanes = lax.broadcasted_iota(jnp.int32, (136, 128), 1)
     total = jnp.zeros((136, width), jnp.float32)
@@ -180,16 +185,25 @@
 
 def own_picks(chosen_index, candidate_index, embeddings):
     rows, width = embeddings.shape
-    vmem = pl.BlockSpec(memory_space=pltpu.VMEM)
+    index = jnp.concatenate([chosen_index, candidate_index]).reshape(5, 128)
+    vmem = pl.BlockSpec(memory_space=pltpu.VMEM)
+    targets = pl.pallas_call(
+        functools.partial(spot_kernel, rows),
+        out_shape=jax.ShapeDtypeStruct((136, 128), jnp.int32),
+        in_specs=[vmem],
+        out_specs=vmem,
+        compiler_params=pltpu.CompilerParams(vmem_limit_bytes=8 << 20),
+        cost_estimate=pl.CostEstimate(flops=1 << 32, bytes_accessed=1 << 17, transcendentals=0),
+    )(index)
     return pl.pallas_call(
         pick_kernel,
         out_shape=[jax.ShapeDtypeStruct((64, width), jnp.bfloat16)] * 2
         + [jax.ShapeDtypeStruct((MOST, width), jnp.bfloat16)],
-        in_specs=[vmem] * 3,
+        in_specs=[vmem] * 2,
         out_specs=[vmem] * 3,
         compiler_params=pltpu.CompilerParams(vmem_limit_bytes=40 << 20),
         cost_estimate=pl.CostEstimate(flops=136 * 2048 * 768 * 2, bytes_accessed=4 << 20, transcendentals=0),
-    )(chosen_index.reshape(4, 128), candidate_index.reshape(1, 128), embeddings)
+    )(targets, embeddings)
 
 
 def local(embeddings, coverage, chosen_index, candidate_index):
@@ -213,7 +227,7 @@
     turned = turned_pieces(cands)
     part, cover = on_chip(gain_kernel, [(128, 32), (1, rows)], [], embeddings, best, other, turned, partner)
     parts = lax.all_to_all(part, CHIPS, 0, 0, tiled=True)
-    gains = lax.dynamic_slice_in_dim(jnp.sum(parts, axis=0), lax.axis_index("z") * 4, 4)
+    gains = jnp.sum(lax.dynamic_slice_in_dim(parts, lax.axis_index("z") * 4, 4, 1), axis=0)
     return cover[0], gains
 
 

time: 87.4 us -> 86.3 us (0.987)
  local copies, waits for them, and re-layouts: 3.87 us -> 1.57 us
  other arithmetic: 0.25 us -> 1.53 us
    unnamed x8 -> x4, local copies, waits for them, and re-layouts: 3.22 us -> 1.5 us
where the time goes in v7:
time: 86.3 us; the launch traced here: 86.1 us
  starting transfers between devices  28.5 us (33%)
  waiting for transfers between devices  23.9 us (28%)
  blocking collectives  20.7 us (24%)
  Pallas kernels  9.13 us (11%)
  local copies, waits for them, and re-layouts  1.57 us (2%)
  other arithmetic  1.53 us (2%)
    all_to_all x1, blocking collectives, local(): lax.all_to_all(jnp.broadcast_to(send, (8, 32 + MOST, width)), 'z', 0, 0)  20.7 us
    ppermute x9, starting transfers between devices, turn(): lax.ppermute(value, AXES, pairs_of(lambda y, x, z, c: (y, x ^ mask, z, c)...  11.4 us
    ppermute x4, starting transfers between devices, swap(): lax.ppermute(value, AXES, pairs_of(lambda y, x, z, c: (y ^ y_mask, x, z,...  11 us
    all_to_all x1, waiting for transfers between devices, local(): parts = lax.all_to_all(part, CHIPS, 0, 0, tiled=True)  10.5 us
    ppermute x9, waiting for transfers between devices, turn(): lax.ppermute(value, AXES, pairs_of(lambda y, x, z, c: (y, x ^ mask, z, c)...  8.6 us
    pallas_call x2, Pallas kernels, on_chip(): pl.pallas_call(kernel, out_shape=[jax.ShapeDtypeStruct(out, jnp.float32)...  7.78 us
    all_to_all x1, starting transfers between devices, local(): parts = lax.all_to_all(part, CHIPS, 0, 0, tiled=True)  6.06 us
    ppermute x4, waiting for transfers between devices, swap(): lax.ppermute(value, AXES, pairs_of(lambda y, x, z, c: (y ^ y_mask, x, z,...  4.78 us
  transfers between devices with their start and end apart: 14, of which 9 were waited for; matrix products, arithmetic and copies ran while one was open for 0% of the time, Pallas kernels for 5%

profile of v7, /device:TPU:1, one launch (start us, length us, event | category | flops | bytes accessed | tf_op | source)
XLA Modules:
  0.0 86.1 jit_solution(959619672119004575)
XLA Ops:
  0.6 0.7 add_bitcast_fusion.index_ref
  1.7 1.5 %copy-done = bf16[2048,768]{1,0:T(8,128)(2,1)S(1)} copy-done((bf16[2048,768]{1,0:T(8,128)(2,1)S(1)}, bf16[2048,768]{1,0:T(8,128)(2,1)}, u32[]{:S(2)}) %copy-start) | copy-done | bytes 3145752
  3.2 0.6 shard_map.60
  3.9 3.3 %collective-permute-start = (bf16[64,768]{1,0:T(8,128)(2,1)S(1)}, bf16[64,768]{1,0:T(8,128)(2,1)S(1)}, u32[]{:S(2)}, u32[]{:S(2)}) collective-permute-start(bf16[64,768]{1,0:T(8,128)(2,1)S(1)} %get-tuple-element.10), channel_id=1, source_target_pairs={{0,1},{1,0},{2,3},{3,2},{4,5},{5,4},{6,7},{7,6},{8,9},{9,8},{10,11... | collective-permute-start | bytes 294920 | tf_op jit(solution)/shard_map/ppermute | solution.py:34
  7.2 0.9 %collective-permute-done = bf16[64,768]{1,0:T(8,128)(2,1)S(1)} collective-permute-done((bf16[64,768]{1,0:T(8,128)(2,1)S(1)}, bf16[64,768]{1,0:T(8,128)(2,1)S(1)}, u32[]{:S(2)}, u32[]{:S(2)}) %collective-permute-start) | collective-permute-done | bytes 98336 | tf_op jit(solution)/shard_map/ppermute | solution.py:34
  8.6 1.2 %collective-permute-start.1 = (bf16[32,768]{1,0:T(8,128)(2,1)S(1)}, bf16[32,768]{1,0:T(8,128)(2,1)S(1)}, u32[]{:S(2)}, u32[]{:S(2)}) collective-permute-start(bf16[32,768]{1,0:T(8,128)(2,1)S(1)} %slice.13), channel_id=1, source_target_pairs={{0,16},{1,17},{2,18},{3,19},{4,20},{5,21},{6,22},{7,23},{8,24},{9,... | collective-permute-start | bytes 147464 | tf_op jit(solution)/shard_map/ppermute | solution.py:34
  9.8 3.3 %collective-permute-done.1 = bf16[32,768]{1,0:T(8,128)(2,1)S(1)} collective-permute-done((bf16[32,768]{1,0:T(8,128)(2,1)S(1)}, bf16[32,768]{1,0:T(8,128)(2,1)S(1)}, u32[]{:S(2)}, u32[]{:S(2)}) %collective-permute-start.1) | collective-permute-done | bytes 49184 | tf_op jit(solution)/shard_map/ppermute | solution.py:34
  13.1 20.7 %all_to_all.14.got_ref = bf16[8,36,768]{2,1,0:T(8,128)(2,1)S(1)} all-to-all(bf16[8,36,768]{2,1,0:T(8,128)(2,1)S(1)} %broadcast_in_dim.3), channel_id=1, replica_groups=mesh['ylo'=2,'x'=4,'yhi'=2,'z'=8,'core'=2] {'z'}, dimensions={0} | all-to-all | bytes 884736 | tf_op jit(solution)/shard_map/all_to_all | solution.py:217
  33.9 1.4 %collective-permute-start.2 = (bf16[64,768]{1,0:T(8,128)(2,1)S(1)}, bf16[64,768]{1,0:T(8,128)(2,1)S(1)}, u32[]{:S(2)}, u32[]{:S(2)}) collective-permute-start(bf16[64,768]{1,0:T(8,128)(2,1)S(1)} %shard_map.61), channel_id=1, source_target_pairs={{0,32},{1,129},{2,34},{3,131},{4,36},{5,133},{6,38},{7,135},{8,40}... | collective-permute-start | bytes 294920 | tf_op jit(solution)/shard_map/ppermute | solution.py:38
  35.3 2.6 %collective-permute-start.3 = (bf16[64,768]{1,0:T(8,128)(2,1)S(1)}, bf16[64,768]{1,0:T(8,128)(2,1)S(1)}, u32[]{:S(2)}, u32[]{:S(2)}) collective-permute-start(bf16[64,768]{1,0:T(8,128)(2,1)S(1)} %shard_map.61), channel_id=1, source_target_pairs={{0,64},{1,17},{2,66},{3,19},{4,68},{5,21},{6,70},{7,23},{8,72},{9,... | collective-permute-start | bytes 294920 | tf_op jit(solution)/shard_map/ppermute | solution.py:38
  37.9 3.0 %collective-permute-done.3 = bf16[64,768]{1,0:T(8,128)(2,1)S(1)} collective-permute-done((bf16[64,768]{1,0:T(8,128)(2,1)S(1)}, bf16[64,768]{1,0:T(8,128)(2,1)S(1)}, u32[]{:S(2)}, u32[]{:S(2)}) %collective-permute-start.3) | collective-permute-done | bytes 98336 | tf_op jit(solution)/shard_map/ppermute | solution.py:38
  41.0 1.6 %collective-permute-done.4 = bf16[64,768]{1,0:T(8,128)(2,1)S(1)} collective-permute-done((bf16[64,768]{1,0:T(8,128)(2,1)S(1)}, bf16[64,768]{1,0:T(8,128)(2,1)S(1)}, u32[]{:S(2)}, u32[]{:S(2)}) %collective-permute-start.4) | collective-permute-done | bytes 98336 | tf_op jit(solution)/shard_map/ppermute | solution.py:38
  42.7 1.4 %collective-permute-start.5 = (bf16[128,768]{1,0:T(8,128)(2,1)S(1)}, bf16[128,768]{1,0:T(8,128)(2,1)S(1)}, u32[]{:S(2)}, u32[]{:S(2)}) collective-permute-start(bf16[128,768]{1,0:T(8,128)(2,1)S(1)} %bitcast.18), channel_id=1, source_target_pairs={{0,128},{1,33},{2,130},{3,35},{4,132},{5,37},{6,134},{7,39},{8,136... | collective-permute-start | bytes 589832 | tf_op jit(solution)/shard_map/ppermute | solution.py:38
  44.1 2.6 %collective-permute-start.6 = (bf16[128,768]{1,0:T(8,128)(2,1)S(1)}, bf16[128,768]{1,0:T(8,128)(2,1)S(1)}, u32[]{:S(2)}, u32[]{:S(2)}) collective-permute-start(bf16[128,768]{1,0:T(8,128)(2,1)S(1)} %bitcast.19), channel_id=1, source_target_pairs={{0,16},{1,65},{2,18},{3,67},{4,20},{5,69},{6,22},{7,71},{8,24},{9,... | collective-permute-start | bytes 589832 | tf_op jit(solution)/shard_map/ppermute | solution.py:38
  47.3 3.3 %collective-permute-start.11 = (bf16[128,768]{1,0:T(8,128)(2,1)S(1)}, bf16[128,768]{1,0:T(8,128)(2,1)S(1)}, u32[]{:S(2)}, u32[]{:S(2)}) collective-permute-start(bf16[128,768]{1,0:T(8,128)(2,1)S(1)} %bitcast.14), channel_id=1, source_target_pairs={{0,16},{1,65},{2,18},{3,67},{4,20},{5,69},{6,22},{7,71},{8,24},{9,... | collective-permute-start | bytes 589832 | tf_op jit(solution)/shard_map/ppermute | solution.py:38
  50.6 1.4 %collective-permute-done.6.c2 = bf16[128,768]{1,0:T(8,128)(2,1)S(1)} collective-permute-done((bf16[128,768]{1,0:T(8,128)(2,1)S(1)}, bf16[128,768]{1,0:T(8,128)(2,1)S(1)}, u32[]{:S(2)}, u32[]{:S(2)}) %collective-permute-start.6) | collective-permute-done | bytes 196640 | tf_op jit(solution)/shard_map/ppermute | solution.py:38
  52.0 2.0 %collective-permute-done.7.c3 = bf16[128,768]{1,0:T(8,128)(2,1)S(1)} collective-permute-done((bf16[128,768]{1,0:T(8,128)(2,1)S(1)}, bf16[128,768]{1,0:T(8,128)(2,1)S(1)}, u32[]{:S(2)}, u32[]{:S(2)}) %collective-permute-start.7) | collective-permute-done | bytes 196640 | tf_op jit(solution)/shard_map/ppermute | solution.py:38
  54.0 3.6 %shard_map.62.best_ref = f32[2,2048]{1,0:T(2,128)S(1)} custom-call(bf16[2048,768]{1,0:T(8,128)(2,1)S(1)} %copy-done, f32[1,2048]{1,0:T(1,128)S(1)} %bitcast.22, bf16[128,768]{1,0:T(8,128)(2,1)S(1)} %bitcast.21, bf16[128,768]{1,0:T(8,128)(2,1)S(1)} %collective-permute-done.5.c1, bf16[128,768]{1,0:T(8,128)(2,1)S(1)} %collective-permute-done.6.c2, ...), custom_call_target="tpu_custom_call" | custom-call | flops 3221225472 | bytes 8388608 | tf_op jit(solution)/shard_map/pallas_call | solution.py:116
  57.7 6.1 %collective-permute-start.9 = (f32[2,2048]{1,0:T(2,128)S(1)}, f32[2,2048]{1,0:T(2,128)S(1)}, u32[]{:S(2)}, u32[]{:S(2)}) collective-permute-start(f32[2,2048]{1,0:T(2,128)S(1)} %shard_map.62.best_ref), channel_id=1, source_target_pairs={{0,1},{1,0},{2,3},{3,2},{4,5},{5,4},{6,7},{7,6},{8,9},{9,8},{10,11... | collective-permute-start | bytes 49160 | tf_op jit(solution)/shard_map/ppermute | solution.py:34
  64.0 0.6 collective-permute-done.9.other_ref
  64.6 4.1 %shard_map.64 = (f32[128,32]{1,0:T(8,128)}, f32[1,2048]{1,0:T(1,128)}) custom-call(bf16[2048,768]{1,0:T(8,128)(2,1)S(1)} %copy-done, f32[2,2048]{1,0:T(2,128)S(1)} %shard_map.62.best_ref, f32[2,2048]{1,0:T(2,128)S(1)} %collective-permute-done.9.other_ref, bf16[768,512]{1,0:T(8,128)(2,1)S(1)} %shard_map.63.turned, ...), custom_call_target="tpu_custom_call" | custom-call | flops 3221225472 | bytes 8388608 | tf_op jit(solution)/shard_map/pallas_call | solution.py:116
  68.7 6.1 %all-to-all-start.1 = ((f32[128,1,32]{2,1,0:T(1,128)}), f32[128,1,32]{2,1,0:T(1,128)S(1)}, u32[]{:S(2)}, u32[]{:S(2)}) async-start(f32[128,1,32]{2,1,0:T(1,128)} %bitcast.10), calls=%async_computation.1 | async-start | bytes 131072 | tf_op jit(solution)/shard_map/all_to_all | solution.py:229
  74.8 10.5 %all-to-all-done.1 = f32[128,1,32]{2,1,0:T(1,128)S(1)} async-done(((f32[128,1,32]{2,1,0:T(1,128)}), f32[128,1,32]{2,1,0:T(1,128)S(1)}, u32[]{:S(2)}, u32[]{:S(2)}) %all-to-all-start.1) | async-done | bytes 16416 | tf_op jit(solution)/shard_map/all_to_all | solution.py:229
  85.4 0.7 dynamic-slice_reduce_fusion
  (24 shorter events, 1.9 us)
Async XLA Ops:
  1.3 1.9 %copy-start = (bf16[2048,768]{1,0:T(8,128)(2,1)S(1)}, bf16[2048,768]{1,0:T(8,128)(2,1)}, u32[]{:S(2)}) copy-start(bf16[2048,768]{1,0:T(8,128)(2,1)} %own_ref.3) | copy-start | bytes 9437188
  3.2 50.8 %copy-start.1 = (f32[2048]{0:T(1024)S(1)}, f32[2048]{0:T(1024)}, u32[]{:S(2)}) copy-start(f32[2048]{0:T(1024)} %param.5) | copy-start | bytes 24580
  3.9 4.3 %collective-permute-start = (bf16[64,768]{1,0:T(8,128)(2,1)S(1)}, bf16[64,768]{1,0:T(8,128)(2,1)S(1)}, u32[]{:S(2)}, u32[]{:S(2)}) collective-permute-start(bf16[64,768]{1,0:T(8,128)(2,1)S(1)} %get-tuple-element.10), channel_id=1, source_target_pairs={{0,1},{1,0},{2,3},{3,2},{4,5},{5,4},{6,7},{7,6},{8,9},{9,8},{10,11... | collective-permute-start | bytes 294920 | tf_op jit(solution)/shard_map/ppermute | solution.py:34
  8.2 45.8 %collective-permute-start.8 = (bf16[2048,768]{1,0:T(8,128)(2,1)S(1)}, bf16[2048,768]{1,0:T(8,128)(2,1)S(1)}, u32[]{:S(2)}, u32[]{:S(2)}) collective-permute-start(bf16[2048,768]{1,0:T(8,128)(2,1)S(1)} %copy-done), channel_id=1, source_target_pairs={{0,1},{1,0},{2,3},{3,2},{4,5},{5,4},{6,7},{7,6},{8,9},{9,8},{10,11... | collective-permute-start | bytes 9437192 | tf_op jit(solution)/shard_map/ppermute | solution.py:34
  8.6 4.4 %collective-permute-start.1 = (bf16[32,768]{1,0:T(8,128)(2,1)S(1)}, bf16[32,768]{1,0:T(8,128)(2,1)S(1)}, u32[]{:S(2)}, u32[]{:S(2)}) collective-permute-start(bf16[32,768]{1,0:T(8,128)(2,1)S(1)} %slice.13), channel_id=1, source_target_pairs={{0,16},{1,17},{2,18},{3,19},{4,20},{5,21},{6,22},{7,23},{8,24},{9,... | collective-permute-start | bytes 147464 | tf_op jit(solution)/shard_map/ppermute | solution.py:34
  33.9 4.0 %collective-permute-start.2 = (bf16[64,768]{1,0:T(8,128)(2,1)S(1)}, bf16[64,768]{1,0:T(8,128)(2,1)S(1)}, u32[]{:S(2)}, u32[]{:S(2)}) collective-permute-start(bf16[64,768]{1,0:T(8,128)(2,1)S(1)} %shard_map.61), channel_id=1, source_target_pairs={{0,32},{1,129},{2,34},{3,131},{4,36},{5,133},{6,38},{7,135},{8,40}... | collective-permute-start | bytes 294920 | tf_op jit(solution)/shard_map/ppermute | solution.py:38
  35.3 5.7 %collective-permute-start.3 = (bf16[64,768]{1,0:T(8,128)(2,1)S(1)}, bf16[64,768]{1,0:T(8,128)(2,1)S(1)}, u32[]{:S(2)}, u32[]{:S(2)}) collective-permute-start(bf16[64,768]{1,0:T(8,128)(2,1)S(1)} %shard_map.61), channel_id=1, source_target_pairs={{0,64},{1,17},{2,66},{3,19},{4,68},{5,21},{6,70},{7,23},{8,72},{9,... | collective-permute-start | bytes 294920 | tf_op jit(solution)/shard_map/ppermute | solution.py:38
  37.9 4.7 %collective-permute-start.4 = (bf16[64,768]{1,0:T(8,128)(2,1)S(1)}, bf16[64,768]{1,0:T(8,128)(2,1)S(1)}, u32[]{:S(2)}, u32[]{:S(2)}) collective-permute-start(bf16[64,768]{1,0:T(8,128)(2,1)S(1)} %shard_map.61), channel_id=1, source_target_pairs={{0,96},{1,145},{2,98},{3,147},{4,100},{5,149},{6,102},{7,151},{8,1... | collective-permute-start | bytes 294920 | tf_op jit(solution)/shard_map/ppermute | solution.py:38
  42.7 4.6 %collective-permute-start.5 = (bf16[128,768]{1,0:T(8,128)(2,1)S(1)}, bf16[128,768]{1,0:T(8,128)(2,1)S(1)}, u32[]{:S(2)}, u32[]{:S(2)}) collective-permute-start(bf16[128,768]{1,0:T(8,128)(2,1)S(1)} %bitcast.18), channel_id=1, source_target_pairs={{0,128},{1,33},{2,130},{3,35},{4,132},{5,37},{6,134},{7,39},{8,136... | collective-permute-start | bytes 589832 | tf_op jit(solution)/shard_map/ppermute | solution.py:38
  44.1 7.9 %collective-permute-start.6 = (bf16[128,768]{1,0:T(8,128)(2,1)S(1)}, bf16[128,768]{1,0:T(8,128)(2,1)S(1)}, u32[]{:S(2)}, u32[]{:S(2)}) collective-permute-start(bf16[128,768]{1,0:T(8,128)(2,1)S(1)} %bitcast.19), channel_id=1, source_target_pairs={{0,16},{1,65},{2,18},{3,67},{4,20},{5,69},{6,22},{7,71},{8,24},{9,... | collective-permute-start | bytes 589832 | tf_op jit(solution)/shard_map/ppermute | solution.py:38
  46.7 7.3 %collective-permute-start.7 = (bf16[128,768]{1,0:T(8,128)(2,1)S(1)}, bf16[128,768]{1,0:T(8,128)(2,1)S(1)}, u32[]{:S(2)}, u32[]{:S(2)}) collective-permute-start(bf16[128,768]{1,0:T(8,128)(2,1)S(1)} %bitcast.20), channel_id=1, source_target_pairs={{0,144},{1,97},{2,146},{3,99},{4,148},{5,101},{6,150},{7,103},{8,1... | collective-permute-start | bytes 589832 | tf_op jit(solution)/shard_map/ppermute | solution.py:38
  46.8 17.0 %collective-permute-start.10 = (bf16[128,768]{1,0:T(8,128)(2,1)S(1)}, bf16[128,768]{1,0:T(8,128)(2,1)S(1)}, u32[]{:S(2)}, u32[]{:S(2)}) collective-permute-start(bf16[128,768]{1,0:T(8,128)(2,1)S(1)} %bitcast.13), channel_id=1, source_target_pairs={{0,128},{1,33},{2,130},{3,35},{4,132},{5,37},{6,134},{7,39},{8,136... | collective-permute-start | bytes 589832 | tf_op jit(solution)/shard_map/ppermute | solution.py:38
  47.3 16.4 %collective-permute-start.11 = (bf16[128,768]{1,0:T(8,128)(2,1)S(1)}, bf16[128,768]{1,0:T(8,128)(2,1)S(1)}, u32[]{:S(2)}, u32[]{:S(2)}) collective-permute-start(bf16[128,768]{1,0:T(8,128)(2,1)S(1)} %bitcast.14), channel_id=1, source_target_pairs={{0,16},{1,65},{2,18},{3,67},{4,20},{5,69},{6,22},{7,71},{8,24},{9,... | collective-permute-start | bytes 589832 | tf_op jit(solution)/shard_map/ppermute | solution.py:38
  52.0 11.8 %collective-permute-start.12 = (bf16[128,768]{1,0:T(8,128)(2,1)S(1)}, bf16[128,768]{1,0:T(8,128)(2,1)S(1)}, u32[]{:S(2)}, u32[]{:S(2)}) collective-permute-start(bf16[128,768]{1,0:T(8,128)(2,1)S(1)} %bitcast.15), channel_id=1, source_target_pairs={{0,144},{1,97},{2,146},{3,99},{4,148},{5,101},{6,150},{7,103},{8,1... | collective-permute-start | bytes 589832 | tf_op jit(solution)/shard_map/ppermute | solution.py:38
  57.7 6.9 %collective-permute-start.9 = (f32[2,2048]{1,0:T(2,128)S(1)}, f32[2,2048]{1,0:T(2,128)S(1)}, u32[]{:S(2)}, u32[]{:S(2)}) collective-permute-start(f32[2,2048]{1,0:T(2,128)S(1)} %shard_map.62.best_ref), channel_id=1, source_target_pairs={{0,1},{1,0},{2,3},{3,2},{4,5},{5,4},{6,7},{7,6},{8,9},{9,8},{10,11... | collective-permute-start | bytes 49160 | tf_op jit(solution)/shard_map/ppermute | solution.py:34
  68.7 16.6 %all-to-all-start.1 = ((f32[128,1,32]{2,1,0:T(1,128)}), f32[128,1,32]{2,1,0:T(1,128)S(1)}, u32[]{:S(2)}, u32[]{:S(2)}) async-start(f32[128,1,32]{2,1,0:T(1,128)} %bitcast.10), calls=%async_computation.1 | async-start | bytes 131072 | tf_op jit(solution)/shard_map/all_to_all | solution.py:229

commit v8 on v7

--- a/solution.py
+++ b/solution.py
@@ -67,19 +67,19 @@
     )(*pieces)
 
 
-def best_kernel(own_ref, coverage_ref, c0, c1, c2, c3, partner_ref, best_ref, turned):
+def best_kernel(own_ref, floor_ref, c0, c1, partner_ref, best_ref, turned):
     rows, width = own_ref.shape
     scale = 1.0 / width**0.5
-    turned_table((c0, c1, c2, c3), turned)
+    turned_table((c0, c1), turned)
     for t, table in enumerate((own_ref, partner_ref)):
         for start in range(0, rows, STEP):
             sims = tile_sims(table, turned, start)
-            top = functools.reduce(jnp.maximum, [sims[:, l : l + 128] for l in range(0, 512, 128)])
+            top = functools.reduce(jnp.maximum, [sims[:, l : l + 128] for l in range(0, 256, 128)])
             for r in range(0, STEP, 128):
                 here = pl.ds(start + r, 128)
                 row = jnp.max(top[r : r + 128].T, axis=0, keepdims=True) * scale
-                if t == 0:
-                    row = jnp.maximum(row, coverage_ref[:, here])
+                if t < floor_ref.shape[0]:
+                    row = jnp.maximum(row, floor_ref[t : t + 1, here])
                 best_ref[t : t + 1, here] = row
 
 
@@ -111,7 +111,7 @@
             gain_ref[pl.ds(at * 8, 8), :] = jnp.broadcast_to(sums[:, lane : lane + 32], (8, 32))
 
 
-def on_chip(kernel, outs, scratch, *operands):
+def on_chip(kernel, outs, scratch, pieces, *operands):
     vmem = pl.BlockSpec(memory_space=pltpu.VMEM)
     return pl.pallas_call(
         kernel,
@@ -120,7 +120,7 @@
         out_specs=[vmem] * len(outs),
         scratch_shapes=scratch,
         compiler_params=pltpu.CompilerParams(vmem_limit_bytes=16 << 20),
-        cost_estimate=pl.CostEstimate(flops=4096 * 512 * 768 * 2, bytes_accessed=8 << 20, transcendentals=0),
+        cost_estimate=pl.CostEstimate(flops=4096 * 128 * 768 * 2 * pieces, bytes_accessed=8 << 20, transcendentals=0),
     )(*operands)
 
 
@@ -221,11 +221,13 @@
     chosen = [chosen] + [turn(chosen, s, False) for s in (1, 2, 3)]
     cands = [cands] + [turn(cands, s, False) for s in (1, 2, 3)]
 
-    table = [pltpu.VMEM((width, 512), jnp.bfloat16)]
-    best = on_chip(best_kernel, [(2, rows)], table, embeddings, coverage.reshape(1, rows), *chosen, partner)[0]
+    table = [pltpu.VMEM((width, 256), jnp.bfloat16)]
+    best = coverage.reshape(1, rows)
+    for pieces in (chosen[:2], chosen[2:]):
+        best = on_chip(best_kernel, [(2, rows)], table, 2, embeddings, best, *pieces, partner)[0]
     other = swap(best, 0, 1)
     turned = turned_pieces(cands)
-    part, cover = on_chip(gain_kernel, [(128, 32), (1, rows)], [], embeddings, best, other, turned, partner)
+    part, cover = on_chip(gain_kernel, [(128, 32), (1, rows)], [], 4, embeddings, best, other, turned, partner)
     parts = lax.all_to_all(part, CHIPS, 0, 0, tiled=True)
     gains = jnp.sum(lax.dynamic_slice_in_dim(parts, lax.axis_index("z") * 4, 4, 1), axis=0)
     return cover[0], gains

time: 86.3 us -> 85 us (0.985)
  waiting for transfers between devices: 23.9 us -> 21.5 us
    ppermute x9, waiting for transfers between devices: 8.6 us -> 6.15 us  [turn(): lax.ppermute(value, AXES, pairs_of(lambda y, x, z, c: (y, x ^ mask, z, c)...]
    pallas_call x2 -> x3, Pallas kernels: 7.78 us -> 8.14 us  [on_chip(): pl.pallas_call(kernel, out_shape=[jax.ShapeDtypeStruct(out, jnp.float32)...]
  transfers between devices with their start and end apart: 14 -> 14, of which waited for: 9 -> 8; matrix products, arithmetic and copies ran while one was open for 0% -> 0% of each run, Pallas kernels for 5% -> 5%
where the time goes in v8:
time: 85 us; the launch traced here: 84.5 us
  starting transfers between devices  28.9 us (34%)
  waiting for transfers between devices  21.5 us (25%)
  blocking collectives  20.7 us (24%)
  Pallas kernels  9.48 us (11%)
  local copies, waits for them, and re-layouts  1.57 us (2%)
  other arithmetic  1.53 us (2%)
    all_to_all x1, blocking collectives, local(): lax.all_to_all(jnp.broadcast_to(send, (8, 32 + MOST, width)), 'z', 0, 0)  20.7 us
    ppermute x9, starting transfers between devices, turn(): lax.ppermute(value, AXES, pairs_of(lambda y, x, z, c: (y, x ^ mask, z, c)...  11.8 us
    ppermute x4, starting transfers between devices, swap(): lax.ppermute(value, AXES, pairs_of(lambda y, x, z, c: (y ^ y_mask, x, z,...  11 us
    all_to_all x1, waiting for transfers between devices, local(): parts = lax.all_to_all(part, CHIPS, 0, 0, tiled=True)  10.6 us
    pallas_call x3, Pallas kernels, on_chip(): pl.pallas_call(kernel, out_shape=[jax.ShapeDtypeStruct(out, jnp.float32)...  8.14 us
    ppermute x9, waiting for transfers between devices, turn(): lax.ppermute(value, AXES, pairs_of(lambda y, x, z, c: (y, x ^ mask, z, c)...  6.15 us
    all_to_all x1, starting transfers between devices, local(): parts = lax.all_to_all(part, CHIPS, 0, 0, tiled=True)  6.06 us
    ppermute x4, waiting for transfers between devices, swap(): lax.ppermute(value, AXES, pairs_of(lambda y, x, z, c: (y ^ y_mask, x, z,...  4.78 us
  transfers between devices with their start and end apart: 14, of which 8 were waited for; matrix products, arithmetic and copies ran while one was open for 0% of the time, Pallas kernels for 5%

profile of v8, /device:TPU:1, one launch (start us, length us, event | category | flops | bytes accessed | tf_op | source)
XLA Modules:
  0.0 84.5 jit_solution(10547373578687640601)
XLA Ops:
  0.6 0.7 add_bitcast_fusion.index_ref
  1.7 1.5 %copy-done = bf16[2048,768]{1,0:T(8,128)(2,1)S(1)} copy-done((bf16[2048,768]{1,0:T(8,128)(2,1)S(1)}, bf16[2048,768]{1,0:T(8,128)(2,1)}, u32[]{:S(2)}) %copy-start) | copy-done | bytes 3145752
  3.2 0.6 shard_map.60
  3.9 3.3 %collective-permute-start = (bf16[64,768]{1,0:T(8,128)(2,1)S(1)}, bf16[64,768]{1,0:T(8,128)(2,1)S(1)}, u32[]{:S(2)}, u32[]{:S(2)}) collective-permute-start(bf16[64,768]{1,0:T(8,128)(2,1)S(1)} %get-tuple-element.10), channel_id=1, source_target_pairs={{0,1},{1,0},{2,3},{3,2},{4,5},{5,4},{6,7},{7,6},{8,9},{9,8},{10,11... | collective-permute-start | bytes 294920 | tf_op jit(solution)/shard_map/ppermute | solution.py:34
  7.2 0.9 %collective-permute-done = bf16[64,768]{1,0:T(8,128)(2,1)S(1)} collective-permute-done((bf16[64,768]{1,0:T(8,128)(2,1)S(1)}, bf16[64,768]{1,0:T(8,128)(2,1)S(1)}, u32[]{:S(2)}, u32[]{:S(2)}) %collective-permute-start) | collective-permute-done | bytes 98336 | tf_op jit(solution)/shard_map/ppermute | solution.py:34
  8.6 1.2 %collective-permute-start.1 = (bf16[32,768]{1,0:T(8,128)(2,1)S(1)}, bf16[32,768]{1,0:T(8,128)(2,1)S(1)}, u32[]{:S(2)}, u32[]{:S(2)}) collective-permute-start(bf16[32,768]{1,0:T(8,128)(2,1)S(1)} %slice.13), channel_id=1, source_target_pairs={{0,16},{1,17},{2,18},{3,19},{4,20},{5,21},{6,22},{7,23},{8,24},{9,... | collective-permute-start | bytes 147464 | tf_op jit(solution)/shard_map/ppermute | solution.py:34
  9.8 3.3 %collective-permute-done.1 = bf16[32,768]{1,0:T(8,128)(2,1)S(1)} collective-permute-done((bf16[32,768]{1,0:T(8,128)(2,1)S(1)}, bf16[32,768]{1,0:T(8,128)(2,1)S(1)}, u32[]{:S(2)}, u32[]{:S(2)}) %collective-permute-start.1) | collective-permute-done | bytes 49184 | tf_op jit(solution)/shard_map/ppermute | solution.py:34
  13.1 20.7 %all_to_all.14.got_ref = bf16[8,36,768]{2,1,0:T(8,128)(2,1)S(1)} all-to-all(bf16[8,36,768]{2,1,0:T(8,128)(2,1)S(1)} %broadcast_in_dim.3), channel_id=1, replica_groups=mesh['ylo'=2,'x'=4,'yhi'=2,'z'=8,'core'=2] {'z'}, dimensions={0} | all-to-all | bytes 884736 | tf_op jit(solution)/shard_map/all_to_all | solution.py:217
  33.9 1.4 %collective-permute-start.2 = (bf16[64,768]{1,0:T(8,128)(2,1)S(1)}, bf16[64,768]{1,0:T(8,128)(2,1)S(1)}, u32[]{:S(2)}, u32[]{:S(2)}) collective-permute-start(bf16[64,768]{1,0:T(8,128)(2,1)S(1)} %shard_map.61), channel_id=1, source_target_pairs={{0,32},{1,129},{2,34},{3,131},{4,36},{5,133},{6,38},{7,135},{8,40}... | collective-permute-start | bytes 294920 | tf_op jit(solution)/shard_map/ppermute | solution.py:38
  35.3 2.6 %collective-permute-start.3 = (bf16[64,768]{1,0:T(8,128)(2,1)S(1)}, bf16[64,768]{1,0:T(8,128)(2,1)S(1)}, u32[]{:S(2)}, u32[]{:S(2)}) collective-permute-start(bf16[64,768]{1,0:T(8,128)(2,1)S(1)} %shard_map.61), channel_id=1, source_target_pairs={{0,64},{1,17},{2,66},{3,19},{4,68},{5,21},{6,70},{7,23},{8,72},{9,... | collective-permute-start | bytes 294920 | tf_op jit(solution)/shard_map/ppermute | solution.py:38
  37.9 3.0 %collective-permute-done.3 = bf16[64,768]{1,0:T(8,128)(2,1)S(1)} collective-permute-done((bf16[64,768]{1,0:T(8,128)(2,1)S(1)}, bf16[64,768]{1,0:T(8,128)(2,1)S(1)}, u32[]{:S(2)}, u32[]{:S(2)}) %collective-permute-start.3) | collective-permute-done | bytes 98336 | tf_op jit(solution)/shard_map/ppermute | solution.py:38
  41.0 1.6 %collective-permute-done.4 = bf16[64,768]{1,0:T(8,128)(2,1)S(1)} collective-permute-done((bf16[64,768]{1,0:T(8,128)(2,1)S(1)}, bf16[64,768]{1,0:T(8,128)(2,1)S(1)}, u32[]{:S(2)}, u32[]{:S(2)}) %collective-permute-start.4) | collective-permute-done | bytes 98336 | tf_op jit(solution)/shard_map/ppermute | solution.py:38
  42.7 1.4 %collective-permute-start.5 = (bf16[128,768]{1,0:T(8,128)(2,1)S(1)}, bf16[128,768]{1,0:T(8,128)(2,1)S(1)}, u32[]{:S(2)}, u32[]{:S(2)}) collective-permute-start(bf16[128,768]{1,0:T(8,128)(2,1)S(1)} %bitcast.13), channel_id=1, source_target_pairs={{0,128},{1,33},{2,130},{3,35},{4,132},{5,37},{6,134},{7,39},{8,136... | collective-permute-start | bytes 589832 | tf_op jit(solution)/shard_map/ppermute | solution.py:38
  44.1 2.6 %collective-permute-start.7 = (bf16[128,768]{1,0:T(8,128)(2,1)S(1)}, bf16[128,768]{1,0:T(8,128)(2,1)S(1)}, u32[]{:S(2)}, u32[]{:S(2)}) collective-permute-start(bf16[128,768]{1,0:T(8,128)(2,1)S(1)} %bitcast.14), channel_id=1, source_target_pairs={{0,16},{1,65},{2,18},{3,67},{4,20},{5,69},{6,22},{7,71},{8,24},{9,... | collective-permute-start | bytes 589832 | tf_op jit(solution)/shard_map/ppermute | solution.py:38
  47.3 3.3 %collective-permute-start.11 = (bf16[128,768]{1,0:T(8,128)(2,1)S(1)}, bf16[128,768]{1,0:T(8,128)(2,1)S(1)}, u32[]{:S(2)}, u32[]{:S(2)}) collective-permute-start(bf16[128,768]{1,0:T(8,128)(2,1)S(1)} %bitcast.18), channel_id=1, source_target_pairs={{0,16},{1,65},{2,18},{3,67},{4,20},{5,69},{6,22},{7,71},{8,24},{9,... | collective-permute-start | bytes 589832 | tf_op jit(solution)/shard_map/ppermute | solution.py:38
  51.1 2.0 %shard_map.62.floor_ref = f32[2,2048]{1,0:T(2,128)S(1)} custom-call(bf16[2048,768]{1,0:T(8,128)(2,1)S(1)} %copy-done, f32[1,2048]{1,0:T(1,128)S(1)} %bitcast.22, bf16[128,768]{1,0:T(8,128)(2,1)S(1)} %bitcast.16, bf16[128,768]{1,0:T(8,128)(2,1)S(1)} %collective-permute-done.5.c1, bf16[2048,768]{1,0:T(8,128)(2,1)S(1)} %collective-permute-done.6.partner_ref), custom_call_target="tpu_custom_call" | custom-call | flops 1610612736 | bytes 8388608 | tf_op jit(solution)/shard_map/pallas_call | solution.py:116
  53.1 0.9 %collective-permute-done.8.c1 = bf16[128,768]{1,0:T(8,128)(2,1)S(1)} collective-permute-done((bf16[128,768]{1,0:T(8,128)(2,1)S(1)}, bf16[128,768]{1,0:T(8,128)(2,1)S(1)}, u32[]{:S(2)}, u32[]{:S(2)}) %collective-permute-start.8) | collective-permute-done | bytes 196640 | tf_op jit(solution)/shard_map/ppermute | solution.py:38
  54.0 2.0 %shard_map.63.best_ref = f32[2,2048]{1,0:T(2,128)S(1)} custom-call(bf16[2048,768]{1,0:T(8,128)(2,1)S(1)} %copy-done, f32[2,2048]{1,0:T(2,128)S(1)} %shard_map.62.floor_ref, bf16[128,768]{1,0:T(8,128)(2,1)S(1)} %collective-permute-done.7.c0, bf16[128,768]{1,0:T(8,128)(2,1)S(1)} %collective-permute-done.8.c1, ...), custom_call_target="tpu_custom_call" | custom-call | flops 1610612736 | bytes 8388608 | tf_op jit(solution)/shard_map/pallas_call | solution.py:116
  56.0 6.1 %collective-permute-start.9 = (f32[2,2048]{1,0:T(2,128)S(1)}, f32[2,2048]{1,0:T(2,128)S(1)}, u32[]{:S(2)}, u32[]{:S(2)}) collective-permute-start(f32[2,2048]{1,0:T(2,128)S(1)} %shard_map.63.best_ref), channel_id=1, source_target_pairs={{0,1},{1,0},{2,3},{3,2},{4,5},{5,4},{6,7},{7,6},{8,9},{9,8},{10,11... | collective-permute-start | bytes 49160 | tf_op jit(solution)/shard_map/ppermute | solution.py:34
  62.4 0.6 collective-permute-done.9.other_ref
  62.9 4.1 %shard_map.65 = (f32[128,32]{1,0:T(8,128)}, f32[1,2048]{1,0:T(1,128)}) custom-call(bf16[2048,768]{1,0:T(8,128)(2,1)S(1)} %copy-done, f32[2,2048]{1,0:T(2,128)S(1)} %shard_map.63.best_ref, f32[2,2048]{1,0:T(2,128)S(1)} %collective-permute-done.9.other_ref, bf16[768,512]{1,0:T(8,128)(2,1)S(1)} %shard_map.64.turned, ...), custom_call_target="tpu_custom_call" | custom-call | flops 3221225472 | bytes 8388608 | tf_op jit(solution)/shard_map/pallas_call | solution.py:116
  67.1 6.1 %all-to-all-start.1 = ((f32[128,1,32]{2,1,0:T(1,128)}), f32[128,1,32]{2,1,0:T(1,128)S(1)}, u32[]{:S(2)}, u32[]{:S(2)}) async-start(f32[128,1,32]{2,1,0:T(1,128)} %bitcast.10), calls=%async_computation.1 | async-start | bytes 131072 | tf_op jit(solution)/shard_map/all_to_all | solution.py:231
  73.2 10.6 %all-to-all-done.1 = f32[128,1,32]{2,1,0:T(1,128)S(1)} async-done(((f32[128,1,32]{2,1,0:T(1,128)}), f32[128,1,32]{2,1,0:T(1,128)S(1)}, u32[]{:S(2)}, u32[]{:S(2)}) %all-to-all-start.1) | async-done | bytes 16416 | tf_op jit(solution)/shard_map/all_to_all | solution.py:231
  83.7 0.7 dynamic-slice_reduce_fusion
  (25 shorter events, 2.3 us)
Async XLA Ops:
  1.3 1.9 %copy-start = (bf16[2048,768]{1,0:T(8,128)(2,1)S(1)}, bf16[2048,768]{1,0:T(8,128)(2,1)}, u32[]{:S(2)}) copy-start(bf16[2048,768]{1,0:T(8,128)(2,1)} %own_ref.5) | copy-start | bytes 9437188
  3.2 47.8 %copy-start.1 = (f32[2048]{0:T(1024)S(1)}, f32[2048]{0:T(1024)}, u32[]{:S(2)}) copy-start(f32[2048]{0:T(1024)} %param.5) | copy-start | bytes 24580
  3.9 4.3 %collective-permute-start = (bf16[64,768]{1,0:T(8,128)(2,1)S(1)}, bf16[64,768]{1,0:T(8,128)(2,1)S(1)}, u32[]{:S(2)}, u32[]{:S(2)}) collective-permute-start(bf16[64,768]{1,0:T(8,128)(2,1)S(1)} %get-tuple-element.10), channel_id=1, source_target_pairs={{0,1},{1,0},{2,3},{3,2},{4,5},{5,4},{6,7},{7,6},{8,9},{9,8},{10,11... | collective-permute-start | bytes 294920 | tf_op jit(solution)/shard_map/ppermute | solution.py:34
  8.2 42.4 %collective-permute-start.6 = (bf16[2048,768]{1,0:T(8,128)(2,1)S(1)}, bf16[2048,768]{1,0:T(8,128)(2,1)S(1)}, u32[]{:S(2)}, u32[]{:S(2)}) collective-permute-start(bf16[2048,768]{1,0:T(8,128)(2,1)S(1)} %copy-done), channel_id=1, source_target_pairs={{0,1},{1,0},{2,3},{3,2},{4,5},{5,4},{6,7},{7,6},{8,9},{9,8},{10,11... | collective-permute-start | bytes 9437192 | tf_op jit(solution)/shard_map/ppermute | solution.py:34
  8.6 4.4 %collective-permute-start.1 = (bf16[32,768]{1,0:T(8,128)(2,1)S(1)}, bf16[32,768]{1,0:T(8,128)(2,1)S(1)}, u32[]{:S(2)}, u32[]{:S(2)}) collective-permute-start(bf16[32,768]{1,0:T(8,128)(2,1)S(1)} %slice.13), channel_id=1, source_target_pairs={{0,16},{1,17},{2,18},{3,19},{4,20},{5,21},{6,22},{7,23},{8,24},{9,... | collective-permute-start | bytes 147464 | tf_op jit(solution)/shard_map/ppermute | solution.py:34
  33.9 4.0 %collective-permute-start.2 = (bf16[64,768]{1,0:T(8,128)(2,1)S(1)}, bf16[64,768]{1,0:T(8,128)(2,1)S(1)}, u32[]{:S(2)}, u32[]{:S(2)}) collective-permute-start(bf16[64,768]{1,0:T(8,128)(2,1)S(1)} %shard_map.61), channel_id=1, source_target_pairs={{0,32},{1,129},{2,34},{3,131},{4,36},{5,133},{6,38},{7,135},{8,40}... | collective-permute-start | bytes 294920 | tf_op jit(solution)/shard_map/ppermute | solution.py:38
  35.3 5.7 %collective-permute-start.3 = (bf16[64,768]{1,0:T(8,128)(2,1)S(1)}, bf16[64,768]{1,0:T(8,128)(2,1)S(1)}, u32[]{:S(2)}, u32[]{:S(2)}) collective-permute-start(bf16[64,768]{1,0:T(8,128)(2,1)S(1)} %shard_map.61), channel_id=1, source_target_pairs={{0,64},{1,17},{2,66},{3,19},{4,68},{5,21},{6,70},{7,23},{8,72},{9,... | collective-permute-start | bytes 294920 | tf_op jit(solution)/shard_map/ppermute | solution.py:38
  37.9 4.7 %collective-permute-start.4 = (bf16[64,768]{1,0:T(8,128)(2,1)S(1)}, bf16[64,768]{1,0:T(8,128)(2,1)S(1)}, u32[]{:S(2)}, u32[]{:S(2)}) collective-permute-start(bf16[64,768]{1,0:T(8,128)(2,1)S(1)} %shard_map.61), channel_id=1, source_target_pairs={{0,96},{1,145},{2,98},{3,147},{4,100},{5,149},{6,102},{7,151},{8,1... | collective-permute-start | bytes 294920 | tf_op jit(solution)/shard_map/ppermute | solution.py:38
  42.7 4.6 %collective-permute-start.5 = (bf16[128,768]{1,0:T(8,128)(2,1)S(1)}, bf16[128,768]{1,0:T(8,128)(2,1)S(1)}, u32[]{:S(2)}, u32[]{:S(2)}) collective-permute-start(bf16[128,768]{1,0:T(8,128)(2,1)S(1)} %bitcast.13), channel_id=1, source_target_pairs={{0,128},{1,33},{2,130},{3,35},{4,132},{5,37},{6,134},{7,39},{8,136... | collective-permute-start | bytes 589832 | tf_op jit(solution)/shard_map/ppermute | solution.py:38
  44.1 8.9 %collective-permute-start.7 = (bf16[128,768]{1,0:T(8,128)(2,1)S(1)}, bf16[128,768]{1,0:T(8,128)(2,1)S(1)}, u32[]{:S(2)}, u32[]{:S(2)}) collective-permute-start(bf16[128,768]{1,0:T(8,128)(2,1)S(1)} %bitcast.14), channel_id=1, source_target_pairs={{0,16},{1,65},{2,18},{3,67},{4,20},{5,69},{6,22},{7,71},{8,24},{9,... | collective-permute-start | bytes 589832 | tf_op jit(solution)/shard_map/ppermute | solution.py:38
  46.7 7.3 %collective-permute-start.8 = (bf16[128,768]{1,0:T(8,128)(2,1)S(1)}, bf16[128,768]{1,0:T(8,128)(2,1)S(1)}, u32[]{:S(2)}, u32[]{:S(2)}) collective-permute-start(bf16[128,768]{1,0:T(8,128)(2,1)S(1)} %bitcast.15), channel_id=1, source_target_pairs={{0,144},{1,97},{2,146},{3,99},{4,148},{5,101},{6,150},{7,103},{8,1... | collective-permute-start | bytes 589832 | tf_op jit(solution)/shard_map/ppermute | solution.py:38
  46.8 15.4 %collective-permute-start.10 = (bf16[128,768]{1,0:T(8,128)(2,1)S(1)}, bf16[128,768]{1,0:T(8,128)(2,1)S(1)}, u32[]{:S(2)}, u32[]{:S(2)}) collective-permute-start(bf16[128,768]{1,0:T(8,128)(2,1)S(1)} %bitcast.17), channel_id=1, source_target_pairs={{0,128},{1,33},{2,130},{3,35},{4,132},{5,37},{6,134},{7,39},{8,136... | collective-permute-start | bytes 589832 | tf_op jit(solution)/shard_map/ppermute | solution.py:38
  47.3 14.8 %collective-permute-start.11 = (bf16[128,768]{1,0:T(8,128)(2,1)S(1)}, bf16[128,768]{1,0:T(8,128)(2,1)S(1)}, u32[]{:S(2)}, u32[]{:S(2)}) collective-permute-start(bf16[128,768]{1,0:T(8,128)(2,1)S(1)} %bitcast.18), channel_id=1, source_target_pairs={{0,16},{1,65},{2,18},{3,67},{4,20},{5,69},{6,22},{7,71},{8,24},{9,... | collective-permute-start | bytes 589832 | tf_op jit(solution)/shard_map/ppermute | solution.py:38
  50.6 11.5 %collective-permute-start.12 = (bf16[128,768]{1,0:T(8,128)(2,1)S(1)}, bf16[128,768]{1,0:T(8,128)(2,1)S(1)}, u32[]{:S(2)}, u32[]{:S(2)}) collective-permute-start(bf16[128,768]{1,0:T(8,128)(2,1)S(1)} %bitcast.19), channel_id=1, source_target_pairs={{0,144},{1,97},{2,146},{3,99},{4,148},{5,101},{6,150},{7,103},{8,1... | collective-permute-start | bytes 589832 | tf_op jit(solution)/shard_map/ppermute | solution.py:38
  56.0 6.9 %collective-permute-start.9 = (f32[2,2048]{1,0:T(2,128)S(1)}, f32[2,2048]{1,0:T(2,128)S(1)}, u32[]{:S(2)}, u32[]{:S(2)}) collective-permute-start(f32[2,2048]{1,0:T(2,128)S(1)} %shard_map.63.best_ref), channel_id=1, source_target_pairs={{0,1},{1,0},{2,3},{3,2},{4,5},{5,4},{6,7},{7,6},{8,9},{9,8},{10,11... | collective-permute-start | bytes 49160 | tf_op jit(solution)/shard_map/ppermute | solution.py:34
  67.1 16.6 %all-to-all-start.1 = ((f32[128,1,32]{2,1,0:T(1,128)}), f32[128,1,32]{2,1,0:T(1,128)S(1)}, u32[]{:S(2)}, u32[]{:S(2)}) async-start(f32[128,1,32]{2,1,0:T(1,128)} %bitcast.10), calls=%async_computation.1 | async-start | bytes 131072 | tf_op jit(solution)/shard_map/all_to_all | solution.py:231

commit v9 on v8

--- a/solution.py
+++ b/solution.py
@@ -49,22 +49,6 @@
 
 def tile_sims(table, turned, start):
     return jnp.dot(table[pl.ds(start, STEP), :], turned[...], preferred_element_type=jnp.float32)
-
-
-def turn_kernel(c0, c1, c2, c3, turned):
-    turned_table((c0, c1, c2, c3), turned)
-
-
-def turned_pieces(pieces):
-    vmem = pl.BlockSpec(memory_space=pltpu.VMEM)
-    return pl.pallas_call(
-        turn_kernel,
-        out_shape=jax.ShapeDtypeStruct((pieces[0].shape[1], 512), jnp.bfloat16),
-        in_specs=[vmem] * 4,
-        out_specs=vmem,
-        compiler_params=pltpu.CompilerParams(vmem_limit_bytes=8 << 20),
-        cost_estimate=pl.CostEstimate(flops=1 << 20, bytes_accessed=2 << 20, transcendentals=0),
-    )(*pieces)
 
 
 def best_kernel(own_ref, floor_ref, c0, c1, partner_ref, best_ref, turned):
@@ -83,22 +67,38 @@
                 best_ref[t : t + 1, here] = row
 
 
-def gain_kernel(own_ref, best_ref, other_ref, turned, partner_ref, gain_ref, cover_ref):
-    rows, width = own_ref.shape
-    scale = 1.0 / width**0.5
-    total = jnp.zeros((8, 512), jnp.float32)
-    for t, table in enumerate((own_ref, partner_ref)):
+def gains_over(tables, floors, pieces, turned):
+    rows, width = tables[0].shape
+    turned_table(pieces, turned)
+    total = jnp.zeros((8, 256), jnp.float32)
+    for t, table in enumerate(tables):
         for start in range(0, rows, STEP):
             sims = tile_sims(table, turned, start)
             for r in range(0, STEP, 128):
-                here = pl.ds(start + r, 128)
-                line = jnp.maximum(best_ref[t : t + 1, here], other_ref[1 - t : 2 - t, here])
-                if t == 0:
-                    cover_ref[:, here] = line
+                line = floors(t, pl.ds(start + r, 128))
                 floor = jnp.broadcast_to(line * width**0.5, (128, 128)).T
-                over = jnp.maximum(sims[r : r + 128] - jnp.concatenate([floor] * 4, axis=1), 0.0)
-                total = total + jnp.sum(over.reshape(16, 8, 512), axis=0)
-    sums = jnp.sum(total, axis=0, keepdims=True) * scale
+                over = jnp.maximum(sims[r : r + 128] - jnp.concatenate([floor] * 2, axis=1), 0.0)
+                total = total + jnp.sum(over.reshape(16, 8, 256), axis=0)
+    return jnp.sum(total, axis=0, keepdims=True) / width**0.5
+
+
+def near_gain_kernel(own_ref, best_ref, other_ref, c0, c1, partner_ref, sums_ref, cover_ref, turned):
+    def floors(t, here):
+        line = jnp.maximum(best_ref[t : t + 1, here], other_ref[1 - t : 2 - t, here])
+        if t == 0:
+            cover_ref[:, here] = line
+        return line
+
+    sums = gains_over((own_ref, partner_ref), floors, (c0, c1), turned)
+    sums_ref[...] = jnp.broadcast_to(sums, (8, 256))
+
+
+def far_gain_kernel(own_ref, best_ref, other_ref, sums_ref, c0, c1, partner_ref, gain_ref, turned):
+    def floors(t, here):
+        return jnp.maximum(best_ref[t : t + 1, here], other_ref[1 - t : 2 - t, here])
+
+    far = gains_over((own_ref, partner_ref), floors, (c0, c1), turned)
+    halves = (sums_ref[:1, :], far)
     first = lax.axis_index("core") == 0
     x = lax.axis_index("x")
     yhi, ylo = lax.axis_index("yhi"), lax.axis_index("ylo")
@@ -107,8 +107,8 @@
             x_mask = jnp.where(first, early, late)
             y_mask = jnp.where(first, late, early)
             at = ((ylo ^ (y_mask & 1)) * 4 + (x ^ x_mask)) * 2 + (yhi ^ (y_mask >> 1))
-            lane = late * 128 + early * 32
-            gain_ref[pl.ds(at * 8, 8), :] = jnp.broadcast_to(sums[:, lane : lane + 32], (8, 32))
+            lane = late % 2 * 128 + early * 32
+            gain_ref[pl.ds(at * 8, 8), :] = jnp.broadcast_to(halves[late // 2][:, lane : lane + 32], (8, 32))
 
 
 def on_chip(kernel, outs, scratch, pieces, *operands):
@@ -226,8 +226,10 @@
     for pieces in (chosen[:2], chosen[2:]):
         best = on_chip(best_kernel, [(2, rows)], table, 2, embeddings, best, *pieces, partner)[0]
     other = swap(best, 0, 1)
-    turned = turned_pieces(cands)
-    part, cover = on_chip(gain_kernel, [(128, 32), (1, rows)], [], 4, embeddings, best, other, turned, partner)
+    sums, cover = on_chip(
+        near_gain_kernel, [(8, 256), (1, rows)], table, 2, embeddings, best, other, *cands[:2], partner
+    )
+    part = on_chip(far_gain_kernel, [(128, 32)], table, 2, embeddings, best, other, sums, *cands[2:], partner)[0]
     parts = lax.all_to_all(part, CHIPS, 0, 0, tiled=True)
     gains = jnp.sum(lax.dynamic_slice_in_dim(parts, lax.axis_index("z") * 4, 4, 1), axis=0)
     return cover[0], gains

time: 85 us -> 85.6 us (level)
    pallas_call x3 -> x4, Pallas kernels: 8.14 us -> 9.06 us  [on_chip(): pl.pallas_call(kernel, out_shape=[jax.ShapeDtypeStruct(out, jnp.float32)...]
  transfers between devices with their start and end apart: 14 -> 14, of which waited for: 8 -> 8; matrix products, arithmetic and copies ran while one was open for 0% -> 0% of each run, Pallas kernels for 5% -> 8%
where the time goes in v9:
time: 85.6 us; the launch traced here: 85.4 us
  starting transfers between devices  28.9 us (34%)
  waiting for transfers between devices  21.8 us (25%)
  blocking collectives  20.7 us (24%)
  Pallas kernels  10.1 us (12%)
  local copies, waits for them, and re-layouts  1.57 us (2%)
  other arithmetic  1.53 us (2%)
    all_to_all x1, blocking collectives, local(): lax.all_to_all(jnp.broadcast_to(send, (8, 32 + MOST, width)), 'z', 0, 0)  20.7 us
    ppermute x9, starting transfers between devices, turn(): lax.ppermute(value, AXES, pairs_of(lambda y, x, z, c: (y, x ^ mask, z, c)...  11.8 us
    ppermute x4, starting transfers between devices, swap(): lax.ppermute(value, AXES, pairs_of(lambda y, x, z, c: (y ^ y_mask, x, z,...  11 us
    all_to_all x1, waiting for transfers between devices, local(): parts = lax.all_to_all(part, CHIPS, 0, 0, tiled=True)  10.6 us
    pallas_call x4, Pallas kernels, on_chip(): pl.pallas_call(kernel, out_shape=[jax.ShapeDtypeStruct(out, jnp.float32)...  9.06 us
    ppermute x9, waiting for transfers between devices, turn(): lax.ppermute(value, AXES, pairs_of(lambda y, x, z, c: (y, x ^ mask, z, c)...  6.15 us
    all_to_all x1, starting transfers between devices, local(): parts = lax.all_to_all(part, CHIPS, 0, 0, tiled=True)  6.06 us
    ppermute x4, waiting for transfers between devices, swap(): lax.ppermute(value, AXES, pairs_of(lambda y, x, z, c: (y ^ y_mask, x, z,...  5.05 us
  transfers between devices with their start and end apart: 14, of which 8 were waited for; matrix products, arithmetic and copies ran while one was open for 0% of the time, Pallas kernels for 8%

profile of v9, /device:TPU:1, one launch (start us, length us, event | category | flops | bytes accessed | tf_op | source)
XLA Modules:
  0.0 85.4 jit_solution(2811802875098477529)
XLA Ops:
  0.6 0.7 add_bitcast_fusion.index_ref
  1.7 1.5 %copy-done = bf16[2048,768]{1,0:T(8,128)(2,1)S(1)} copy-done((bf16[2048,768]{1,0:T(8,128)(2,1)S(1)}, bf16[2048,768]{1,0:T(8,128)(2,1)}, u32[]{:S(2)}) %copy-start) | copy-done | bytes 3145752
  3.9 3.3 %collective-permute-start = (bf16[64,768]{1,0:T(8,128)(2,1)S(1)}, bf16[64,768]{1,0:T(8,128)(2,1)S(1)}, u32[]{:S(2)}, u32[]{:S(2)}) collective-permute-start(bf16[64,768]{1,0:T(8,128)(2,1)S(1)} %get-tuple-element.10), channel_id=1, source_target_pairs={{0,1},{1,0},{2,3},{3,2},{4,5},{5,4},{6,7},{7,6},{8,9},{9,8},{10,11... | collective-permute-start | bytes 294920 | tf_op jit(solution)/shard_map/ppermute | solution.py:34
  7.2 0.9 %collective-permute-done = bf16[64,768]{1,0:T(8,128)(2,1)S(1)} collective-permute-done((bf16[64,768]{1,0:T(8,128)(2,1)S(1)}, bf16[64,768]{1,0:T(8,128)(2,1)S(1)}, u32[]{:S(2)}, u32[]{:S(2)}) %collective-permute-start) | collective-permute-done | bytes 98336 | tf_op jit(solution)/shard_map/ppermute | solution.py:34
  8.6 1.2 %collective-permute-start.1 = (bf16[32,768]{1,0:T(8,128)(2,1)S(1)}, bf16[32,768]{1,0:T(8,128)(2,1)S(1)}, u32[]{:S(2)}, u32[]{:S(2)}) collective-permute-start(bf16[32,768]{1,0:T(8,128)(2,1)S(1)} %slice.13), channel_id=1, source_target_pairs={{0,16},{1,17},{2,18},{3,19},{4,20},{5,21},{6,22},{7,23},{8,24},{9,... | collective-permute-start | bytes 147464 | tf_op jit(solution)/shard_map/ppermute | solution.py:34
  9.8 3.3 %collective-permute-done.1 = bf16[32,768]{1,0:T(8,128)(2,1)S(1)} collective-permute-done((bf16[32,768]{1,0:T(8,128)(2,1)S(1)}, bf16[32,768]{1,0:T(8,128)(2,1)S(1)}, u32[]{:S(2)}, u32[]{:S(2)}) %collective-permute-start.1) | collective-permute-done | bytes 49184 | tf_op jit(solution)/shard_map/ppermute | solution.py:34
  13.1 20.7 %all_to_all.14.got_ref = bf16[8,36,768]{2,1,0:T(8,128)(2,1)S(1)} all-to-all(bf16[8,36,768]{2,1,0:T(8,128)(2,1)S(1)} %broadcast_in_dim.3), channel_id=1, replica_groups=mesh['ylo'=2,'x'=4,'yhi'=2,'z'=8,'core'=2] {'z'}, dimensions={0} | all-to-all | bytes 884736 | tf_op jit(solution)/shard_map/all_to_all | solution.py:217
  33.9 1.4 %collective-permute-start.2 = (bf16[64,768]{1,0:T(8,128)(2,1)S(1)}, bf16[64,768]{1,0:T(8,128)(2,1)S(1)}, u32[]{:S(2)}, u32[]{:S(2)}) collective-permute-start(bf16[64,768]{1,0:T(8,128)(2,1)S(1)} %shard_map.61), channel_id=1, source_target_pairs={{0,32},{1,129},{2,34},{3,131},{4,36},{5,133},{6,38},{7,135},{8,40}... | collective-permute-start | bytes 294920 | tf_op jit(solution)/shard_map/ppermute | solution.py:38
  35.3 2.6 %collective-permute-start.3 = (bf16[64,768]{1,0:T(8,128)(2,1)S(1)}, bf16[64,768]{1,0:T(8,128)(2,1)S(1)}, u32[]{:S(2)}, u32[]{:S(2)}) collective-permute-start(bf16[64,768]{1,0:T(8,128)(2,1)S(1)} %shard_map.61), channel_id=1, source_target_pairs={{0,64},{1,17},{2,66},{3,19},{4,68},{5,21},{6,70},{7,23},{8,72},{9,... | collective-permute-start | bytes 294920 | tf_op jit(solution)/shard_map/ppermute | solution.py:38
  37.9 3.0 %collective-permute-done.3 = bf16[64,768]{1,0:T(8,128)(2,1)S(1)} collective-permute-done((bf16[64,768]{1,0:T(8,128)(2,1)S(1)}, bf16[64,768]{1,0:T(8,128)(2,1)S(1)}, u32[]{:S(2)}, u32[]{:S(2)}) %collective-permute-start.3) | collective-permute-done | bytes 98336 | tf_op jit(solution)/shard_map/ppermute | solution.py:38
  41.0 1.6 %collective-permute-done.4 = bf16[64,768]{1,0:T(8,128)(2,1)S(1)} collective-permute-done((bf16[64,768]{1,0:T(8,128)(2,1)S(1)}, bf16[64,768]{1,0:T(8,128)(2,1)S(1)}, u32[]{:S(2)}, u32[]{:S(2)}) %collective-permute-start.4) | collective-permute-done | bytes 98336 | tf_op jit(solution)/shard_map/ppermute | solution.py:38
  42.7 1.4 %collective-permute-start.5 = (bf16[128,768]{1,0:T(8,128)(2,1)S(1)}, bf16[128,768]{1,0:T(8,128)(2,1)S(1)}, u32[]{:S(2)}, u32[]{:S(2)}) collective-permute-start(bf16[128,768]{1,0:T(8,128)(2,1)S(1)} %bitcast.17), channel_id=1, source_target_pairs={{0,128},{1,33},{2,130},{3,35},{4,132},{5,37},{6,134},{7,39},{8,136... | collective-permute-start | bytes 589832 | tf_op jit(solution)/shard_map/ppermute | solution.py:38
  44.1 2.6 %collective-permute-start.7 = (bf16[128,768]{1,0:T(8,128)(2,1)S(1)}, bf16[128,768]{1,0:T(8,128)(2,1)S(1)}, u32[]{:S(2)}, u32[]{:S(2)}) collective-permute-start(bf16[128,768]{1,0:T(8,128)(2,1)S(1)} %bitcast.18), channel_id=1, source_target_pairs={{0,16},{1,65},{2,18},{3,67},{4,20},{5,69},{6,22},{7,71},{8,24},{9,... | collective-permute-start | bytes 589832 | tf_op jit(solution)/shard_map/ppermute | solution.py:38
  47.3 3.3 %collective-permute-start.11 = (bf16[128,768]{1,0:T(8,128)(2,1)S(1)}, bf16[128,768]{1,0:T(8,128)(2,1)S(1)}, u32[]{:S(2)}, u32[]{:S(2)}) collective-permute-start(bf16[128,768]{1,0:T(8,128)(2,1)S(1)} %bitcast.14), channel_id=1, source_target_pairs={{0,16},{1,65},{2,18},{3,67},{4,20},{5,69},{6,22},{7,71},{8,24},{9,... | collective-permute-start | bytes 589832 | tf_op jit(solution)/shard_map/ppermute | solution.py:38
  51.1 2.0 %shard_map.62.floor_ref = f32[2,2048]{1,0:T(2,128)S(1)} custom-call(bf16[2048,768]{1,0:T(8,128)(2,1)S(1)} %copy-done, f32[1,2048]{1,0:T(1,128)S(1)} %bitcast.22, bf16[128,768]{1,0:T(8,128)(2,1)S(1)} %bitcast.20, bf16[128,768]{1,0:T(8,128)(2,1)S(1)} %collective-permute-done.5.c1, bf16[2048,768]{1,0:T(8,128)(2,1)S(1)} %collective-permute-done.6.partner_ref), custom_call_target="tpu_custom_call" | custom-call | flops 1610612736 | bytes 8388608 | tf_op jit(solution)/shard_map/pallas_call | solution.py:116
  53.1 0.9 %collective-permute-done.8.c1 = bf16[128,768]{1,0:T(8,128)(2,1)S(1)} collective-permute-done((bf16[128,768]{1,0:T(8,128)(2,1)S(1)}, bf16[128,768]{1,0:T(8,128)(2,1)S(1)}, u32[]{:S(2)}, u32[]{:S(2)}) %collective-permute-start.8) | collective-permute-done | bytes 196640 | tf_op jit(solution)/shard_map/ppermute | solution.py:38
  54.0 2.0 %shard_map.63.best_ref = f32[2,2048]{1,0:T(2,128)S(1)} custom-call(bf16[2048,768]{1,0:T(8,128)(2,1)S(1)} %copy-done, f32[2,2048]{1,0:T(2,128)S(1)} %shard_map.62.floor_ref, bf16[128,768]{1,0:T(8,128)(2,1)S(1)} %collective-permute-done.7.c0, bf16[128,768]{1,0:T(8,128)(2,1)S(1)} %collective-permute-done.8.c1, ...), custom_call_target="tpu_custom_call" | custom-call | flops 1610612736 | bytes 8388608 | tf_op jit(solution)/shard_map/pallas_call | solution.py:116
  56.0 6.1 %collective-permute-start.9 = (f32[2,2048]{1,0:T(2,128)S(1)}, f32[2,2048]{1,0:T(2,128)S(1)}, u32[]{:S(2)}, u32[]{:S(2)}) collective-permute-start(f32[2,2048]{1,0:T(2,128)S(1)} %shard_map.63.best_ref), channel_id=1, source_target_pairs={{0,1},{1,0},{2,3},{3,2},{4,5},{5,4},{6,7},{7,6},{8,9},{9,8},{10,11... | collective-permute-start | bytes 49160 | tf_op jit(solution)/shard_map/ppermute | solution.py:34
  62.1 0.8 collective-permute-done.9.other_ref
  62.9 2.4 %shard_map.64 = (f32[8,256]{1,0:T(8,128)S(1)}, f32[1,2048]{1,0:T(1,128)}) custom-call(bf16[2048,768]{1,0:T(8,128)(2,1)S(1)} %copy-done, f32[2,2048]{1,0:T(2,128)S(1)} %shard_map.63.best_ref, f32[2,2048]{1,0:T(2,128)S(1)} %collective-permute-done.9.other_ref, bf16[128,768]{1,0:T(8,128)(2,1)S(1)} %bitcast.16, bf16[128,768]{1,0:T(8,128)(2,1)S(1)} %collective-permute-done.10.c1, ...), custom_call_target="tpu_custom_call" | custom-call | flops 1610612736 | bytes 8388608 | tf_op jit(solution)/shard_map/pallas_call | solution.py:116
  65.4 2.6 %shard_map.65 = f32[128,32]{1,0:T(8,128)} custom-call(bf16[2048,768]{1,0:T(8,128)(2,1)S(1)} %copy-done, f32[2,2048]{1,0:T(2,128)S(1)} %shard_map.63.best_ref, f32[2,2048]{1,0:T(2,128)S(1)} %collective-permute-done.9.other_ref, f32[8,256]{1,0:T(8,128)S(1)} %get-tuple-element.15.sums_ref, bf16[128,768]{1,0:T(8,128)(2,1)S(1)} %collective-permute-done.11.c0, ...), custom_call_target="tpu_custom_call" | custom-call | flops 1610612736 | bytes 8388608 | tf_op jit(solution)/shard_map/pallas_call | solution.py:116
  68.0 6.1 %all-to-all-start.1 = ((f32[128,1,32]{2,1,0:T(1,128)}), f32[128,1,32]{2,1,0:T(1,128)S(1)}, u32[]{:S(2)}, u32[]{:S(2)}) async-start(f32[128,1,32]{2,1,0:T(1,128)} %bitcast.10), calls=%async_computation.1 | async-start | bytes 131072 | tf_op jit(solution)/shard_map/all_to_all | solution.py:233
  74.1 10.6 %all-to-all-done.1 = f32[128,1,32]{2,1,0:T(1,128)S(1)} async-done(((f32[128,1,32]{2,1,0:T(1,128)}), f32[128,1,32]{2,1,0:T(1,128)S(1)}, u32[]{:S(2)}, u32[]{:S(2)}) %all-to-all-start.1) | async-done | bytes 16416 | tf_op jit(solution)/shard_map/all_to_all | solution.py:233
  84.7 0.7 dynamic-slice_reduce_fusion
  (25 shorter events, 2.7 us)
Async XLA Ops:
  1.3 1.9 %copy-start = (bf16[2048,768]{1,0:T(8,128)(2,1)S(1)}, bf16[2048,768]{1,0:T(8,128)(2,1)}, u32[]{:S(2)}) copy-start(bf16[2048,768]{1,0:T(8,128)(2,1)} %own_ref.7) | copy-start | bytes 9437188
  3.2 47.8 %copy-start.1 = (f32[2048]{0:T(1024)S(1)}, f32[2048]{0:T(1024)}, u32[]{:S(2)}) copy-start(f32[2048]{0:T(1024)} %param.5) | copy-start | bytes 24580
  3.9 4.3 %collective-permute-start = (bf16[64,768]{1,0:T(8,128)(2,1)S(1)}, bf16[64,768]{1,0:T(8,128)(2,1)S(1)}, u32[]{:S(2)}, u32[]{:S(2)}) collective-permute-start(bf16[64,768]{1,0:T(8,128)(2,1)S(1)} %get-tuple-element.10), channel_id=1, source_target_pairs={{0,1},{1,0},{2,3},{3,2},{4,5},{5,4},{6,7},{7,6},{8,9},{9,8},{10,11... | collective-permute-start | bytes 294920 | tf_op jit(solution)/shard_map/ppermute | solution.py:34
  8.2 42.4 %collective-permute-start.6 = (bf16[2048,768]{1,0:T(8,128)(2,1)S(1)}, bf16[2048,768]{1,0:T(8,128)(2,1)S(1)}, u32[]{:S(2)}, u32[]{:S(2)}) collective-permute-start(bf16[2048,768]{1,0:T(8,128)(2,1)S(1)} %copy-done), channel_id=1, source_target_pairs={{0,1},{1,0},{2,3},{3,2},{4,5},{5,4},{6,7},{7,6},{8,9},{9,8},{10,11... | collective-permute-start | bytes 9437192 | tf_op jit(solution)/shard_map/ppermute | solution.py:34
  8.6 4.4 %collective-permute-start.1 = (bf16[32,768]{1,0:T(8,128)(2,1)S(1)}, bf16[32,768]{1,0:T(8,128)(2,1)S(1)}, u32[]{:S(2)}, u32[]{:S(2)}) collective-permute-start(bf16[32,768]{1,0:T(8,128)(2,1)S(1)} %slice.13), channel_id=1, source_target_pairs={{0,16},{1,17},{2,18},{3,19},{4,20},{5,21},{6,22},{7,23},{8,24},{9,... | collective-permute-start | bytes 147464 | tf_op jit(solution)/shard_map/ppermute | solution.py:34
  33.9 4.0 %collective-permute-start.2 = (bf16[64,768]{1,0:T(8,128)(2,1)S(1)}, bf16[64,768]{1,0:T(8,128)(2,1)S(1)}, u32[]{:S(2)}, u32[]{:S(2)}) collective-permute-start(bf16[64,768]{1,0:T(8,128)(2,1)S(1)} %shard_map.61), channel_id=1, source_target_pairs={{0,32},{1,129},{2,34},{3,131},{4,36},{5,133},{6,38},{7,135},{8,40}... | collective-permute-start | bytes 294920 | tf_op jit(solution)/shard_map/ppermute | solution.py:38
  35.3 5.7 %collective-permute-start.3 = (bf16[64,768]{1,0:T(8,128)(2,1)S(1)}, bf16[64,768]{1,0:T(8,128)(2,1)S(1)}, u32[]{:S(2)}, u32[]{:S(2)}) collective-permute-start(bf16[64,768]{1,0:T(8,128)(2,1)S(1)} %shard_map.61), channel_id=1, source_target_pairs={{0,64},{1,17},{2,66},{3,19},{4,68},{5,21},{6,70},{7,23},{8,72},{9,... | collective-permute-start | bytes 294920 | tf_op jit(solution)/shard_map/ppermute | solution.py:38
  37.9 4.7 %collective-permute-start.4 = (bf16[64,768]{1,0:T(8,128)(2,1)S(1)}, bf16[64,768]{1,0:T(8,128)(2,1)S(1)}, u32[]{:S(2)}, u32[]{:S(2)}) collective-permute-start(bf16[64,768]{1,0:T(8,128)(2,1)S(1)} %shard_map.61), channel_id=1, source_target_pairs={{0,96},{1,145},{2,98},{3,147},{4,100},{5,149},{6,102},{7,151},{8,1... | collective-permute-start | bytes 294920 | tf_op jit(solution)/shard_map/ppermute | solution.py:38
  42.7 4.6 %collective-permute-start.5 = (bf16[128,768]{1,0:T(8,128)(2,1)S(1)}, bf16[128,768]{1,0:T(8,128)(2,1)S(1)}, u32[]{:S(2)}, u32[]{:S(2)}) collective-permute-start(bf16[128,768]{1,0:T(8,128)(2,1)S(1)} %bitcast.17), channel_id=1, source_target_pairs={{0,128},{1,33},{2,130},{3,35},{4,132},{5,37},{6,134},{7,39},{8,136... | collective-permute-start | bytes 589832 | tf_op jit(solution)/shard_map/ppermute | solution.py:38
  44.1 8.9 %collective-permute-start.7 = (bf16[128,768]{1,0:T(8,128)(2,1)S(1)}, bf16[128,768]{1,0:T(8,128)(2,1)S(1)}, u32[]{:S(2)}, u32[]{:S(2)}) collective-permute-start(bf16[128,768]{1,0:T(8,128)(2,1)S(1)} %bitcast.18), channel_id=1, source_target_pairs={{0,16},{1,65},{2,18},{3,67},{4,20},{5,69},{6,22},{7,71},{8,24},{9,... | collective-permute-start | bytes 589832 | tf_op jit(solution)/shard_map/ppermute | solution.py:38
  46.7 7.3 %collective-permute-start.8 = (bf16[128,768]{1,0:T(8,128)(2,1)S(1)}, bf16[128,768]{1,0:T(8,128)(2,1)S(1)}, u32[]{:S(2)}, u32[]{:S(2)}) collective-permute-start(bf16[128,768]{1,0:T(8,128)(2,1)S(1)} %bitcast.19), channel_id=1, source_target_pairs={{0,144},{1,97},{2,146},{3,99},{4,148},{5,101},{6,150},{7,103},{8,1... | collective-permute-start | bytes 589832 | tf_op jit(solution)/shard_map/ppermute | solution.py:38
  46.8 15.4 %collective-permute-start.10 = (bf16[128,768]{1,0:T(8,128)(2,1)S(1)}, bf16[128,768]{1,0:T(8,128)(2,1)S(1)}, u32[]{:S(2)}, u32[]{:S(2)}) collective-permute-start(bf16[128,768]{1,0:T(8,128)(2,1)S(1)} %bitcast.13), channel_id=1, source_target_pairs={{0,128},{1,33},{2,130},{3,35},{4,132},{5,37},{6,134},{7,39},{8,136... | collective-permute-start | bytes 589832 | tf_op jit(solution)/shard_map/ppermute | solution.py:38
  47.3 18.1 %collective-permute-start.11 = (bf16[128,768]{1,0:T(8,128)(2,1)S(1)}, bf16[128,768]{1,0:T(8,128)(2,1)S(1)}, u32[]{:S(2)}, u32[]{:S(2)}) collective-permute-start(bf16[128,768]{1,0:T(8,128)(2,1)S(1)} %bitcast.14), channel_id=1, source_target_pairs={{0,16},{1,65},{2,18},{3,67},{4,20},{5,69},{6,22},{7,71},{8,24},{9,... | collective-permute-start | bytes 589832 | tf_op jit(solution)/shard_map/ppermute | solution.py:38
  50.6 14.8 %collective-permute-start.12 = (bf16[128,768]{1,0:T(8,128)(2,1)S(1)}, bf16[128,768]{1,0:T(8,128)(2,1)S(1)}, u32[]{:S(2)}, u32[]{:S(2)}) collective-permute-start(bf16[128,768]{1,0:T(8,128)(2,1)S(1)} %bitcast.15), channel_id=1, source_target_pairs={{0,144},{1,97},{2,146},{3,99},{4,148},{5,101},{6,150},{7,103},{8,1... | collective-permute-start | bytes 589832 | tf_op jit(solution)/shard_map/ppermute | solution.py:38
  56.0 6.9 %collective-permute-start.9 = (f32[2,2048]{1,0:T(2,128)S(1)}, f32[2,2048]{1,0:T(2,128)S(1)}, u32[]{:S(2)}, u32[]{:S(2)}) collective-permute-start(f32[2,2048]{1,0:T(2,128)S(1)} %shard_map.63.best_ref), channel_id=1, source_target_pairs={{0,1},{1,0},{2,3},{3,2},{4,5},{5,4},{6,7},{7,6},{8,9},{9,8},{10,11... | collective-permute-start | bytes 49160 | tf_op jit(solution)/shard_map/ppermute | solution.py:34
  68.0 16.6 %all-to-all-start.1 = ((f32[128,1,32]{2,1,0:T(1,128)}), f32[128,1,32]{2,1,0:T(1,128)S(1)}, u32[]{:S(2)}, u32[]{:S(2)}) async-start(f32[128,1,32]{2,1,0:T(1,128)} %bitcast.10), calls=%async_computation.1 | async-start | bytes 131072 | tf_op jit(solution)/shard_map/all_to_all | solution.py:233

commit v10 on v8

--- a/solution.py
+++ b/solution.py
@@ -38,7 +38,7 @@
     return lax.ppermute(
         value,
         AXES,
-        pairs_of(lambda y, x, z, c: (y, x ^ mask, z, c) if (c == 0) == first else (y ^ mask, x, z, c)),
+        pairs_of(lambda y, x, z, c: (y, x ^ mask, z, c) if (c == 1) == first else (y ^ mask, x, z, c)),
     )
 
 
@@ -99,7 +99,7 @@
                 over = jnp.maximum(sims[r : r + 128] - jnp.concatenate([floor] * 4, axis=1), 0.0)
                 total = total + jnp.sum(over.reshape(16, 8, 512), axis=0)
     sums = jnp.sum(total, axis=0, keepdims=True) * scale
-    first = lax.axis_index("core") == 0
+    first = lax.axis_index("core") == 1
     x = lax.axis_index("x")
     yhi, ylo = lax.axis_index("yhi"), lax.axis_index("ylo")
     for late in range(4):

time: 85 us -> 85 us (level)
  no operation moved by 1% of the time
where the time goes in v10:
time: 85 us; the launch traced here: 84.5 us
  starting transfers between devices  28.9 us (34%)
  waiting for transfers between devices  21.5 us (25%)
  blocking collectives  20.7 us (24%)
  Pallas kernels  9.48 us (11%)
  local copies, waits for them, and re-layouts  1.57 us (2%)
  other arithmetic  1.53 us (2%)
    all_to_all x1, blocking collectives, local(): lax.all_to_all(jnp.broadcast_to(send, (8, 32 + MOST, width)), 'z', 0, 0)  20.7 us
    ppermute x9, starting transfers between devices, turn(): lax.ppermute(value, AXES, pairs_of(lambda y, x, z, c: (y, x ^ mask, z, c)...  11.5 us
    ppermute x4, starting transfers between devices, swap(): lax.ppermute(value, AXES, pairs_of(lambda y, x, z, c: (y ^ y_mask, x, z,...  11.3 us
    all_to_all x1, waiting for transfers between devices, local(): parts = lax.all_to_all(part, CHIPS, 0, 0, tiled=True)  10.6 us
    pallas_call x3, Pallas kernels, on_chip(): pl.pallas_call(kernel, out_shape=[jax.ShapeDtypeStruct(out, jnp.float32)...  8.14 us
    ppermute x9, waiting for transfers between devices, turn(): lax.ppermute(value, AXES, pairs_of(lambda y, x, z, c: (y, x ^ mask, z, c)...  6.16 us
    all_to_all x1, starting transfers between devices, local(): parts = lax.all_to_all(part, CHIPS, 0, 0, tiled=True)  6.07 us
    ppermute x4, waiting for transfers between devices, swap(): lax.ppermute(value, AXES, pairs_of(lambda y, x, z, c: (y ^ y_mask, x, z,...  4.78 us
  transfers between devices with their start and end apart: 14, of which 8 were waited for; matrix products, arithmetic and copies ran while one was open for 0% of the time, Pallas kernels for 5%

profile of v10, /device:TPU:1, one launch (start us, length us, event | category | flops | bytes accessed | tf_op | source)
XLA Modules:
  0.0 84.5 jit_solution(11316298688610368383)
XLA Ops:
  0.6 0.7 add_bitcast_fusion.index_ref
  1.7 1.5 %copy-done = bf16[2048,768]{1,0:T(8,128)(2,1)S(1)} copy-done((bf16[2048,768]{1,0:T(8,128)(2,1)S(1)}, bf16[2048,768]{1,0:T(8,128)(2,1)}, u32[]{:S(2)}) %copy-start) | copy-done | bytes 3145752
  3.2 0.6 shard_map.60
  3.9 3.3 %collective-permute-start = (bf16[64,768]{1,0:T(8,128)(2,1)S(1)}, bf16[64,768]{1,0:T(8,128)(2,1)S(1)}, u32[]{:S(2)}, u32[]{:S(2)}) collective-permute-start(bf16[64,768]{1,0:T(8,128)(2,1)S(1)} %get-tuple-element.10), channel_id=1, source_target_pairs={{0,1},{1,0},{2,3},{3,2},{4,5},{5,4},{6,7},{7,6},{8,9},{9,8},{10,11... | collective-permute-start | bytes 294920 | tf_op jit(solution)/shard_map/ppermute | solution.py:34
  7.2 0.9 %collective-permute-done = bf16[64,768]{1,0:T(8,128)(2,1)S(1)} collective-permute-done((bf16[64,768]{1,0:T(8,128)(2,1)S(1)}, bf16[64,768]{1,0:T(8,128)(2,1)S(1)}, u32[]{:S(2)}, u32[]{:S(2)}) %collective-permute-start) | collective-permute-done | bytes 98336 | tf_op jit(solution)/shard_map/ppermute | solution.py:34
  8.6 1.2 %collective-permute-start.1 = (bf16[32,768]{1,0:T(8,128)(2,1)S(1)}, bf16[32,768]{1,0:T(8,128)(2,1)S(1)}, u32[]{:S(2)}, u32[]{:S(2)}) collective-permute-start(bf16[32,768]{1,0:T(8,128)(2,1)S(1)} %slice.13), channel_id=1, source_target_pairs={{0,16},{1,17},{2,18},{3,19},{4,20},{5,21},{6,22},{7,23},{8,24},{9,... | collective-permute-start | bytes 147464 | tf_op jit(solution)/shard_map/ppermute | solution.py:34
  9.8 3.3 %collective-permute-done.1 = bf16[32,768]{1,0:T(8,128)(2,1)S(1)} collective-permute-done((bf16[32,768]{1,0:T(8,128)(2,1)S(1)}, bf16[32,768]{1,0:T(8,128)(2,1)S(1)}, u32[]{:S(2)}, u32[]{:S(2)}) %collective-permute-start.1) | collective-permute-done | bytes 49184 | tf_op jit(solution)/shard_map/ppermute | solution.py:34
  13.1 20.7 %all_to_all.14.got_ref = bf16[8,36,768]{2,1,0:T(8,128)(2,1)S(1)} all-to-all(bf16[8,36,768]{2,1,0:T(8,128)(2,1)S(1)} %broadcast_in_dim.3), channel_id=1, replica_groups=mesh['ylo'=2,'x'=4,'yhi'=2,'z'=8,'core'=2] {'z'}, dimensions={0} | all-to-all | bytes 884736 | tf_op jit(solution)/shard_map/all_to_all | solution.py:217
  33.9 1.3 %collective-permute-start.2 = (bf16[64,768]{1,0:T(8,128)(2,1)S(1)}, bf16[64,768]{1,0:T(8,128)(2,1)S(1)}, u32[]{:S(2)}, u32[]{:S(2)}) collective-permute-start(bf16[64,768]{1,0:T(8,128)(2,1)S(1)} %shard_map.61), channel_id=1, source_target_pairs={{0,128},{1,33},{2,130},{3,35},{4,132},{5,37},{6,134},{7,39},{8,136... | collective-permute-start | bytes 294920 | tf_op jit(solution)/shard_map/ppermute | solution.py:38
  35.2 2.5 %collective-permute-start.3 = (bf16[64,768]{1,0:T(8,128)(2,1)S(1)}, bf16[64,768]{1,0:T(8,128)(2,1)S(1)}, u32[]{:S(2)}, u32[]{:S(2)}) collective-permute-start(bf16[64,768]{1,0:T(8,128)(2,1)S(1)} %shard_map.61), channel_id=1, source_target_pairs={{0,16},{1,65},{2,18},{3,67},{4,20},{5,69},{6,22},{7,71},{8,24},{9,... | collective-permute-start | bytes 294920 | tf_op jit(solution)/shard_map/ppermute | solution.py:38
  37.9 2.9 %collective-permute-done.3 = bf16[64,768]{1,0:T(8,128)(2,1)S(1)} collective-permute-done((bf16[64,768]{1,0:T(8,128)(2,1)S(1)}, bf16[64,768]{1,0:T(8,128)(2,1)S(1)}, u32[]{:S(2)}, u32[]{:S(2)}) %collective-permute-start.3) | collective-permute-done | bytes 98336 | tf_op jit(solution)/shard_map/ppermute | solution.py:38
  40.7 1.6 %collective-permute-done.4 = bf16[64,768]{1,0:T(8,128)(2,1)S(1)} collective-permute-done((bf16[64,768]{1,0:T(8,128)(2,1)S(1)}, bf16[64,768]{1,0:T(8,128)(2,1)S(1)}, u32[]{:S(2)}, u32[]{:S(2)}) %collective-permute-start.4) | collective-permute-done | bytes 98336 | tf_op jit(solution)/shard_map/ppermute | solution.py:38
  42.5 1.4 %collective-permute-start.5 = (bf16[128,768]{1,0:T(8,128)(2,1)S(1)}, bf16[128,768]{1,0:T(8,128)(2,1)S(1)}, u32[]{:S(2)}, u32[]{:S(2)}) collective-permute-start(bf16[128,768]{1,0:T(8,128)(2,1)S(1)} %bitcast.13), channel_id=1, source_target_pairs={{0,32},{1,129},{2,34},{3,131},{4,36},{5,133},{6,38},{7,135},{8,40}... | collective-permute-start | bytes 589832 | tf_op jit(solution)/shard_map/ppermute | solution.py:38
  43.8 2.6 %collective-permute-start.7 = (bf16[128,768]{1,0:T(8,128)(2,1)S(1)}, bf16[128,768]{1,0:T(8,128)(2,1)S(1)}, u32[]{:S(2)}, u32[]{:S(2)}) collective-permute-start(bf16[128,768]{1,0:T(8,128)(2,1)S(1)} %bitcast.14), channel_id=1, source_target_pairs={{0,64},{1,17},{2,66},{3,19},{4,68},{5,21},{6,70},{7,23},{8,72},{9,... | collective-permute-start | bytes 589832 | tf_op jit(solution)/shard_map/ppermute | solution.py:38
  46.5 0.7 collective-permute-done.5.c1
  47.2 3.1 %collective-permute-start.11 = (bf16[128,768]{1,0:T(8,128)(2,1)S(1)}, bf16[128,768]{1,0:T(8,128)(2,1)S(1)}, u32[]{:S(2)}, u32[]{:S(2)}) collective-permute-start(bf16[128,768]{1,0:T(8,128)(2,1)S(1)} %bitcast.18), channel_id=1, source_target_pairs={{0,64},{1,17},{2,66},{3,19},{4,68},{5,21},{6,70},{7,23},{8,72},{9,... | collective-permute-start | bytes 589832 | tf_op jit(solution)/shard_map/ppermute | solution.py:38
  50.8 2.0 %shard_map.62.floor_ref = f32[2,2048]{1,0:T(2,128)S(1)} custom-call(bf16[2048,768]{1,0:T(8,128)(2,1)S(1)} %copy-done, f32[1,2048]{1,0:T(1,128)S(1)} %bitcast.22, bf16[128,768]{1,0:T(8,128)(2,1)S(1)} %bitcast.16, bf16[128,768]{1,0:T(8,128)(2,1)S(1)} %collective-permute-done.5.c1, bf16[2048,768]{1,0:T(8,128)(2,1)S(1)} %collective-permute-done.6.partner_ref), custom_call_target="tpu_custom_call" | custom-call | flops 1610612736 | bytes 8388608 | tf_op jit(solution)/shard_map/pallas_call | solution.py:116
  52.8 1.0 %collective-permute-done.8.c1 = bf16[128,768]{1,0:T(8,128)(2,1)S(1)} collective-permute-done((bf16[128,768]{1,0:T(8,128)(2,1)S(1)}, bf16[128,768]{1,0:T(8,128)(2,1)S(1)}, u32[]{:S(2)}, u32[]{:S(2)}) %collective-permute-start.8) | collective-permute-done | bytes 196640 | tf_op jit(solution)/shard_map/ppermute | solution.py:38
  53.7 2.0 %shard_map.63.best_ref = f32[2,2048]{1,0:T(2,128)S(1)} custom-call(bf16[2048,768]{1,0:T(8,128)(2,1)S(1)} %copy-done, f32[2,2048]{1,0:T(2,128)S(1)} %shard_map.62.floor_ref, bf16[128,768]{1,0:T(8,128)(2,1)S(1)} %collective-permute-done.7.c0, bf16[128,768]{1,0:T(8,128)(2,1)S(1)} %collective-permute-done.8.c1, ...), custom_call_target="tpu_custom_call" | custom-call | flops 1610612736 | bytes 8388608 | tf_op jit(solution)/shard_map/pallas_call | solution.py:116
  55.7 6.4 %collective-permute-start.9 = (f32[2,2048]{1,0:T(2,128)S(1)}, f32[2,2048]{1,0:T(2,128)S(1)}, u32[]{:S(2)}, u32[]{:S(2)}) collective-permute-start(f32[2,2048]{1,0:T(2,128)S(1)} %shard_map.63.best_ref), channel_id=1, source_target_pairs={{0,1},{1,0},{2,3},{3,2},{4,5},{5,4},{6,7},{7,6},{8,9},{9,8},{10,11... | collective-permute-start | bytes 49160 | tf_op jit(solution)/shard_map/ppermute | solution.py:34
  62.9 4.1 %shard_map.65 = (f32[128,32]{1,0:T(8,128)}, f32[1,2048]{1,0:T(1,128)}) custom-call(bf16[2048,768]{1,0:T(8,128)(2,1)S(1)} %copy-done, f32[2,2048]{1,0:T(2,128)S(1)} %shard_map.63.best_ref, f32[2,2048]{1,0:T(2,128)S(1)} %collective-permute-done.9.other_ref, bf16[768,512]{1,0:T(8,128)(2,1)S(1)} %shard_map.64.turned, ...), custom_call_target="tpu_custom_call" | custom-call | flops 3221225472 | bytes 8388608 | tf_op jit(solution)/shard_map/pallas_call | solution.py:116
  67.1 6.1 %all-to-all-start.1 = ((f32[128,1,32]{2,1,0:T(1,128)}), f32[128,1,32]{2,1,0:T(1,128)S(1)}, u32[]{:S(2)}, u32[]{:S(2)}) async-start(f32[128,1,32]{2,1,0:T(1,128)} %bitcast.10), calls=%async_computation.1 | async-start | bytes 131072 | tf_op jit(solution)/shard_map/all_to_all | solution.py:231
  73.2 10.6 %all-to-all-done.1 = f32[128,1,32]{2,1,0:T(1,128)S(1)} async-done(((f32[128,1,32]{2,1,0:T(1,128)}), f32[128,1,32]{2,1,0:T(1,128)S(1)}, u32[]{:S(2)}, u32[]{:S(2)}) %all-to-all-start.1) | async-done | bytes 16416 | tf_op jit(solution)/shard_map/all_to_all | solution.py:231
  83.7 0.7 dynamic-slice_reduce_fusion
  (25 shorter events, 2.6 us)
Async XLA Ops:
  1.3 1.9 %copy-start = (bf16[2048,768]{1,0:T(8,128)(2,1)S(1)}, bf16[2048,768]{1,0:T(8,128)(2,1)}, u32[]{:S(2)}) copy-start(bf16[2048,768]{1,0:T(8,128)(2,1)} %own_ref.5) | copy-start | bytes 9437188
  3.2 47.5 %copy-start.1 = (f32[2048]{0:T(1024)S(1)}, f32[2048]{0:T(1024)}, u32[]{:S(2)}) copy-start(f32[2048]{0:T(1024)} %param.5) | copy-start | bytes 24580
  3.9 4.3 %collective-permute-start = (bf16[64,768]{1,0:T(8,128)(2,1)S(1)}, bf16[64,768]{1,0:T(8,128)(2,1)S(1)}, u32[]{:S(2)}, u32[]{:S(2)}) collective-permute-start(bf16[64,768]{1,0:T(8,128)(2,1)S(1)} %get-tuple-element.10), channel_id=1, source_target_pairs={{0,1},{1,0},{2,3},{3,2},{4,5},{5,4},{6,7},{7,6},{8,9},{9,8},{10,11... | collective-permute-start | bytes 294920 | tf_op jit(solution)/shard_map/ppermute | solution.py:34
  8.2 42.1 %collective-permute-start.6 = (bf16[2048,768]{1,0:T(8,128)(2,1)S(1)}, bf16[2048,768]{1,0:T(8,128)(2,1)S(1)}, u32[]{:S(2)}, u32[]{:S(2)}) collective-permute-start(bf16[2048,768]{1,0:T(8,128)(2,1)S(1)} %copy-done), channel_id=1, source_target_pairs={{0,1},{1,0},{2,3},{3,2},{4,5},{5,4},{6,7},{7,6},{8,9},{9,8},{10,11... | collective-permute-start | bytes 9437192 | tf_op jit(solution)/shard_map/ppermute | solution.py:34
  8.6 4.4 %collective-permute-start.1 = (bf16[32,768]{1,0:T(8,128)(2,1)S(1)}, bf16[32,768]{1,0:T(8,128)(2,1)S(1)}, u32[]{:S(2)}, u32[]{:S(2)}) collective-permute-start(bf16[32,768]{1,0:T(8,128)(2,1)S(1)} %slice.13), channel_id=1, source_target_pairs={{0,16},{1,17},{2,18},{3,19},{4,20},{5,21},{6,22},{7,23},{8,24},{9,... | collective-permute-start | bytes 147464 | tf_op jit(solution)/shard_map/ppermute | solution.py:34
  33.9 3.9 %collective-permute-start.2 = (bf16[64,768]{1,0:T(8,128)(2,1)S(1)}, bf16[64,768]{1,0:T(8,128)(2,1)S(1)}, u32[]{:S(2)}, u32[]{:S(2)}) collective-permute-start(bf16[64,768]{1,0:T(8,128)(2,1)S(1)} %shard_map.61), channel_id=1, source_target_pairs={{0,128},{1,33},{2,130},{3,35},{4,132},{5,37},{6,134},{7,39},{8,136... | collective-permute-start | bytes 294920 | tf_op jit(solution)/shard_map/ppermute | solution.py:38
  35.2 5.5 %collective-permute-start.3 = (bf16[64,768]{1,0:T(8,128)(2,1)S(1)}, bf16[64,768]{1,0:T(8,128)(2,1)S(1)}, u32[]{:S(2)}, u32[]{:S(2)}) collective-permute-start(bf16[64,768]{1,0:T(8,128)(2,1)S(1)} %shard_map.61), channel_id=1, source_target_pairs={{0,16},{1,65},{2,18},{3,67},{4,20},{5,69},{6,22},{7,71},{8,24},{9,... | collective-permute-start | bytes 294920 | tf_op jit(solution)/shard_map/ppermute | solution.py:38
  37.7 4.7 %collective-permute-start.4 = (bf16[64,768]{1,0:T(8,128)(2,1)S(1)}, bf16[64,768]{1,0:T(8,128)(2,1)S(1)}, u32[]{:S(2)}, u32[]{:S(2)}) collective-permute-start(bf16[64,768]{1,0:T(8,128)(2,1)S(1)} %shard_map.61), channel_id=1, source_target_pairs={{0,144},{1,97},{2,146},{3,99},{4,148},{5,101},{6,150},{7,103},{8,1... | collective-permute-start | bytes 294920 | tf_op jit(solution)/shard_map/ppermute | solution.py:38
  42.5 4.7 %collective-permute-start.5 = (bf16[128,768]{1,0:T(8,128)(2,1)S(1)}, bf16[128,768]{1,0:T(8,128)(2,1)S(1)}, u32[]{:S(2)}, u32[]{:S(2)}) collective-permute-start(bf16[128,768]{1,0:T(8,128)(2,1)S(1)} %bitcast.13), channel_id=1, source_target_pairs={{0,32},{1,129},{2,34},{3,131},{4,36},{5,133},{6,38},{7,135},{8,40}... | collective-permute-start | bytes 589832 | tf_op jit(solution)/shard_map/ppermute | solution.py:38
  43.8 8.9 %collective-permute-start.7 = (bf16[128,768]{1,0:T(8,128)(2,1)S(1)}, bf16[128,768]{1,0:T(8,128)(2,1)S(1)}, u32[]{:S(2)}, u32[]{:S(2)}) collective-permute-start(bf16[128,768]{1,0:T(8,128)(2,1)S(1)} %bitcast.14), channel_id=1, source_target_pairs={{0,64},{1,17},{2,66},{3,19},{4,68},{5,21},{6,70},{7,23},{8,72},{9,... | collective-permute-start | bytes 589832 | tf_op jit(solution)/shard_map/ppermute | solution.py:38
  46.5 7.3 %collective-permute-start.8 = (bf16[128,768]{1,0:T(8,128)(2,1)S(1)}, bf16[128,768]{1,0:T(8,128)(2,1)S(1)}, u32[]{:S(2)}, u32[]{:S(2)}) collective-permute-start(bf16[128,768]{1,0:T(8,128)(2,1)S(1)} %bitcast.15), channel_id=1, source_target_pairs={{0,96},{1,145},{2,98},{3,147},{4,100},{5,149},{6,102},{7,151},{8,1... | collective-permute-start | bytes 589832 | tf_op jit(solution)/shard_map/ppermute | solution.py:38
  46.5 15.7 %collective-permute-start.10 = (bf16[128,768]{1,0:T(8,128)(2,1)S(1)}, bf16[128,768]{1,0:T(8,128)(2,1)S(1)}, u32[]{:S(2)}, u32[]{:S(2)}) collective-permute-start(bf16[128,768]{1,0:T(8,128)(2,1)S(1)} %bitcast.17), channel_id=1, source_target_pairs={{0,32},{1,129},{2,34},{3,131},{4,36},{5,133},{6,38},{7,135},{8,40}... | collective-permute-start | bytes 589832 | tf_op jit(solution)/shard_map/ppermute | solution.py:38
  47.2 14.9 %collective-permute-start.11 = (bf16[128,768]{1,0:T(8,128)(2,1)S(1)}, bf16[128,768]{1,0:T(8,128)(2,1)S(1)}, u32[]{:S(2)}, u32[]{:S(2)}) collective-permute-start(bf16[128,768]{1,0:T(8,128)(2,1)S(1)} %bitcast.18), channel_id=1, source_target_pairs={{0,64},{1,17},{2,66},{3,19},{4,68},{5,21},{6,70},{7,23},{8,72},{9,... | collective-permute-start | bytes 589832 | tf_op jit(solution)/shard_map/ppermute | solution.py:38
  50.3 11.8 %collective-permute-start.12 = (bf16[128,768]{1,0:T(8,128)(2,1)S(1)}, bf16[128,768]{1,0:T(8,128)(2,1)S(1)}, u32[]{:S(2)}, u32[]{:S(2)}) collective-permute-start(bf16[128,768]{1,0:T(8,128)(2,1)S(1)} %bitcast.19), channel_id=1, source_target_pairs={{0,96},{1,145},{2,98},{3,147},{4,100},{5,149},{6,102},{7,151},{8,1... | collective-permute-start | bytes 589832 | tf_op jit(solution)/shard_map/ppermute | solution.py:38
  55.7 7.2 %collective-permute-start.9 = (f32[2,2048]{1,0:T(2,128)S(1)}, f32[2,2048]{1,0:T(2,128)S(1)}, u32[]{:S(2)}, u32[]{:S(2)}) collective-permute-start(f32[2,2048]{1,0:T(2,128)S(1)} %shard_map.63.best_ref), channel_id=1, source_target_pairs={{0,1},{1,0},{2,3},{3,2},{4,5},{5,4},{6,7},{7,6},{8,9},{9,8},{10,11... | collective-permute-start | bytes 49160 | tf_op jit(solution)/shard_map/ppermute | solution.py:34
  67.1 16.6 %all-to-all-start.1 = ((f32[128,1,32]{2,1,0:T(1,128)}), f32[128,1,32]{2,1,0:T(1,128)S(1)}, u32[]{:S(2)}, u32[]{:S(2)}) async-start(f32[128,1,32]{2,1,0:T(1,128)} %bitcast.10), calls=%async_computation.1 | async-start | bytes 131072 | tf_op jit(solution)/shard_map/all_to_all | solution.py:231

commit v11 on v8

--- a/solution.py
+++ b/solution.py
@@ -40,6 +40,12 @@
         AXES,
         pairs_of(lambda y, x, z, c: (y, x ^ mask, z, c) if (c == 0) == first else (y ^ mask, x, z, c)),
     )
+
+
+def ring_of(piece):
+    near, back = turn(piece, 1, False), turn(piece, 3, False)
+    across = [turn(back[:64], 1, False), turn(near[64:], 3, False)]
+    return [piece, near, jnp.concatenate(across), back]
 
 
 def turned_table(pieces, turned):
@@ -218,8 +224,7 @@
     block = settled(got)
     line = jnp.stack([block] + [turn(block, s, True) for s in (1, 2, 3)])
     cands, chosen = line[:, :32].reshape(128, width), line[:, 32:].reshape(128, width)
-    chosen = [chosen] + [turn(chosen, s, False) for s in (1, 2, 3)]
-    cands = [cands] + [turn(cands, s, False) for s in (1, 2, 3)]
+    chosen, cands = ring_of(chosen), ring_of(cands)
 
     table = [pltpu.VMEM((width, 256), jnp.bfloat16)]
     best = coverage.reshape(1, rows)

time: 85 us -> 90.2 us (1.061)
  starting transfers between devices: 28.9 us -> 32 us
  waiting for transfers between devices: 21.5 us -> 23.9 us
    ppermute x4, starting transfers between devices: 11 us -> 13.6 us  [swap(): lax.ppermute(value, AXES, pairs_of(lambda y, x, z, c: (y ^ y_mask, x, z,...]
    ppermute x9 -> x11, waiting for transfers between devices: 6.15 us -> 8.57 us  [turn(): lax.ppermute(value, AXES, pairs_of(lambda y, x, z, c: (y, x ^ mask, z, c)...]
    ppermute x9 -> x11, starting transfers between devices: 11.8 us -> 12.2 us  [turn(): lax.ppermute(value, AXES, pairs_of(lambda y, x, z, c: (y, x ^ mask, z, c)...]
  transfers between devices with their start and end apart: 14 -> 16, of which waited for: 8 -> 9; matrix products, arithmetic and copies ran while one was open for 0% -> 0% of each run, Pallas kernels for 5% -> 5%
where the time goes in v11:
time: 90.2 us; the launch traced here: 90 us
  starting transfers between devices  32 us (35%)
  waiting for transfers between devices  23.9 us (26%)
  blocking collectives  20.7 us (23%)
  Pallas kernels  9.48 us (11%)
  local copies, waits for them, and re-layouts  1.6 us (2%)
  other arithmetic  1.56 us (2%)
    all_to_all x1, blocking collectives, local(): lax.all_to_all(jnp.broadcast_to(send, (8, 32 + MOST, width)), 'z', 0, 0)  20.7 us
    ppermute x4, starting transfers between devices, swap(): lax.ppermute(value, AXES, pairs_of(lambda y, x, z, c: (y ^ y_mask, x, z,...  13.6 us
    ppermute x11, starting transfers between devices, turn(): lax.ppermute(value, AXES, pairs_of(lambda y, x, z, c: (y, x ^ mask, z, c)...  12.2 us
    all_to_all x1, waiting for transfers between devices, local(): parts = lax.all_to_all(part, CHIPS, 0, 0, tiled=True)  10.6 us
    ppermute x11, waiting for transfers between devices, turn(): lax.ppermute(value, AXES, pairs_of(lambda y, x, z, c: (y, x ^ mask, z, c)...  8.57 us
    pallas_call x3, Pallas kernels, on_chip(): pl.pallas_call(kernel, out_shape=[jax.ShapeDtypeStruct(out, jnp.float32)...  8.14 us
    all_to_all x1, starting transfers between devices, local(): parts = lax.all_to_all(part, CHIPS, 0, 0, tiled=True)  6.17 us
    ppermute x4, waiting for transfers between devices, swap(): lax.ppermute(value, AXES, pairs_of(lambda y, x, z, c: (y ^ y_mask, x, z,...  4.76 us
  transfers between devices with their start and end apart: 16, of which 9 were waited for; matrix products, arithmetic and copies ran while one was open for 0% of the time, Pallas kernels for 5%

profile of v11, /device:TPU:1, one launch (start us, length us, event | category | flops | bytes accessed | tf_op | source)
XLA Modules:
  0.0 90.0 jit_solution(9851115378902709241)
XLA Ops:
  1.7 1.5 %copy-done = bf16[2048,768]{1,0:T(8,128)(2,1)S(1)} copy-done((bf16[2048,768]{1,0:T(8,128)(2,1)S(1)}, bf16[2048,768]{1,0:T(8,128)(2,1)}, u32[]{:S(2)}) %copy-start) | copy-done | bytes 3145752
  3.9 3.3 %collective-permute-start = (bf16[64,768]{1,0:T(8,128)(2,1)S(1)}, bf16[64,768]{1,0:T(8,128)(2,1)S(1)}, u32[]{:S(2)}, u32[]{:S(2)}) collective-permute-start(bf16[64,768]{1,0:T(8,128)(2,1)S(1)} %get-tuple-element.10), channel_id=1, source_target_pairs={{0,1},{1,0},{2,3},{3,2},{4,5},{5,4},{6,7},{7,6},{8,9},{9,8},{10,11... | collective-permute-start | bytes 294920 | tf_op jit(solution)/shard_map/ppermute | solution.py:34
  7.2 0.9 %collective-permute-done = bf16[64,768]{1,0:T(8,128)(2,1)S(1)} collective-permute-done((bf16[64,768]{1,0:T(8,128)(2,1)S(1)}, bf16[64,768]{1,0:T(8,128)(2,1)S(1)}, u32[]{:S(2)}, u32[]{:S(2)}) %collective-permute-start) | collective-permute-done | bytes 98336 | tf_op jit(solution)/shard_map/ppermute | solution.py:34
  8.6 1.2 %collective-permute-start.1 = (bf16[32,768]{1,0:T(8,128)(2,1)S(1)}, bf16[32,768]{1,0:T(8,128)(2,1)S(1)}, u32[]{:S(2)}, u32[]{:S(2)}) collective-permute-start(bf16[32,768]{1,0:T(8,128)(2,1)S(1)} %slice.25), channel_id=1, source_target_pairs={{0,16},{1,17},{2,18},{3,19},{4,20},{5,21},{6,22},{7,23},{8,24},{9,... | collective-permute-start | bytes 147464 | tf_op jit(solution)/shard_map/ppermute | solution.py:34
  9.8 3.3 %collective-permute-done.1 = bf16[32,768]{1,0:T(8,128)(2,1)S(1)} collective-permute-done((bf16[32,768]{1,0:T(8,128)(2,1)S(1)}, bf16[32,768]{1,0:T(8,128)(2,1)S(1)}, u32[]{:S(2)}, u32[]{:S(2)}) %collective-permute-start.1) | collective-permute-done | bytes 49184 | tf_op jit(solution)/shard_map/ppermute | solution.py:34
  13.1 20.7 %all_to_all.14.got_ref = bf16[8,36,768]{2,1,0:T(8,128)(2,1)S(1)} all-to-all(bf16[8,36,768]{2,1,0:T(8,128)(2,1)S(1)} %broadcast_in_dim.3), channel_id=1, replica_groups=mesh['ylo'=2,'x'=4,'yhi'=2,'z'=8,'core'=2] {'z'}, dimensions={0} | all-to-all | bytes 884736 | tf_op jit(solution)/shard_map/all_to_all | solution.py:223
  33.9 1.4 %collective-permute-start.2 = (bf16[64,768]{1,0:T(8,128)(2,1)S(1)}, bf16[64,768]{1,0:T(8,128)(2,1)S(1)}, u32[]{:S(2)}, u32[]{:S(2)}) collective-permute-start(bf16[64,768]{1,0:T(8,128)(2,1)S(1)} %shard_map.61), channel_id=1, source_target_pairs={{0,32},{1,129},{2,34},{3,131},{4,36},{5,133},{6,38},{7,135},{8,40}... | collective-permute-start | bytes 294920 | tf_op jit(solution)/shard_map/ppermute | solution.py:38
  35.3 2.6 %collective-permute-start.3 = (bf16[64,768]{1,0:T(8,128)(2,1)S(1)}, bf16[64,768]{1,0:T(8,128)(2,1)S(1)}, u32[]{:S(2)}, u32[]{:S(2)}) collective-permute-start(bf16[64,768]{1,0:T(8,128)(2,1)S(1)} %shard_map.61), channel_id=1, source_target_pairs={{0,64},{1,17},{2,66},{3,19},{4,68},{5,21},{6,70},{7,23},{8,72},{9,... | collective-permute-start | bytes 294920 | tf_op jit(solution)/shard_map/ppermute | solution.py:38
  38.0 3.0 %collective-permute-done.3 = bf16[64,768]{1,0:T(8,128)(2,1)S(1)} collective-permute-done((bf16[64,768]{1,0:T(8,128)(2,1)S(1)}, bf16[64,768]{1,0:T(8,128)(2,1)S(1)}, u32[]{:S(2)}, u32[]{:S(2)}) %collective-permute-start.3) | collective-permute-done | bytes 98336 | tf_op jit(solution)/shard_map/ppermute | solution.py:38
  41.0 1.6 %collective-permute-done.4 = bf16[64,768]{1,0:T(8,128)(2,1)S(1)} collective-permute-done((bf16[64,768]{1,0:T(8,128)(2,1)S(1)}, bf16[64,768]{1,0:T(8,128)(2,1)S(1)}, u32[]{:S(2)}, u32[]{:S(2)}) %collective-permute-start.4) | collective-permute-done | bytes 98336 | tf_op jit(solution)/shard_map/ppermute | solution.py:38
  42.7 2.9 %collective-permute-start.7 = (bf16[128,768]{1,0:T(8,128)(2,1)S(1)}, bf16[128,768]{1,0:T(8,128)(2,1)S(1)}, u32[]{:S(2)}, u32[]{:S(2)}) collective-permute-start(bf16[128,768]{1,0:T(8,128)(2,1)S(1)} %bitcast.13), channel_id=1, source_target_pairs={{0,144},{1,97},{2,146},{3,99},{4,148},{5,101},{6,150},{7,103},{8,1... | collective-permute-start | bytes 589832 | tf_op jit(solution)/shard_map/ppermute | solution.py:38
  46.2 0.8 collective-permute-start.11
  47.0 1.7 %collective-permute-done.7.c1 = bf16[128,768]{1,0:T(8,128)(2,1)S(1)} collective-permute-done((bf16[128,768]{1,0:T(8,128)(2,1)S(1)}, bf16[128,768]{1,0:T(8,128)(2,1)S(1)}, u32[]{:S(2)}, u32[]{:S(2)}) %collective-permute-start.7) | collective-permute-done | bytes 196640 | tf_op jit(solution)/shard_map/ppermute | solution.py:38
  48.9 1.2 %collective-permute-done.5.c1 = bf16[128,768]{1,0:T(8,128)(2,1)S(1)} collective-permute-done((bf16[128,768]{1,0:T(8,128)(2,1)S(1)}, bf16[128,768]{1,0:T(8,128)(2,1)S(1)}, u32[]{:S(2)}, u32[]{:S(2)}) %collective-permute-start.5) | collective-permute-done | bytes 196640 | tf_op jit(solution)/shard_map/ppermute | solution.py:38
  50.1 1.4 %collective-permute-start.9 = (bf16[64,768]{1,0:T(8,128)(2,1)S(1)}, bf16[64,768]{1,0:T(8,128)(2,1)S(1)}, u32[]{:S(2)}, u32[]{:S(2)}) collective-permute-start(bf16[64,768]{1,0:T(8,128)(2,1)S(1)} %slice.34), channel_id=1, source_target_pairs={{0,144},{1,97},{2,146},{3,99},{4,148},{5,101},{6,150},{7,103},{8,1... | collective-permute-start | bytes 294920 | tf_op jit(solution)/shard_map/ppermute | solution.py:38
  51.5 0.9 %collective-permute-start.13 = (bf16[64,768]{1,0:T(8,128)(2,1)S(1)}, bf16[64,768]{1,0:T(8,128)(2,1)S(1)}, u32[]{:S(2)}, u32[]{:S(2)}) collective-permute-start(bf16[64,768]{1,0:T(8,128)(2,1)S(1)} %slice.36), channel_id=1, source_target_pairs={{0,128},{1,33},{2,130},{3,35},{4,132},{5,37},{6,134},{7,39},{8,136... | collective-permute-start | bytes 294920 | tf_op jit(solution)/shard_map/ppermute | solution.py:38
  52.5 1.4 %collective-permute-start.14 = (bf16[64,768]{1,0:T(8,128)(2,1)S(1)}, bf16[64,768]{1,0:T(8,128)(2,1)S(1)}, u32[]{:S(2)}, u32[]{:S(2)}) collective-permute-start(bf16[64,768]{1,0:T(8,128)(2,1)S(1)} %slice.37), channel_id=1, source_target_pairs={{0,144},{1,97},{2,146},{3,99},{4,148},{5,101},{6,150},{7,103},{8,1... | collective-permute-start | bytes 294920 | tf_op jit(solution)/shard_map/ppermute | solution.py:38
  53.9 0.9 %collective-permute-done.9 = bf16[64,768]{1,0:T(8,128)(2,1)S(1)} collective-permute-done((bf16[64,768]{1,0:T(8,128)(2,1)S(1)}, bf16[64,768]{1,0:T(8,128)(2,1)S(1)}, u32[]{:S(2)}, u32[]{:S(2)}) %collective-permute-start.9) | collective-permute-done | bytes 98336 | tf_op jit(solution)/shard_map/ppermute | solution.py:38
  54.9 2.0 %shard_map.62.floor_ref = f32[2,2048]{1,0:T(2,128)S(1)} custom-call(bf16[2048,768]{1,0:T(8,128)(2,1)S(1)} %copy-done, f32[1,2048]{1,0:T(1,128)S(1)} %bitcast.20, bf16[128,768]{1,0:T(8,128)(2,1)S(1)} %bitcast.15, bf16[128,768]{1,0:T(8,128)(2,1)S(1)} %collective-permute-done.5.c1, bf16[2048,768]{1,0:T(8,128)(2,1)S(1)} %collective-permute-done.6.partner_ref), custom_call_target="tpu_custom_call" | custom-call | flops 1610612736 | bytes 8388608 | tf_op jit(solution)/shard_map/pallas_call | solution.py:122
  56.9 2.0 %shard_map.63.best_ref = f32[2,2048]{1,0:T(2,128)S(1)} custom-call(bf16[2048,768]{1,0:T(8,128)(2,1)S(1)} %copy-done, f32[2,2048]{1,0:T(2,128)S(1)} %shard_map.62.floor_ref, bf16[128,768]{1,0:T(8,128)(2,1)S(1)} %pad_maximum_fusion.1.c0, bf16[128,768]{1,0:T(8,128)(2,1)S(1)} %collective-permute-done.7.c1, bf16[2048,768]{1,0:T(8,128)(2,1)S(1)} %collective-permute-done.6.partner_ref), custom_call_target="tpu_custom_call" | custom-call | flops 1610612736 | bytes 8388608 | tf_op jit(solution)/shard_map/pallas_call | solution.py:122
  58.9 8.6 %collective-permute-start.10 = (f32[2,2048]{1,0:T(2,128)S(1)}, f32[2,2048]{1,0:T(2,128)S(1)}, u32[]{:S(2)}, u32[]{:S(2)}) collective-permute-start(f32[2,2048]{1,0:T(2,128)S(1)} %shard_map.63.best_ref), channel_id=1, source_target_pairs={{0,1},{1,0},{2,3},{3,2},{4,5},{5,4},{6,7},{7,6},{8,9},{9,8},{10,11... | collective-permute-start | bytes 49160 | tf_op jit(solution)/shard_map/ppermute | solution.py:34
  68.4 4.1 %shard_map.65 = (f32[128,32]{1,0:T(8,128)}, f32[1,2048]{1,0:T(1,128)}) custom-call(bf16[2048,768]{1,0:T(8,128)(2,1)S(1)} %copy-done, f32[2,2048]{1,0:T(2,128)S(1)} %shard_map.63.best_ref, f32[2,2048]{1,0:T(2,128)S(1)} %collective-permute-done.10.other_ref, bf16[768,512]{1,0:T(8,128)(2,1)S(1)} %shard_map.64.turned, ...), custom_call_target="tpu_custom_call" | custom-call | flops 3221225472 | bytes 8388608 | tf_op jit(solution)/shard_map/pallas_call | solution.py:122
  72.5 6.2 %all-to-all-start.1 = ((f32[128,1,32]{2,1,0:T(1,128)}), f32[128,1,32]{2,1,0:T(1,128)S(1)}, u32[]{:S(2)}, u32[]{:S(2)}) async-start(f32[128,1,32]{2,1,0:T(1,128)} %bitcast.10), calls=%async_computation.1 | async-start | bytes 131072 | tf_op jit(solution)/shard_map/all_to_all | solution.py:236
  78.7 10.6 %all-to-all-done.1 = f32[128,1,32]{2,1,0:T(1,128)S(1)} async-done(((f32[128,1,32]{2,1,0:T(1,128)}), f32[128,1,32]{2,1,0:T(1,128)S(1)}, u32[]{:S(2)}, u32[]{:S(2)}) %all-to-all-start.1) | async-done | bytes 16416 | tf_op jit(solution)/shard_map/all_to_all | solution.py:236
  (35 shorter events, 4.8 us)
Async XLA Ops:
  1.3 1.9 %copy-start = (bf16[2048,768]{1,0:T(8,128)(2,1)S(1)}, bf16[2048,768]{1,0:T(8,128)(2,1)}, u32[]{:S(2)}) copy-start(bf16[2048,768]{1,0:T(8,128)(2,1)} %own_ref.5) | copy-start | bytes 9437188
  3.9 51.0 %copy-start.1 = (f32[2048]{0:T(1024)S(1)}, f32[2048]{0:T(1024)}, u32[]{:S(2)}) copy-start(f32[2048]{0:T(1024)} %param.5) | copy-start | bytes 24580
  3.9 4.3 %collective-permute-start = (bf16[64,768]{1,0:T(8,128)(2,1)S(1)}, bf16[64,768]{1,0:T(8,128)(2,1)S(1)}, u32[]{:S(2)}, u32[]{:S(2)}) collective-permute-start(bf16[64,768]{1,0:T(8,128)(2,1)S(1)} %get-tuple-element.10), channel_id=1, source_target_pairs={{0,1},{1,0},{2,3},{3,2},{4,5},{5,4},{6,7},{7,6},{8,9},{9,8},{10,11... | collective-permute-start | bytes 294920 | tf_op jit(solution)/shard_map/ppermute | solution.py:34
  8.2 46.7 %collective-permute-start.6 = (bf16[2048,768]{1,0:T(8,128)(2,1)S(1)}, bf16[2048,768]{1,0:T(8,128)(2,1)S(1)}, u32[]{:S(2)}, u32[]{:S(2)}) collective-permute-start(bf16[2048,768]{1,0:T(8,128)(2,1)S(1)} %copy-done), channel_id=1, source_target_pairs={{0,1},{1,0},{2,3},{3,2},{4,5},{5,4},{6,7},{7,6},{8,9},{9,8},{10,11... | collective-permute-start | bytes 9437192 | tf_op jit(solution)/shard_map/ppermute | solution.py:34
  8.6 4.4 %collective-permute-start.1 = (bf16[32,768]{1,0:T(8,128)(2,1)S(1)}, bf16[32,768]{1,0:T(8,128)(2,1)S(1)}, u32[]{:S(2)}, u32[]{:S(2)}) collective-permute-start(bf16[32,768]{1,0:T(8,128)(2,1)S(1)} %slice.25), channel_id=1, source_target_pairs={{0,16},{1,17},{2,18},{3,19},{4,20},{5,21},{6,22},{7,23},{8,24},{9,... | collective-permute-start | bytes 147464 | tf_op jit(solution)/shard_map/ppermute | solution.py:34
  33.9 4.0 %collective-permute-start.2 = (bf16[64,768]{1,0:T(8,128)(2,1)S(1)}, bf16[64,768]{1,0:T(8,128)(2,1)S(1)}, u32[]{:S(2)}, u32[]{:S(2)}) collective-permute-start(bf16[64,768]{1,0:T(8,128)(2,1)S(1)} %shard_map.61), channel_id=1, source_target_pairs={{0,32},{1,129},{2,34},{3,131},{4,36},{5,133},{6,38},{7,135},{8,40}... | collective-permute-start | bytes 294920 | tf_op jit(solution)/shard_map/ppermute | solution.py:38
  35.3 5.7 %collective-permute-start.3 = (bf16[64,768]{1,0:T(8,128)(2,1)S(1)}, bf16[64,768]{1,0:T(8,128)(2,1)S(1)}, u32[]{:S(2)}, u32[]{:S(2)}) collective-permute-start(bf16[64,768]{1,0:T(8,128)(2,1)S(1)} %shard_map.61), channel_id=1, source_target_pairs={{0,64},{1,17},{2,66},{3,19},{4,68},{5,21},{6,70},{7,23},{8,72},{9,... | collective-permute-start | bytes 294920 | tf_op jit(solution)/shard_map/ppermute | solution.py:38
  37.9 4.7 %collective-permute-start.4 = (bf16[64,768]{1,0:T(8,128)(2,1)S(1)}, bf16[64,768]{1,0:T(8,128)(2,1)S(1)}, u32[]{:S(2)}, u32[]{:S(2)}) collective-permute-start(bf16[64,768]{1,0:T(8,128)(2,1)S(1)} %shard_map.61), channel_id=1, source_target_pairs={{0,96},{1,145},{2,98},{3,147},{4,100},{5,149},{6,102},{7,151},{8,1... | collective-permute-start | bytes 294920 | tf_op jit(solution)/shard_map/ppermute | solution.py:38
  42.7 6.0 %collective-permute-start.7 = (bf16[128,768]{1,0:T(8,128)(2,1)S(1)}, bf16[128,768]{1,0:T(8,128)(2,1)S(1)}, u32[]{:S(2)}, u32[]{:S(2)}) collective-permute-start(bf16[128,768]{1,0:T(8,128)(2,1)S(1)} %bitcast.13), channel_id=1, source_target_pairs={{0,144},{1,97},{2,146},{3,99},{4,148},{5,101},{6,150},{7,103},{8,1... | collective-permute-start | bytes 589832 | tf_op jit(solution)/shard_map/ppermute | solution.py:38
  45.6 4.5 %collective-permute-start.5 = (bf16[128,768]{1,0:T(8,128)(2,1)S(1)}, bf16[128,768]{1,0:T(8,128)(2,1)S(1)}, u32[]{:S(2)}, u32[]{:S(2)}) collective-permute-start(bf16[128,768]{1,0:T(8,128)(2,1)S(1)} %bitcast.14), channel_id=1, source_target_pairs={{0,128},{1,33},{2,130},{3,35},{4,132},{5,37},{6,134},{7,39},{8,136... | collective-permute-start | bytes 589832 | tf_op jit(solution)/shard_map/ppermute | solution.py:38
  45.6 6.0 %collective-permute-start.12 = (bf16[128,768]{1,0:T(8,128)(2,1)S(1)}, bf16[128,768]{1,0:T(8,128)(2,1)S(1)}, u32[]{:S(2)}, u32[]{:S(2)}) collective-permute-start(bf16[128,768]{1,0:T(8,128)(2,1)S(1)} %bitcast.16), channel_id=1, source_target_pairs={{0,144},{1,97},{2,146},{3,99},{4,148},{5,101},{6,150},{7,103},{8,1... | collective-permute-start | bytes 589832 | tf_op jit(solution)/shard_map/ppermute | solution.py:38
  46.2 6.2 %collective-permute-start.11 = (bf16[128,768]{1,0:T(8,128)(2,1)S(1)}, bf16[128,768]{1,0:T(8,128)(2,1)S(1)}, u32[]{:S(2)}, u32[]{:S(2)}) collective-permute-start(bf16[128,768]{1,0:T(8,128)(2,1)S(1)} %bitcast.17), channel_id=1, source_target_pairs={{0,128},{1,33},{2,130},{3,35},{4,132},{5,37},{6,134},{7,39},{8,136... | collective-permute-start | bytes 589832 | tf_op jit(solution)/shard_map/ppermute | solution.py:38
  48.8 5.2 %collective-permute-start.8 = (bf16[64,768]{1,0:T(8,128)(2,1)S(1)}, bf16[64,768]{1,0:T(8,128)(2,1)S(1)}, u32[]{:S(2)}, u32[]{:S(2)}) collective-permute-start(bf16[64,768]{1,0:T(8,128)(2,1)S(1)} %slice.33), channel_id=1, source_target_pairs={{0,128},{1,33},{2,130},{3,35},{4,132},{5,37},{6,134},{7,39},{8,136... | collective-permute-start | bytes 294920 | tf_op jit(solution)/shard_map/ppermute | solution.py:38
  50.1 4.8 %collective-permute-start.9 = (bf16[64,768]{1,0:T(8,128)(2,1)S(1)}, bf16[64,768]{1,0:T(8,128)(2,1)S(1)}, u32[]{:S(2)}, u32[]{:S(2)}) collective-permute-start(bf16[64,768]{1,0:T(8,128)(2,1)S(1)} %slice.34), channel_id=1, source_target_pairs={{0,144},{1,97},{2,146},{3,99},{4,148},{5,101},{6,150},{7,103},{8,1... | collective-permute-start | bytes 294920 | tf_op jit(solution)/shard_map/ppermute | solution.py:38
  51.5 16.0 %collective-permute-start.13 = (bf16[64,768]{1,0:T(8,128)(2,1)S(1)}, bf16[64,768]{1,0:T(8,128)(2,1)S(1)}, u32[]{:S(2)}, u32[]{:S(2)}) collective-permute-start(bf16[64,768]{1,0:T(8,128)(2,1)S(1)} %slice.36), channel_id=1, source_target_pairs={{0,128},{1,33},{2,130},{3,35},{4,132},{5,37},{6,134},{7,39},{8,136... | collective-permute-start | bytes 294920 | tf_op jit(solution)/shard_map/ppermute | solution.py:38
  52.5 15.0 %collective-permute-start.14 = (bf16[64,768]{1,0:T(8,128)(2,1)S(1)}, bf16[64,768]{1,0:T(8,128)(2,1)S(1)}, u32[]{:S(2)}, u32[]{:S(2)}) collective-permute-start(bf16[64,768]{1,0:T(8,128)(2,1)S(1)} %slice.37), channel_id=1, source_target_pairs={{0,144},{1,97},{2,146},{3,99},{4,148},{5,101},{6,150},{7,103},{8,1... | collective-permute-start | bytes 294920 | tf_op jit(solution)/shard_map/ppermute | solution.py:38
  58.9 9.5 %collective-permute-start.10 = (f32[2,2048]{1,0:T(2,128)S(1)}, f32[2,2048]{1,0:T(2,128)S(1)}, u32[]{:S(2)}, u32[]{:S(2)}) collective-permute-start(f32[2,2048]{1,0:T(2,128)S(1)} %shard_map.63.best_ref), channel_id=1, source_target_pairs={{0,1},{1,0},{2,3},{3,2},{4,5},{5,4},{6,7},{7,6},{8,9},{9,8},{10,11... | collective-permute-start | bytes 49160 | tf_op jit(solution)/shard_map/ppermute | solution.py:34
  72.5 16.8 %all-to-all-start.1 = ((f32[128,1,32]{2,1,0:T(1,128)}), f32[128,1,32]{2,1,0:T(1,128)S(1)}, u32[]{:S(2)}, u32[]{:S(2)}) async-start(f32[128,1,32]{2,1,0:T(1,128)} %bitcast.10), calls=%async_computation.1 | async-start | bytes 131072 | tf_op jit(solution)/shard_map/all_to_all | solution.py:236

commit v12 on v9

--- a/solution.py
+++ b/solution.py
@@ -75,27 +75,33 @@
         for start in range(0, rows, STEP):
             sims = tile_sims(table, turned, start)
             for r in range(0, STEP, 128):
-                line = floors(t, pl.ds(start + r, 128))
-                floor = jnp.broadcast_to(line * width**0.5, (128, 128)).T
+                floor = floors(t, start + r)
                 over = jnp.maximum(sims[r : r + 128] - jnp.concatenate([floor] * 2, axis=1), 0.0)
                 total = total + jnp.sum(over.reshape(16, 8, 256), axis=0)
     return jnp.sum(total, axis=0, keepdims=True) / width**0.5
 
 
-def near_gain_kernel(own_ref, best_ref, other_ref, c0, c1, partner_ref, sums_ref, cover_ref, turned):
-    def floors(t, here):
+def near_gain_kernel(own_ref, best_ref, other_ref, c0, c1, partner_ref, sums_ref, cover_ref, floor_ref, turned):
+    rows, width = own_ref.shape
+
+    def floors(t, start):
+        here = pl.ds(start, 128)
         line = jnp.maximum(best_ref[t : t + 1, here], other_ref[1 - t : 2 - t, here])
         if t == 0:
             cover_ref[:, here] = line
-        return line
+        floor = jnp.broadcast_to(line * width**0.5, (128, 128)).T
+        floor_ref[pl.ds(t * rows + start, 128), :] = floor
+        return floor
 
     sums = gains_over((own_ref, partner_ref), floors, (c0, c1), turned)
     sums_ref[...] = jnp.broadcast_to(sums, (8, 256))
 
 
-def far_gain_kernel(own_ref, best_ref, other_ref, sums_ref, c0, c1, partner_ref, gain_ref, turned):
-    def floors(t, here):
-        return jnp.maximum(best_ref[t : t + 1, here], other_ref[1 - t : 2 - t, here])
+def far_gain_kernel(own_ref, floor_ref, sums_ref, c0, c1, partner_ref, gain_ref, turned):
+    rows = own_ref.shape[0]
+
+    def floors(t, start):
+        return floor_ref[pl.ds(t * rows + start, 128), :]
 
     far = gains_over((own_ref, partner_ref), floors, (c0, c1), turned)
     halves = (sums_ref[:1, :], far)
@@ -226,10 +232,10 @@
     for pieces in (chosen[:2], chosen[2:]):
         best = on_chip(best_kernel, [(2, rows)], table, 2, embeddings, best, *pieces, partner)[0]
     other = swap(best, 0, 1)
-    sums, cover = on_chip(
-        near_gain_kernel, [(8, 256), (1, rows)], table, 2, embeddings, best, other, *cands[:2], partner
+    sums, cover, floor = on_chip(
+        near_gain_kernel, [(8, 256), (1, rows), (2 * rows, 128)], table, 2, embeddings, best, other, *cands[:2], partner
     )
-    part = on_chip(far_gain_kernel, [(128, 32)], table, 2, embeddings, best, other, sums, *cands[2:], partner)[0]
+    part = on_chip(far_gain_kernel, [(128, 32)], table, 2, embeddings, floor, sums, *cands[2:], partner)[0]
     parts = lax.all_to_all(part, CHIPS, 0, 0, tiled=True)
     gains = jnp.sum(lax.dynamic_slice_in_dim(parts, lax.axis_index("z") * 4, 4, 1), axis=0)
     return cover[0], gains

time: 85.6 us -> 86.3 us (level)
    all_to_all x1, starting transfers between devices: 6.06 us -> 7.52 us  [local(): parts = lax.all_to_all(part, CHIPS, 0, 0, tiled=True)]
    ppermute x9, starting transfers between devices: 11.8 us -> 10.6 us  [turn(): lax.ppermute(value, AXES, pairs_of(lambda y, x, z, c: (y, x ^ mask, z, c)...]
where the time goes in v12:
time: 86.3 us; the launch traced here: 86.1 us
  starting transfers between devices  29.6 us (34%)
  waiting for transfers between devices  21.8 us (25%)
  blocking collectives  20.7 us (24%)
  Pallas kernels  10.1 us (12%)
  local copies, waits for them, and re-layouts  1.57 us (2%)
  other arithmetic  1.53 us (2%)
    all_to_all x1, blocking collectives, local(): lax.all_to_all(jnp.broadcast_to(send, (8, 32 + MOST, width)), 'z', 0, 0)  20.7 us
    ppermute x4, starting transfers between devices, swap(): lax.ppermute(value, AXES, pairs_of(lambda y, x, z, c: (y ^ y_mask, x, z,...  11.4 us
    ppermute x9, starting transfers between devices, turn(): lax.ppermute(value, AXES, pairs_of(lambda y, x, z, c: (y, x ^ mask, z, c)...  10.6 us
    all_to_all x1, waiting for transfers between devices, local(): parts = lax.all_to_all(part, CHIPS, 0, 0, tiled=True)  10.5 us
    pallas_call x4, Pallas kernels, on_chip(): pl.pallas_call(kernel, out_shape=[jax.ShapeDtypeStruct(out, jnp.float32)...  9.05 us
    all_to_all x1, starting transfers between devices, local(): parts = lax.all_to_all(part, CHIPS, 0, 0, tiled=True)  7.52 us
    ppermute x9, waiting for transfers between devices, turn(): lax.ppermute(value, AXES, pairs_of(lambda y, x, z, c: (y, x ^ mask, z, c)...  6.21 us
    ppermute x4, waiting for transfers between devices, swap(): lax.ppermute(value, AXES, pairs_of(lambda y, x, z, c: (y ^ y_mask, x, z,...  5.05 us
  transfers between devices with their start and end apart: 14, of which 8 were waited for; matrix products, arithmetic and copies ran while one was open for 0% of the time, Pallas kernels for 8%

profile of v12, /device:TPU:1, one launch (start us, length us, event | category | flops | bytes accessed | tf_op | source)
XLA Modules:
  0.0 86.1 jit_solution(2184499613740223409)
XLA Ops:
  0.6 0.7 add_bitcast_fusion.index_ref
  1.7 1.5 %copy-done = bf16[2048,768]{1,0:T(8,128)(2,1)S(1)} copy-done((bf16[2048,768]{1,0:T(8,128)(2,1)S(1)}, bf16[2048,768]{1,0:T(8,128)(2,1)}, u32[]{:S(2)}) %copy-start) | copy-done | bytes 3145752
  3.9 3.3 %collective-permute-start = (bf16[64,768]{1,0:T(8,128)(2,1)S(1)}, bf16[64,768]{1,0:T(8,128)(2,1)S(1)}, u32[]{:S(2)}, u32[]{:S(2)}) collective-permute-start(bf16[64,768]{1,0:T(8,128)(2,1)S(1)} %get-tuple-element.11), channel_id=1, source_target_pairs={{0,1},{1,0},{2,3},{3,2},{4,5},{5,4},{6,7},{7,6},{8,9},{9,8},{10,11... | collective-permute-start | bytes 294920 | tf_op jit(solution)/shard_map/ppermute | solution.py:34
  7.2 0.9 %collective-permute-done = bf16[64,768]{1,0:T(8,128)(2,1)S(1)} collective-permute-done((bf16[64,768]{1,0:T(8,128)(2,1)S(1)}, bf16[64,768]{1,0:T(8,128)(2,1)S(1)}, u32[]{:S(2)}, u32[]{:S(2)}) %collective-permute-start) | collective-permute-done | bytes 98336 | tf_op jit(solution)/shard_map/ppermute | solution.py:34
  8.6 1.2 %collective-permute-start.1 = (bf16[32,768]{1,0:T(8,128)(2,1)S(1)}, bf16[32,768]{1,0:T(8,128)(2,1)S(1)}, u32[]{:S(2)}, u32[]{:S(2)}) collective-permute-start(bf16[32,768]{1,0:T(8,128)(2,1)S(1)} %slice.13), channel_id=1, source_target_pairs={{0,16},{1,17},{2,18},{3,19},{4,20},{5,21},{6,22},{7,23},{8,24},{9,... | collective-permute-start | bytes 147464 | tf_op jit(solution)/shard_map/ppermute | solution.py:34
  9.8 3.3 %collective-permute-done.1 = bf16[32,768]{1,0:T(8,128)(2,1)S(1)} collective-permute-done((bf16[32,768]{1,0:T(8,128)(2,1)S(1)}, bf16[32,768]{1,0:T(8,128)(2,1)S(1)}, u32[]{:S(2)}, u32[]{:S(2)}) %collective-permute-start.1) | collective-permute-done | bytes 49184 | tf_op jit(solution)/shard_map/ppermute | solution.py:34
  13.1 20.7 %all_to_all.14.got_ref = bf16[8,36,768]{2,1,0:T(8,128)(2,1)S(1)} all-to-all(bf16[8,36,768]{2,1,0:T(8,128)(2,1)S(1)} %broadcast_in_dim.3), channel_id=1, replica_groups=mesh['ylo'=2,'x'=4,'yhi'=2,'z'=8,'core'=2] {'z'}, dimensions={0} | all-to-all | bytes 884736 | tf_op jit(solution)/shard_map/all_to_all | solution.py:223
  33.9 2.8 %collective-permute-start.4 = (bf16[64,768]{1,0:T(8,128)(2,1)S(1)}, bf16[64,768]{1,0:T(8,128)(2,1)S(1)}, u32[]{:S(2)}, u32[]{:S(2)}) collective-permute-start(bf16[64,768]{1,0:T(8,128)(2,1)S(1)} %shard_map.61), channel_id=1, source_target_pairs={{0,96},{1,145},{2,98},{3,147},{4,100},{5,149},{6,102},{7,151},{8,1... | collective-permute-start | bytes 294920 | tf_op jit(solution)/shard_map/ppermute | solution.py:38
  37.4 1.9 %collective-permute-done.4 = bf16[64,768]{1,0:T(8,128)(2,1)S(1)} collective-permute-done((bf16[64,768]{1,0:T(8,128)(2,1)S(1)}, bf16[64,768]{1,0:T(8,128)(2,1)S(1)}, u32[]{:S(2)}, u32[]{:S(2)}) %collective-permute-start.4) | collective-permute-done | bytes 98336 | tf_op jit(solution)/shard_map/ppermute | solution.py:38
  39.4 2.4 %collective-permute-done.3 = bf16[64,768]{1,0:T(8,128)(2,1)S(1)} collective-permute-done((bf16[64,768]{1,0:T(8,128)(2,1)S(1)}, bf16[64,768]{1,0:T(8,128)(2,1)S(1)}, u32[]{:S(2)}, u32[]{:S(2)}) %collective-permute-start.3) | collective-permute-done | bytes 98336 | tf_op jit(solution)/shard_map/ppermute | solution.py:38
  41.8 1.3 %collective-permute-start.5 = (bf16[128,768]{1,0:T(8,128)(2,1)S(1)}, bf16[128,768]{1,0:T(8,128)(2,1)S(1)}, u32[]{:S(2)}, u32[]{:S(2)}) collective-permute-start(bf16[128,768]{1,0:T(8,128)(2,1)S(1)} %bitcast.17), channel_id=1, source_target_pairs={{0,128},{1,33},{2,130},{3,35},{4,132},{5,37},{6,134},{7,39},{8,136... | collective-permute-start | bytes 589832 | tf_op jit(solution)/shard_map/ppermute | solution.py:38
  43.1 2.4 %collective-permute-start.7 = (bf16[128,768]{1,0:T(8,128)(2,1)S(1)}, bf16[128,768]{1,0:T(8,128)(2,1)S(1)}, u32[]{:S(2)}, u32[]{:S(2)}) collective-permute-start(bf16[128,768]{1,0:T(8,128)(2,1)S(1)} %bitcast.18), channel_id=1, source_target_pairs={{0,16},{1,65},{2,18},{3,67},{4,20},{5,69},{6,22},{7,71},{8,24},{9,... | collective-permute-start | bytes 589832 | tf_op jit(solution)/shard_map/ppermute | solution.py:38
  45.8 1.1 %collective-permute-done.5.c1 = bf16[128,768]{1,0:T(8,128)(2,1)S(1)} collective-permute-done((bf16[128,768]{1,0:T(8,128)(2,1)S(1)}, bf16[128,768]{1,0:T(8,128)(2,1)S(1)}, u32[]{:S(2)}, u32[]{:S(2)}) %collective-permute-start.5) | collective-permute-done | bytes 196640 | tf_op jit(solution)/shard_map/ppermute | solution.py:38
  46.9 2.6 %collective-permute-start.11 = (bf16[128,768]{1,0:T(8,128)(2,1)S(1)}, bf16[128,768]{1,0:T(8,128)(2,1)S(1)}, u32[]{:S(2)}, u32[]{:S(2)}) collective-permute-start(bf16[128,768]{1,0:T(8,128)(2,1)S(1)} %bitcast.14), channel_id=1, source_target_pairs={{0,16},{1,65},{2,18},{3,67},{4,20},{5,69},{6,22},{7,71},{8,24},{9,... | collective-permute-start | bytes 589832 | tf_op jit(solution)/shard_map/ppermute | solution.py:38
  50.1 2.0 %shard_map.62.floor_ref = f32[2,2048]{1,0:T(2,128)S(1)} custom-call(bf16[2048,768]{1,0:T(8,128)(2,1)S(1)} %copy-done, f32[1,2048]{1,0:T(1,128)S(1)} %bitcast.22, bf16[128,768]{1,0:T(8,128)(2,1)S(1)} %bitcast.20, bf16[128,768]{1,0:T(8,128)(2,1)S(1)} %collective-permute-done.5.c1, bf16[2048,768]{1,0:T(8,128)(2,1)S(1)} %collective-permute-done.6.partner_ref), custom_call_target="tpu_custom_call" | custom-call | flops 1610612736 | bytes 8388608 | tf_op jit(solution)/shard_map/pallas_call | solution.py:122
  52.1 0.8 collective-permute-done.8.c1
  52.9 2.0 %shard_map.63.best_ref = f32[2,2048]{1,0:T(2,128)S(1)} custom-call(bf16[2048,768]{1,0:T(8,128)(2,1)S(1)} %copy-done, f32[2,2048]{1,0:T(2,128)S(1)} %shard_map.62.floor_ref, bf16[128,768]{1,0:T(8,128)(2,1)S(1)} %collective-permute-done.7.c0, bf16[128,768]{1,0:T(8,128)(2,1)S(1)} %collective-permute-done.8.c1, ...), custom_call_target="tpu_custom_call" | custom-call | flops 1610612736 | bytes 8388608 | tf_op jit(solution)/shard_map/pallas_call | solution.py:122
  54.8 6.5 %collective-permute-start.9 = (f32[2,2048]{1,0:T(2,128)S(1)}, f32[2,2048]{1,0:T(2,128)S(1)}, u32[]{:S(2)}, u32[]{:S(2)}) collective-permute-start(f32[2,2048]{1,0:T(2,128)S(1)} %shard_map.63.best_ref), channel_id=1, source_target_pairs={{0,1},{1,0},{2,3},{3,2},{4,5},{5,4},{6,7},{7,6},{8,9},{9,8},{10,11... | collective-permute-start | bytes 49160 | tf_op jit(solution)/shard_map/ppermute | solution.py:34
  61.3 0.8 collective-permute-done.9.other_ref
  62.2 2.4 %shard_map.64 = (f32[8,256]{1,0:T(8,128)S(1)}, f32[1,2048]{1,0:T(1,128)}, f32[4096,128]{1,0:T(8,128)S(1)}) custom-call(bf16[2048,768]{1,0:T(8,128)(2,1)S(1)} %copy-done, f32[2,2048]{1,0:T(2,128)S(1)} %shard_map.63.best_ref, f32[2,2048]{1,0:T(2,128)S(1)} %collective-permute-done.9.other_ref, bf16[128,768]{1,0:T(8,128)(2,1)S(1)} %bitcast.16, ...), custom_call_target="tpu_custom_call" | custom-call | flops 1610612736 | bytes 8388608 | tf_op jit(solution)/shard_map/pallas_call | solution.py:122
  64.6 2.6 %shard_map.65 = f32[128,32]{1,0:T(8,128)} custom-call(bf16[2048,768]{1,0:T(8,128)(2,1)S(1)} %copy-done, f32[4096,128]{1,0:T(8,128)S(1)} %get-tuple-element.16.floor_ref, f32[8,256]{1,0:T(8,128)S(1)} %get-tuple-element.17.sums_ref, bf16[128,768]{1,0:T(8,128)(2,1)S(1)} %collective-permute-done.11.c0, bf16[128,768]{1,0:T(8,128)(2,1)S(1)} %collective-permute-done.12.c1, ...), custom_call_target="tpu_custom_call" | custom-call | flops 1610612736 | bytes 8388608 | tf_op jit(solution)/shard_map/pallas_call | solution.py:122
  67.2 7.5 %all-to-all-start.1 = ((f32[128,1,32]{2,1,0:T(1,128)}), f32[128,1,32]{2,1,0:T(1,128)S(1)}, u32[]{:S(2)}, u32[]{:S(2)}) async-start(f32[128,1,32]{2,1,0:T(1,128)} %bitcast.10), calls=%async_computation.1 | async-start | bytes 131072 | tf_op jit(solution)/shard_map/all_to_all | solution.py:239
  74.8 10.5 %all-to-all-done.1 = f32[128,1,32]{2,1,0:T(1,128)S(1)} async-done(((f32[128,1,32]{2,1,0:T(1,128)}), f32[128,1,32]{2,1,0:T(1,128)S(1)}, u32[]{:S(2)}, u32[]{:S(2)}) %all-to-all-start.1) | async-done | bytes 16416 | tf_op jit(solution)/shard_map/all_to_all | solution.py:239
  85.3 0.7 dynamic-slice_reduce_fusion
  (25 shorter events, 3.2 us)
Async XLA Ops:
  1.3 1.9 %copy-start = (bf16[2048,768]{1,0:T(8,128)(2,1)S(1)}, bf16[2048,768]{1,0:T(8,128)(2,1)}, u32[]{:S(2)}) copy-start(bf16[2048,768]{1,0:T(8,128)(2,1)} %own_ref.7) | copy-start | bytes 9437188
  3.2 46.8 %copy-start.1 = (f32[2048]{0:T(1024)S(1)}, f32[2048]{0:T(1024)}, u32[]{:S(2)}) copy-start(f32[2048]{0:T(1024)} %param.5) | copy-start | bytes 24580
  3.9 4.3 %collective-permute-start = (bf16[64,768]{1,0:T(8,128)(2,1)S(1)}, bf16[64,768]{1,0:T(8,128)(2,1)S(1)}, u32[]{:S(2)}, u32[]{:S(2)}) collective-permute-start(bf16[64,768]{1,0:T(8,128)(2,1)S(1)} %get-tuple-element.11), channel_id=1, source_target_pairs={{0,1},{1,0},{2,3},{3,2},{4,5},{5,4},{6,7},{7,6},{8,9},{9,8},{10,11... | collective-permute-start | bytes 294920 | tf_op jit(solution)/shard_map/ppermute | solution.py:34
  8.2 41.3 %collective-permute-start.6 = (bf16[2048,768]{1,0:T(8,128)(2,1)S(1)}, bf16[2048,768]{1,0:T(8,128)(2,1)S(1)}, u32[]{:S(2)}, u32[]{:S(2)}) collective-permute-start(bf16[2048,768]{1,0:T(8,128)(2,1)S(1)} %copy-done), channel_id=1, source_target_pairs={{0,1},{1,0},{2,3},{3,2},{4,5},{5,4},{6,7},{7,6},{8,9},{9,8},{10,11... | collective-permute-start | bytes 9437192 | tf_op jit(solution)/shard_map/ppermute | solution.py:34
  8.6 4.4 %collective-permute-start.1 = (bf16[32,768]{1,0:T(8,128)(2,1)S(1)}, bf16[32,768]{1,0:T(8,128)(2,1)S(1)}, u32[]{:S(2)}, u32[]{:S(2)}) collective-permute-start(bf16[32,768]{1,0:T(8,128)(2,1)S(1)} %slice.13), channel_id=1, source_target_pairs={{0,16},{1,17},{2,18},{3,19},{4,20},{5,21},{6,22},{7,23},{8,24},{9,... | collective-permute-start | bytes 147464 | tf_op jit(solution)/shard_map/ppermute | solution.py:34
  33.9 5.4 %collective-permute-start.4 = (bf16[64,768]{1,0:T(8,128)(2,1)S(1)}, bf16[64,768]{1,0:T(8,128)(2,1)S(1)}, u32[]{:S(2)}, u32[]{:S(2)}) collective-permute-start(bf16[64,768]{1,0:T(8,128)(2,1)S(1)} %shard_map.61), channel_id=1, source_target_pairs={{0,96},{1,145},{2,98},{3,147},{4,100},{5,149},{6,102},{7,151},{8,1... | collective-permute-start | bytes 294920 | tf_op jit(solution)/shard_map/ppermute | solution.py:38
  36.8 5.0 %collective-permute-start.3 = (bf16[64,768]{1,0:T(8,128)(2,1)S(1)}, bf16[64,768]{1,0:T(8,128)(2,1)S(1)}, u32[]{:S(2)}, u32[]{:S(2)}) collective-permute-start(bf16[64,768]{1,0:T(8,128)(2,1)S(1)} %shard_map.61), channel_id=1, source_target_pairs={{0,64},{1,17},{2,66},{3,19},{4,68},{5,21},{6,70},{7,23},{8,72},{9,... | collective-permute-start | bytes 294920 | tf_op jit(solution)/shard_map/ppermute | solution.py:38
  37.1 4.6 %collective-permute-start.2 = (bf16[64,768]{1,0:T(8,128)(2,1)S(1)}, bf16[64,768]{1,0:T(8,128)(2,1)S(1)}, u32[]{:S(2)}, u32[]{:S(2)}) collective-permute-start(bf16[64,768]{1,0:T(8,128)(2,1)S(1)} %shard_map.61), channel_id=1, source_target_pairs={{0,32},{1,129},{2,34},{3,131},{4,36},{5,133},{6,38},{7,135},{8,40}... | collective-permute-start | bytes 294920 | tf_op jit(solution)/shard_map/ppermute | solution.py:38
  41.8 5.1 %collective-permute-start.5 = (bf16[128,768]{1,0:T(8,128)(2,1)S(1)}, bf16[128,768]{1,0:T(8,128)(2,1)S(1)}, u32[]{:S(2)}, u32[]{:S(2)}) collective-permute-start(bf16[128,768]{1,0:T(8,128)(2,1)S(1)} %bitcast.17), channel_id=1, source_target_pairs={{0,128},{1,33},{2,130},{3,35},{4,132},{5,37},{6,134},{7,39},{8,136... | collective-permute-start | bytes 589832 | tf_op jit(solution)/shard_map/ppermute | solution.py:38
  43.1 8.9 %collective-permute-start.7 = (bf16[128,768]{1,0:T(8,128)(2,1)S(1)}, bf16[128,768]{1,0:T(8,128)(2,1)S(1)}, u32[]{:S(2)}, u32[]{:S(2)}) collective-permute-start(bf16[128,768]{1,0:T(8,128)(2,1)S(1)} %bitcast.18), channel_id=1, source_target_pairs={{0,16},{1,65},{2,18},{3,67},{4,20},{5,69},{6,22},{7,71},{8,24},{9,... | collective-permute-start | bytes 589832 | tf_op jit(solution)/shard_map/ppermute | solution.py:38
  45.6 7.3 %collective-permute-start.8 = (bf16[128,768]{1,0:T(8,128)(2,1)S(1)}, bf16[128,768]{1,0:T(8,128)(2,1)S(1)}, u32[]{:S(2)}, u32[]{:S(2)}) collective-permute-start(bf16[128,768]{1,0:T(8,128)(2,1)S(1)} %bitcast.19), channel_id=1, source_target_pairs={{0,144},{1,97},{2,146},{3,99},{4,148},{5,101},{6,150},{7,103},{8,1... | collective-permute-start | bytes 589832 | tf_op jit(solution)/shard_map/ppermute | solution.py:38
  45.8 15.6 %collective-permute-start.10 = (bf16[128,768]{1,0:T(8,128)(2,1)S(1)}, bf16[128,768]{1,0:T(8,128)(2,1)S(1)}, u32[]{:S(2)}, u32[]{:S(2)}) collective-permute-start(bf16[128,768]{1,0:T(8,128)(2,1)S(1)} %bitcast.13), channel_id=1, source_target_pairs={{0,128},{1,33},{2,130},{3,35},{4,132},{5,37},{6,134},{7,39},{8,136... | collective-permute-start | bytes 589832 | tf_op jit(solution)/shard_map/ppermute | solution.py:38
  46.9 17.8 %collective-permute-start.11 = (bf16[128,768]{1,0:T(8,128)(2,1)S(1)}, bf16[128,768]{1,0:T(8,128)(2,1)S(1)}, u32[]{:S(2)}, u32[]{:S(2)}) collective-permute-start(bf16[128,768]{1,0:T(8,128)(2,1)S(1)} %bitcast.14), channel_id=1, source_target_pairs={{0,16},{1,65},{2,18},{3,67},{4,20},{5,69},{6,22},{7,71},{8,24},{9,... | collective-permute-start | bytes 589832 | tf_op jit(solution)/shard_map/ppermute | solution.py:38
  49.4 15.2 %collective-permute-start.12 = (bf16[128,768]{1,0:T(8,128)(2,1)S(1)}, bf16[128,768]{1,0:T(8,128)(2,1)S(1)}, u32[]{:S(2)}, u32[]{:S(2)}) collective-permute-start(bf16[128,768]{1,0:T(8,128)(2,1)S(1)} %bitcast.15), channel_id=1, source_target_pairs={{0,144},{1,97},{2,146},{3,99},{4,148},{5,101},{6,150},{7,103},{8,1... | collective-permute-start | bytes 589832 | tf_op jit(solution)/shard_map/ppermute | solution.py:38
  54.8 7.3 %collective-permute-start.9 = (f32[2,2048]{1,0:T(2,128)S(1)}, f32[2,2048]{1,0:T(2,128)S(1)}, u32[]{:S(2)}, u32[]{:S(2)}) collective-permute-start(f32[2,2048]{1,0:T(2,128)S(1)} %shard_map.63.best_ref), channel_id=1, source_target_pairs={{0,1},{1,0},{2,3},{3,2},{4,5},{5,4},{6,7},{7,6},{8,9},{9,8},{10,11... | collective-permute-start | bytes 49160 | tf_op jit(solution)/shard_map/ppermute | solution.py:34
  67.2 18.1 %all-to-all-start.1 = ((f32[128,1,32]{2,1,0:T(1,128)}), f32[128,1,32]{2,1,0:T(1,128)S(1)}, u32[]{:S(2)}, u32[]{:S(2)}) async-start(f32[128,1,32]{2,1,0:T(1,128)} %bitcast.10), calls=%async_computation.1 | async-start | bytes 131072 | tf_op jit(solution)/shard_map/all_to_all | solution.py:239

commit v13 on v8

--- a/solution.py
+++ b/solution.py
@@ -210,10 +210,10 @@
     rows, width = embeddings.shape
     kept, given, found = own_picks(chosen_index, candidate_index, embeddings)
     half = kept + swap(given, 0, 1)
-    half, later = lax.optimization_barrier((half, embeddings))
-    partner = swap(later, 0, 1)
     quarter = half[:32] + swap(half[32:], 2, 0)
     send = jnp.concatenate([quarter, found], axis=0)
+    send, later = lax.optimization_barrier((send, embeddings))
+    partner = swap(later, 0, 1)
     got = lax.all_to_all(jnp.broadcast_to(send, (8, 32 + MOST, width)), "z", 0, 0)
     block = settled(got)
     line = jnp.stack([block] + [turn(block, s, True) for s in (1, 2, 3)])

time: 85 us -> 86.2 us (1.014)
  blocking collectives: 20.7 us -> 23.5 us
  starting transfers between devices: 28.9 us -> 27.4 us
    all_to_all x1, blocking collectives: 20.7 us -> 23.5 us  [local(): lax.all_to_all(jnp.broadcast_to(send, (8, 32 + MOST, width)), 'z', 0, 0)]
    ppermute x4, starting transfers between devices: 11 us -> 9.47 us  [swap(): lax.ppermute(value, AXES, pairs_of(lambda y, x, z, c: (y ^ y_mask, x, z,...]
where the time goes in v13:
time: 86.2 us; the launch traced here: 85.7 us
  starting transfers between devices  27.4 us (32%)
  blocking collectives  23.5 us (27%)
  waiting for transfers between devices  21.5 us (25%)
  Pallas kernels  9.48 us (11%)
  local copies, waits for them, and re-layouts  1.57 us (2%)
  other arithmetic  1.53 us (2%)
    all_to_all x1, blocking collectives, local(): lax.all_to_all(jnp.broadcast_to(send, (8, 32 + MOST, width)), 'z', 0, 0)  23.5 us
    ppermute x9, starting transfers between devices, turn(): lax.ppermute(value, AXES, pairs_of(lambda y, x, z, c: (y, x ^ mask, z, c)...  11.9 us
    all_to_all x1, waiting for transfers between devices, local(): parts = lax.all_to_all(part, CHIPS, 0, 0, tiled=True)  10.6 us
    ppermute x4, starting transfers between devices, swap(): lax.ppermute(value, AXES, pairs_of(lambda y, x, z, c: (y ^ y_mask, x, z,...  9.47 us
    pallas_call x3, Pallas kernels, on_chip(): pl.pallas_call(kernel, out_shape=[jax.ShapeDtypeStruct(out, jnp.float32)...  8.14 us
    ppermute x9, waiting for transfers between devices, turn(): lax.ppermute(value, AXES, pairs_of(lambda y, x, z, c: (y, x ^ mask, z, c)...  6.13 us
    all_to_all x1, starting transfers between devices, local(): parts = lax.all_to_all(part, CHIPS, 0, 0, tiled=True)  6.06 us
    ppermute x4, waiting for transfers between devices, swap(): lax.ppermute(value, AXES, pairs_of(lambda y, x, z, c: (y ^ y_mask, x, z,...  4.78 us
  transfers between devices with their start and end apart: 14, of which 8 were waited for; matrix products, arithmetic and copies ran while one was open for 0% of the time, Pallas kernels for 5%

profile of v13, /device:TPU:1, one launch (start us, length us, event | category | flops | bytes accessed | tf_op | source)
XLA Modules:
  0.0 85.7 jit_solution(6096174756491663436)
XLA Ops:
  0.6 0.7 add_bitcast_fusion.index_ref
  1.7 1.5 %copy-done = bf16[2048,768]{1,0:T(8,128)(2,1)S(1)} copy-done((bf16[2048,768]{1,0:T(8,128)(2,1)S(1)}, bf16[2048,768]{1,0:T(8,128)(2,1)}, u32[]{:S(2)}) %copy-start) | copy-done | bytes 3145752
  3.9 3.3 %collective-permute-start = (bf16[64,768]{1,0:T(8,128)(2,1)S(1)}, bf16[64,768]{1,0:T(8,128)(2,1)S(1)}, u32[]{:S(2)}, u32[]{:S(2)}) collective-permute-start(bf16[64,768]{1,0:T(8,128)(2,1)S(1)} %get-tuple-element.10), channel_id=1, source_target_pairs={{0,1},{1,0},{2,3},{3,2},{4,5},{5,4},{6,7},{7,6},{8,9},{9,8},{10,11... | collective-permute-start | bytes 294920 | tf_op jit(solution)/shard_map/ppermute | solution.py:34
  7.2 0.9 %collective-permute-done = bf16[64,768]{1,0:T(8,128)(2,1)S(1)} collective-permute-done((bf16[64,768]{1,0:T(8,128)(2,1)S(1)}, bf16[64,768]{1,0:T(8,128)(2,1)S(1)}, u32[]{:S(2)}, u32[]{:S(2)}) %collective-permute-start) | collective-permute-done | bytes 98336 | tf_op jit(solution)/shard_map/ppermute | solution.py:34
  8.2 1.3 %collective-permute-start.1 = (bf16[32,768]{1,0:T(8,128)(2,1)S(1)}, bf16[32,768]{1,0:T(8,128)(2,1)S(1)}, u32[]{:S(2)}, u32[]{:S(2)}) collective-permute-start(bf16[32,768]{1,0:T(8,128)(2,1)S(1)} %slice.17), channel_id=1, source_target_pairs={{0,16},{1,17},{2,18},{3,19},{4,20},{5,21},{6,22},{7,23},{8,24},{9,... | collective-permute-start | bytes 147464 | tf_op jit(solution)/shard_map/ppermute | solution.py:34
  9.5 3.3 %collective-permute-done.1 = bf16[32,768]{1,0:T(8,128)(2,1)S(1)} collective-permute-done((bf16[32,768]{1,0:T(8,128)(2,1)S(1)}, bf16[32,768]{1,0:T(8,128)(2,1)S(1)}, u32[]{:S(2)}, u32[]{:S(2)}) %collective-permute-start.1) | collective-permute-done | bytes 49184 | tf_op jit(solution)/shard_map/ppermute | solution.py:34
  12.7 1.6 %collective-permute-start.6 = (bf16[2048,768]{1,0:T(8,128)(2,1)S(1)}, bf16[2048,768]{1,0:T(8,128)(2,1)S(1)}, u32[]{:S(2)}, u32[]{:S(2)}) collective-permute-start(bf16[2048,768]{1,0:T(8,128)(2,1)S(1)} %copy-done), channel_id=1, source_target_pairs={{0,1},{1,0},{2,3},{3,2},{4,5},{5,4},{6,7},{7,6},{8,9},{9,8},{10,11... | collective-permute-start | bytes 9437192 | tf_op jit(solution)/shard_map/ppermute | solution.py:34
  14.4 23.5 %all_to_all.14.got_ref = bf16[8,36,768]{2,1,0:T(8,128)(2,1)S(1)} all-to-all(bf16[8,36,768]{2,1,0:T(8,128)(2,1)S(1)} %broadcast_in_dim.3), channel_id=1, replica_groups=mesh['ylo'=2,'x'=4,'yhi'=2,'z'=8,'core'=2] {'z'}, dimensions={0} | all-to-all | bytes 884736 | tf_op jit(solution)/shard_map/all_to_all | solution.py:217
  38.0 1.4 %collective-permute-start.2 = (bf16[64,768]{1,0:T(8,128)(2,1)S(1)}, bf16[64,768]{1,0:T(8,128)(2,1)S(1)}, u32[]{:S(2)}, u32[]{:S(2)}) collective-permute-start(bf16[64,768]{1,0:T(8,128)(2,1)S(1)} %shard_map.61), channel_id=1, source_target_pairs={{0,32},{1,129},{2,34},{3,131},{4,36},{5,133},{6,38},{7,135},{8,40}... | collective-permute-start | bytes 294920 | tf_op jit(solution)/shard_map/ppermute | solution.py:38
  39.4 2.6 %collective-permute-start.3 = (bf16[64,768]{1,0:T(8,128)(2,1)S(1)}, bf16[64,768]{1,0:T(8,128)(2,1)S(1)}, u32[]{:S(2)}, u32[]{:S(2)}) collective-permute-start(bf16[64,768]{1,0:T(8,128)(2,1)S(1)} %shard_map.61), channel_id=1, source_target_pairs={{0,64},{1,17},{2,66},{3,19},{4,68},{5,21},{6,70},{7,23},{8,72},{9,... | collective-permute-start | bytes 294920 | tf_op jit(solution)/shard_map/ppermute | solution.py:38
  42.0 3.3 %collective-permute-done.3 = bf16[64,768]{1,0:T(8,128)(2,1)S(1)} collective-permute-done((bf16[64,768]{1,0:T(8,128)(2,1)S(1)}, bf16[64,768]{1,0:T(8,128)(2,1)S(1)}, u32[]{:S(2)}, u32[]{:S(2)}) %collective-permute-start.3) | collective-permute-done | bytes 98336 | tf_op jit(solution)/shard_map/ppermute | solution.py:38
  45.3 1.3 %collective-permute-done.4 = bf16[64,768]{1,0:T(8,128)(2,1)S(1)} collective-permute-done((bf16[64,768]{1,0:T(8,128)(2,1)S(1)}, bf16[64,768]{1,0:T(8,128)(2,1)S(1)}, u32[]{:S(2)}, u32[]{:S(2)}) %collective-permute-start.4) | collective-permute-done | bytes 98336 | tf_op jit(solution)/shard_map/ppermute | solution.py:38
  46.7 1.3 %collective-permute-start.5 = (bf16[128,768]{1,0:T(8,128)(2,1)S(1)}, bf16[128,768]{1,0:T(8,128)(2,1)S(1)}, u32[]{:S(2)}, u32[]{:S(2)}) collective-permute-start(bf16[128,768]{1,0:T(8,128)(2,1)S(1)} %bitcast.13), channel_id=1, source_target_pairs={{0,128},{1,33},{2,130},{3,35},{4,132},{5,37},{6,134},{7,39},{8,136... | collective-permute-start | bytes 589832 | tf_op jit(solution)/shard_map/ppermute | solution.py:38
  48.0 2.4 %collective-permute-start.7 = (bf16[128,768]{1,0:T(8,128)(2,1)S(1)}, bf16[128,768]{1,0:T(8,128)(2,1)S(1)}, u32[]{:S(2)}, u32[]{:S(2)}) collective-permute-start(bf16[128,768]{1,0:T(8,128)(2,1)S(1)} %bitcast.14), channel_id=1, source_target_pairs={{0,16},{1,65},{2,18},{3,67},{4,20},{5,69},{6,22},{7,71},{8,24},{9,... | collective-permute-start | bytes 589832 | tf_op jit(solution)/shard_map/ppermute | solution.py:38
  51.4 3.0 %collective-permute-start.11 = (bf16[128,768]{1,0:T(8,128)(2,1)S(1)}, bf16[128,768]{1,0:T(8,128)(2,1)S(1)}, u32[]{:S(2)}, u32[]{:S(2)}) collective-permute-start(bf16[128,768]{1,0:T(8,128)(2,1)S(1)} %bitcast.18), channel_id=1, source_target_pairs={{0,16},{1,65},{2,18},{3,67},{4,20},{5,69},{6,22},{7,71},{8,24},{9,... | collective-permute-start | bytes 589832 | tf_op jit(solution)/shard_map/ppermute | solution.py:38
  54.4 0.9 %collective-permute-start.12 = (bf16[128,768]{1,0:T(8,128)(2,1)S(1)}, bf16[128,768]{1,0:T(8,128)(2,1)S(1)}, u32[]{:S(2)}, u32[]{:S(2)}) collective-permute-start(bf16[128,768]{1,0:T(8,128)(2,1)S(1)} %bitcast.19), channel_id=1, source_target_pairs={{0,144},{1,97},{2,146},{3,99},{4,148},{5,101},{6,150},{7,103},{8,1... | collective-permute-start | bytes 589832 | tf_op jit(solution)/shard_map/ppermute | solution.py:38
  55.3 2.0 %shard_map.62.floor_ref = f32[2,2048]{1,0:T(2,128)S(1)} custom-call(bf16[2048,768]{1,0:T(8,128)(2,1)S(1)} %copy-done, f32[1,2048]{1,0:T(1,128)S(1)} %bitcast.22, bf16[128,768]{1,0:T(8,128)(2,1)S(1)} %bitcast.16, bf16[128,768]{1,0:T(8,128)(2,1)S(1)} %collective-permute-done.5.c1, bf16[2048,768]{1,0:T(8,128)(2,1)S(1)} %collective-permute-done.6.partner_ref), custom_call_target="tpu_custom_call" | custom-call | flops 1610612736 | bytes 8388608 | tf_op jit(solution)/shard_map/pallas_call | solution.py:116
  57.3 0.8 collective-permute-done.8.c1
  58.1 2.0 %shard_map.63.best_ref = f32[2,2048]{1,0:T(2,128)S(1)} custom-call(bf16[2048,768]{1,0:T(8,128)(2,1)S(1)} %copy-done, f32[2,2048]{1,0:T(2,128)S(1)} %shard_map.62.floor_ref, bf16[128,768]{1,0:T(8,128)(2,1)S(1)} %collective-permute-done.7.c0, bf16[128,768]{1,0:T(8,128)(2,1)S(1)} %collective-permute-done.8.c1, ...), custom_call_target="tpu_custom_call" | custom-call | flops 1610612736 | bytes 8388608 | tf_op jit(solution)/shard_map/pallas_call | solution.py:116
  60.1 3.3 %collective-permute-start.9 = (f32[2,2048]{1,0:T(2,128)S(1)}, f32[2,2048]{1,0:T(2,128)S(1)}, u32[]{:S(2)}, u32[]{:S(2)}) collective-permute-start(f32[2,2048]{1,0:T(2,128)S(1)} %shard_map.63.best_ref), channel_id=1, source_target_pairs={{0,1},{1,0},{2,3},{3,2},{4,5},{5,4},{6,7},{7,6},{8,9},{9,8},{10,11... | collective-permute-start | bytes 49160 | tf_op jit(solution)/shard_map/ppermute | solution.py:34
  64.2 4.1 %shard_map.65 = (f32[128,32]{1,0:T(8,128)}, f32[1,2048]{1,0:T(1,128)}) custom-call(bf16[2048,768]{1,0:T(8,128)(2,1)S(1)} %copy-done, f32[2,2048]{1,0:T(2,128)S(1)} %shard_map.63.best_ref, f32[2,2048]{1,0:T(2,128)S(1)} %collective-permute-done.9.other_ref, bf16[768,512]{1,0:T(8,128)(2,1)S(1)} %shard_map.64.turned, ...), custom_call_target="tpu_custom_call" | custom-call | flops 3221225472 | bytes 8388608 | tf_op jit(solution)/shard_map/pallas_call | solution.py:116
  68.3 6.1 %all-to-all-start.1 = ((f32[128,1,32]{2,1,0:T(1,128)}), f32[128,1,32]{2,1,0:T(1,128)S(1)}, u32[]{:S(2)}, u32[]{:S(2)}) async-start(f32[128,1,32]{2,1,0:T(1,128)} %bitcast.10), calls=%async_computation.1 | async-start | bytes 131072 | tf_op jit(solution)/shard_map/all_to_all | solution.py:231
  74.4 10.6 %all-to-all-done.1 = f32[128,1,32]{2,1,0:T(1,128)S(1)} async-done(((f32[128,1,32]{2,1,0:T(1,128)}), f32[128,1,32]{2,1,0:T(1,128)S(1)}, u32[]{:S(2)}, u32[]{:S(2)}) %all-to-all-start.1) | async-done | bytes 16416 | tf_op jit(solution)/shard_map/all_to_all | solution.py:231
  85.0 0.7 dynamic-slice_reduce_fusion
  (25 shorter events, 3.0 us)
Async XLA Ops:
  1.3 1.9 %copy-start = (bf16[2048,768]{1,0:T(8,128)(2,1)S(1)}, bf16[2048,768]{1,0:T(8,128)(2,1)}, u32[]{:S(2)}) copy-start(bf16[2048,768]{1,0:T(8,128)(2,1)} %own_ref.5) | copy-start | bytes 9437188
  3.2 52.0 %copy-start.1 = (f32[2048]{0:T(1024)S(1)}, f32[2048]{0:T(1024)}, u32[]{:S(2)}) copy-start(f32[2048]{0:T(1024)} %param.5) | copy-start | bytes 24580
  3.9 4.3 %collective-permute-start = (bf16[64,768]{1,0:T(8,128)(2,1)S(1)}, bf16[64,768]{1,0:T(8,128)(2,1)S(1)}, u32[]{:S(2)}, u32[]{:S(2)}) collective-permute-start(bf16[64,768]{1,0:T(8,128)(2,1)S(1)} %get-tuple-element.10), channel_id=1, source_target_pairs={{0,1},{1,0},{2,3},{3,2},{4,5},{5,4},{6,7},{7,6},{8,9},{9,8},{10,11... | collective-permute-start | bytes 294920 | tf_op jit(solution)/shard_map/ppermute | solution.py:34
  8.2 4.5 %collective-permute-start.1 = (bf16[32,768]{1,0:T(8,128)(2,1)S(1)}, bf16[32,768]{1,0:T(8,128)(2,1)S(1)}, u32[]{:S(2)}, u32[]{:S(2)}) collective-permute-start(bf16[32,768]{1,0:T(8,128)(2,1)S(1)} %slice.17), channel_id=1, source_target_pairs={{0,16},{1,17},{2,18},{3,19},{4,20},{5,21},{6,22},{7,23},{8,24},{9,... | collective-permute-start | bytes 147464 | tf_op jit(solution)/shard_map/ppermute | solution.py:34
  12.7 41.7 %collective-permute-start.6 = (bf16[2048,768]{1,0:T(8,128)(2,1)S(1)}, bf16[2048,768]{1,0:T(8,128)(2,1)S(1)}, u32[]{:S(2)}, u32[]{:S(2)}) collective-permute-start(bf16[2048,768]{1,0:T(8,128)(2,1)S(1)} %copy-done), channel_id=1, source_target_pairs={{0,1},{1,0},{2,3},{3,2},{4,5},{5,4},{6,7},{7,6},{8,9},{9,8},{10,11... | collective-permute-start | bytes 9437192 | tf_op jit(solution)/shard_map/ppermute | solution.py:34
  38.0 4.0 %collective-permute-start.2 = (bf16[64,768]{1,0:T(8,128)(2,1)S(1)}, bf16[64,768]{1,0:T(8,128)(2,1)S(1)}, u32[]{:S(2)}, u32[]{:S(2)}) collective-permute-start(bf16[64,768]{1,0:T(8,128)(2,1)S(1)} %shard_map.61), channel_id=1, source_target_pairs={{0,32},{1,129},{2,34},{3,131},{4,36},{5,133},{6,38},{7,135},{8,40}... | collective-permute-start | bytes 294920 | tf_op jit(solution)/shard_map/ppermute | solution.py:38
  39.4 6.0 %collective-permute-start.3 = (bf16[64,768]{1,0:T(8,128)(2,1)S(1)}, bf16[64,768]{1,0:T(8,128)(2,1)S(1)}, u32[]{:S(2)}, u32[]{:S(2)}) collective-permute-start(bf16[64,768]{1,0:T(8,128)(2,1)S(1)} %shard_map.61), channel_id=1, source_target_pairs={{0,64},{1,17},{2,66},{3,19},{4,68},{5,21},{6,70},{7,23},{8,72},{9,... | collective-permute-start | bytes 294920 | tf_op jit(solution)/shard_map/ppermute | solution.py:38
  42.0 4.7 %collective-permute-start.4 = (bf16[64,768]{1,0:T(8,128)(2,1)S(1)}, bf16[64,768]{1,0:T(8,128)(2,1)S(1)}, u32[]{:S(2)}, u32[]{:S(2)}) collective-permute-start(bf16[64,768]{1,0:T(8,128)(2,1)S(1)} %shard_map.61), channel_id=1, source_target_pairs={{0,96},{1,145},{2,98},{3,147},{4,100},{5,149},{6,102},{7,151},{8,1... | collective-permute-start | bytes 294920 | tf_op jit(solution)/shard_map/ppermute | solution.py:38
  46.7 4.6 %collective-permute-start.5 = (bf16[128,768]{1,0:T(8,128)(2,1)S(1)}, bf16[128,768]{1,0:T(8,128)(2,1)S(1)}, u32[]{:S(2)}, u32[]{:S(2)}) collective-permute-start(bf16[128,768]{1,0:T(8,128)(2,1)S(1)} %bitcast.13), channel_id=1, source_target_pairs={{0,128},{1,33},{2,130},{3,35},{4,132},{5,37},{6,134},{7,39},{8,136... | collective-permute-start | bytes 589832 | tf_op jit(solution)/shard_map/ppermute | solution.py:38
  48.0 9.2 %collective-permute-start.7 = (bf16[128,768]{1,0:T(8,128)(2,1)S(1)}, bf16[128,768]{1,0:T(8,128)(2,1)S(1)}, u32[]{:S(2)}, u32[]{:S(2)}) collective-permute-start(bf16[128,768]{1,0:T(8,128)(2,1)S(1)} %bitcast.14), channel_id=1, source_target_pairs={{0,16},{1,65},{2,18},{3,67},{4,20},{5,69},{6,22},{7,71},{8,24},{9,... | collective-permute-start | bytes 589832 | tf_op jit(solution)/shard_map/ppermute | solution.py:38
  50.5 7.6 %collective-permute-start.8 = (bf16[128,768]{1,0:T(8,128)(2,1)S(1)}, bf16[128,768]{1,0:T(8,128)(2,1)S(1)}, u32[]{:S(2)}, u32[]{:S(2)}) collective-permute-start(bf16[128,768]{1,0:T(8,128)(2,1)S(1)} %bitcast.15), channel_id=1, source_target_pairs={{0,144},{1,97},{2,146},{3,99},{4,148},{5,101},{6,150},{7,103},{8,1... | collective-permute-start | bytes 589832 | tf_op jit(solution)/shard_map/ppermute | solution.py:38
  50.7 12.7 %collective-permute-start.10 = (bf16[128,768]{1,0:T(8,128)(2,1)S(1)}, bf16[128,768]{1,0:T(8,128)(2,1)S(1)}, u32[]{:S(2)}, u32[]{:S(2)}) collective-permute-start(bf16[128,768]{1,0:T(8,128)(2,1)S(1)} %bitcast.17), channel_id=1, source_target_pairs={{0,128},{1,33},{2,130},{3,35},{4,132},{5,37},{6,134},{7,39},{8,136... | collective-permute-start | bytes 589832 | tf_op jit(solution)/shard_map/ppermute | solution.py:38
  51.4 12.0 %collective-permute-start.11 = (bf16[128,768]{1,0:T(8,128)(2,1)S(1)}, bf16[128,768]{1,0:T(8,128)(2,1)S(1)}, u32[]{:S(2)}, u32[]{:S(2)}) collective-permute-start(bf16[128,768]{1,0:T(8,128)(2,1)S(1)} %bitcast.18), channel_id=1, source_target_pairs={{0,16},{1,65},{2,18},{3,67},{4,20},{5,69},{6,22},{7,71},{8,24},{9,... | collective-permute-start | bytes 589832 | tf_op jit(solution)/shard_map/ppermute | solution.py:38
  54.4 9.0 %collective-permute-start.12 = (bf16[128,768]{1,0:T(8,128)(2,1)S(1)}, bf16[128,768]{1,0:T(8,128)(2,1)S(1)}, u32[]{:S(2)}, u32[]{:S(2)}) collective-permute-start(bf16[128,768]{1,0:T(8,128)(2,1)S(1)} %bitcast.19), channel_id=1, source_target_pairs={{0,144},{1,97},{2,146},{3,99},{4,148},{5,101},{6,150},{7,103},{8,1... | collective-permute-start | bytes 589832 | tf_op jit(solution)/shard_map/ppermute | solution.py:38
  60.1 4.1 %collective-permute-start.9 = (f32[2,2048]{1,0:T(2,128)S(1)}, f32[2,2048]{1,0:T(2,128)S(1)}, u32[]{:S(2)}, u32[]{:S(2)}) collective-permute-start(f32[2,2048]{1,0:T(2,128)S(1)} %shard_map.63.best_ref), channel_id=1, source_target_pairs={{0,1},{1,0},{2,3},{3,2},{4,5},{5,4},{6,7},{7,6},{8,9},{9,8},{10,11... | collective-permute-start | bytes 49160 | tf_op jit(solution)/shard_map/ppermute | solution.py:34
  68.3 16.6 %all-to-all-start.1 = ((f32[128,1,32]{2,1,0:T(1,128)}), f32[128,1,32]{2,1,0:T(1,128)S(1)}, u32[]{:S(2)}, u32[]{:S(2)}) async-start(f32[128,1,32]{2,1,0:T(1,128)} %bitcast.10), calls=%async_computation.1 | async-start | bytes 131072 | tf_op jit(solution)/shard_map/all_to_all | solution.py:231
